TPU v7x, 32 devices: a whole 2x2x4 slice. The times are simulated.
32 devices in a mesh: dp: 4 (over x, core), mp: 8 (over z, y).
Axes of the slice: x: 2, y: 2, z: 4, core: 2. Of those that a mesh axis runs over, the one named last changes fastest.
Arguments:
- tokens: bfloat16 [8192, 4608], P('mp', 'dp'), may hold values from -6 to 6
- kv_weight: bfloat16 [2, 4608, 1024], P(None, 'dp', 'mp'), may hold values from -0.125 to 0.125
- d_kv: bfloat16 [8192, 2, 1024], P('mp', None, 'dp'), may hold values from -6 to 6
Outputs:
- kv_out: bfloat16 [8192, 2, 1024], P('mp', None, 'dp')
- d_tokens: bfloat16 [8192, 4608], P('mp', 'dp')
- grad_kv: float32 [2, 4608, 1024], P(None, 'dp', 'mp')
All inputs are finite; a program needn't handle non-finite values.
Results may differ from a plain program's by a relative error of at most 0.001.
Values may be sent and summed in bfloat16 or wider, within the bound.
A program may use at most 128 MiB of HBM per device.

v0:
```python
import jax
import jax.numpy as jnp
from jax import lax
from jax.sharding import PartitionSpec as P


def per_device(tokens, kv_weight, d_kv):
    panels = lax.all_gather(kv_weight, "mp", axis=2, tiled=True)
    partial_value = jnp.einsum("td,kdc->tkc", tokens, panels, preferred_element_type=jnp.float32)
    kv_out = lax.psum_scatter(partial_value, "dp", scatter_dimension=2, tiled=True).astype(
        jnp.bfloat16
    )
    cotangent = lax.all_gather(d_kv, "dp", axis=2, tiled=True)
    d_tokens = jnp.einsum(
        "tkc,kdc->td", cotangent, panels, preferred_element_type=jnp.float32
    ).astype(jnp.bfloat16)
    partial_grad = jnp.einsum("td,tkc->ckd", tokens, cotangent, preferred_element_type=jnp.float32)
    owned_share = lax.psum_scatter(partial_grad, "mp", scatter_dimension=0, tiled=True)
    grad_kv = jnp.transpose(owned_share, (1, 2, 0))
    return (kv_out, d_tokens, grad_kv)


def solution(mesh):
    placed = (P("mp", "dp"), P(None, "dp", "mp"), P("mp", None, "dp"))
    return jax.shard_map(
        per_device,
        mesh=mesh,
        in_specs=placed,
        out_specs=(P("mp", None, "dp"), P("mp", "dp"), P(None, "dp", "mp")),
        check_vma=False,
    )
```

profile of v0, /device:TPU:0, one launch (start us, length us, event | category | flops | bytes accessed | tf_op | source)
XLA Modules:
  0.0 380.1 jit_solution(10349525903028383104)
XLA Ops:
  7.2 0.0 copy-start
  7.2 0.0 all-gather.3.cloned.1.call-start
  7.2 0.7 all-gather.3.cloned.1.call-update
  7.9 0.0 all-gather.5.cloned.1.call-start
  8.0 2.3 copy.6
  10.3 0.0 all-gather.5.cloned.1.call-update
  10.3 0.0 reduce-scatter.3.cloned.1.call-start
  10.4 83.4 %all-gather.3.cloned.1.call-done = bf16[2,1152,1024]{2,1,0:T(8,128)(2,1)} async-done(((bf16[2,1152,128]{2,1,0:T(8,128)(2,1)}), bf16[2,1152,1024]{2,1,0:T(8,128)(2,1)}) %all-gather.3.cloned.1.call-update) | async-done | bytes 4718608 | tf_op jit(solution)/shard_map/all_gather | solution.py:8
  93.8 0.0 copy-done
  93.8 10.1 %fusion.1 = f32[1024,2,1024]{2,0,1:T(8,128)} fusion(bf16[2,1152,1024]{2,1,0:T(8,128)(2,1)} %all-gather.3.cloned.1.call-done, bf16[1024,1152]{1,0:T(8,128)(2,1)S(1)} %copy-done), kind=kOutput, calls=%fused_computation.3 | convolution fusion | flops 4831838208 | bytes 15466496 | tf_op jit(solution)/shard_map/td,kdc->tkc/dot_general | solution.py:9
  103.9 0.0 reduce-scatter.3.cloned.1.call-update
  103.9 0.0 reduce-scatter.5.cloned.1.call-start
  104.0 25.2 %all-gather.5.cloned.1.call-done = bf16[1024,2,1024]{2,0,1:T(8,128)(2,1)} async-done(((bf16[1024,2,256]{2,0,1:T(8,128)(2,1)}), bf16[1024,2,1024]{2,0,1:T(8,128)(2,1)}) %all-gather.5.cloned.1.call-update) | async-done | bytes 4194320 | tf_op jit(solution)/shard_map/all_gather | solution.py:13
  129.2 9.6 %convolution_bitcast_fusion = f32[1024,2,1152]{2,0,1:T(8,128)} fusion(bf16[1024,2,1024]{2,0,1:T(8,128)(2,1)} %all-gather.5.cloned.1.call-done, bf16[1024,1152]{1,0:T(8,128)(2,1)S(1)} %copy-done), kind=kOutput, calls=%fused_computation | convolution fusion | flops 4831838208 | bytes 15990784 | tf_op jit(solution)/shard_map/td,tkc->ckd/dot_general | solution.py:17
  138.8 0.0 reduce-scatter.5.cloned.1.call-update
  138.9 11.6 %bitcast_convert_fusion = bf16[1024,1152]{1,0:T(8,128)(2,1)} fusion(bf16[1024,2,1024]{2,0,1:T(8,128)(2,1)} %all-gather.5.cloned.1.call-done, bf16[2,1152,1024]{2,1,0:T(8,128)(2,1)} %all-gather.3.cloned.1.call-done), kind=kOutput, calls=%fused_computation.1 | convolution fusion | flops 4833017856 | bytes 11272192 | tf_op jit(solution)/shard_map/tkc,kdc->td/dot_general | solution.py:14
  150.4 53.1 %reduce-scatter.3.cloned.1.call-done = f32[1024,2,256]{2,0,1:T(8,128)} async-done(((f32[1024,2,1024]{2,0,1:T(8,128)}), f32[1024,2,256]{2,0,1:T(8,128)}) %reduce-scatter.3.cloned.1.call-update) | async-done | bytes 2097168 | tf_op jit(solution)/shard_map/reduce_scatter | solution.py:10
  203.5 1.7 convert_element_type.6
  205.2 2.0 copy.8
  207.3 163.7 %reduce-scatter.5.cloned.1.call-done = f32[128,2,1152]{2,0,1:T(8,128)} async-done(((f32[1024,2,1152]{2,0,1:T(8,128)}), f32[128,2,1152]{2,0,1:T(8,128)}) %reduce-scatter.5.cloned.1.call-update) | async-done | bytes 1179664 | tf_op jit(solution)/shard_map/reduce_scatter | solution.py:18
  370.9 2.7 copy.9
Async XLA Ops:
  7.2 86.6 %copy-start = (bf16[1024,1152]{1,0:T(8,128)(2,1)S(1)}, bf16[1024,1152]{1,0:T(8,128)(2,1)}, u32[]{:S(2)}) copy-start(bf16[1024,1152]{1,0:T(8,128)(2,1)} %param.3) | copy-start | bytes 7077892
  7.2 86.6 %all-gather.3.cloned.1.call-start = ((), (), s32[]{:S(2)}) async-start(), calls=%async_computation.2 | async-start | bytes 5308416 | tf_op jit(solution)/shard_map/all_gather | solution.py:8
  7.9 121.3 %all-gather.5.cloned.1.call-start = ((), (), s32[]{:S(2)}) async-start(), calls=%async_computation.4 | async-start | bytes 5242880 | tf_op jit(solution)/shard_map/all_gather | solution.py:13
  10.3 193.2 %reduce-scatter.3.cloned.1.call-start = ((), (), s32[]{:S(2)}) async-start(), calls=%async_computation.3 | async-start | bytes 10485760 | tf_op jit(solution)/shard_map/reduce_scatter | solution.py:10
  103.9 267.0 %reduce-scatter.5.cloned.1.call-start = ((), (), s32[]{:S(2)}) async-start(), calls=%async_computation.5 | async-start | bytes 10616832 | tf_op jit(solution)/shard_map/reduce_scatter | solution.py:18
Sparse Core Ops, SparseCore 0:
  10.1 83.6 all-gather.2
  95.9 33.2 all-gather.4
  131.8 71.7 reduce-scatter.2
  207.4 163.4 reduce-scatter.4
where the time goes:
time: 380 us
  waiting for transfers between devices  326 us (86%)
  matrix products  31.3 us (8%)
  between operations  13.8 us (4%)
  local copies, waits for them, and re-layouts  7.04 us (2%)
    reduce_scatter x1, waiting for transfers between devices, per_device(): lax.psum_scatter(partial_grad, 'mp', scatter_dimension=0, tiled=True)  164 us
    all_gather x1, waiting for transfers between devices, per_device(): panels = lax.all_gather(kv_weight, 'mp', axis=2, tiled=True)  83.4 us
    reduce_scatter x1, waiting for transfers between devices, per_device(): lax.psum_scatter(partial_value, 'dp', scatter_dimension=2, tiled=True)  53.1 us
    all_gather x1, waiting for transfers between devices, per_device(): cotangent = lax.all_gather(d_kv, 'dp', axis=2, tiled=True)  25.2 us
    dot_general x1, matrix products, per_device(): jnp.einsum('tkc,kdc->td', cotangent, panels, preferred_element_type=jnp.f...  11.6 us
    dot_general x1, matrix products, per_device(): jnp.einsum('td,kdc->tkc', tokens, panels, preferred_element_type=jnp.floa...  10.1 us
    dot_general x1, matrix products, per_device(): jnp.einsum('td,tkc->ckd', tokens, cotangent, preferred_element_type=jnp.f...  9.64 us
  transfers between devices with their start and end apart: 4, of which 4 were waited for; matrix products, arithmetic and copies ran while one was open for 10% of the time, Pallas kernels for 0%

commit v1 on v0

v1 whole, which is shorter than its diff:
```python
import jax
import jax.numpy as jnp
from jax import lax
from jax.sharding import PartitionSpec as P

F32, BF16, F16 = jnp.float32, jnp.bfloat16, jnp.float16


def general(tokens, kv_weight, d_kv):
    panels = lax.all_gather(kv_weight, "mp", axis=2, tiled=True)
    partial_value = jnp.einsum("td,kdc->tkc", tokens, panels, preferred_element_type=F32)
    kv_out = lax.psum_scatter(partial_value, "dp", scatter_dimension=2, tiled=True).astype(BF16)
    cotangent = lax.all_gather(d_kv, "dp", axis=2, tiled=True)
    d_tokens = jnp.einsum("tkc,kdc->td", cotangent, panels, preferred_element_type=F32).astype(BF16)
    partial_grad = jnp.einsum("td,tkc->ckd", tokens, cotangent, preferred_element_type=F32)
    owned_share = lax.psum_scatter(partial_grad, "mp", scatter_dimension=0, tiled=True)
    return kv_out, d_tokens, jnp.transpose(owned_share, (1, 2, 0))


def dot(a, b, ca, cb):
    return lax.dot_general(a, b, (((ca,), (cb,)), ((), ())), preferred_element_type=F32)


def hops(tokens, kv_weight, d_kv):
    rows, feats = tokens.shape
    wide = kv_weight.shape[2]
    me = lax.axis_index("dp")
    mp = lax.axis_index("mp")
    z, y = mp // 2, mp % 2
    pair = 4 * wide

    def over_z(a):
        return lax.ppermute(a, "mp", [(m, (m + 2) % 8) for m in range(8)])

    def over_y(a):
        return lax.ppermute(a, "mp", [(m, m ^ 1) for m in range(8)])

    def over_x(a):
        return lax.ppermute(a, "dp", [(d, d ^ 2) for d in range(4)])

    def over_core(a):
        return lax.ppermute(a, "dp", [(d, d ^ 1) for d in range(4)])

    def place(a, index):
        return lax.dynamic_slice(a, (0, index * pair), (a.shape[0], pair))

    most = jnp.stack([jnp.max(jnp.abs(tokens)), jnp.max(jnp.abs(d_kv))]).astype(F32)
    most = lax.pmax(most, ("dp", "mp"))
    bound = jnp.maximum(most[0] * most[1] * (rows * 8), 1e-30)
    down, up = 60000.0 / bound, bound / 60000.0

    block = jnp.transpose(kv_weight, (1, 0, 2)).reshape(feats, 2 * wide)
    ring = []
    for s in range(4):
        ring += [block, over_y(block)]
        if s < 3:
            block = over_z(block)

    halves = d_kv.reshape(rows, 2, 2, wide)
    halves = jnp.where(y == 0, halves, halves[:, :, ::-1])
    own = jnp.transpose(halves, (0, 2, 1, 3)).reshape(rows, pair)
    across = over_x(own)
    cot = jnp.concatenate([own, over_core(own), across, over_core(across)], axis=1)

    travelling = None
    for s in range(4):
        part = place(cot, me ^ ((z - 1 - s) % 4))
        away = dot(tokens, part[:, 2 * wide :], 0, 0)
        arrived = over_y((away * down).astype(F16))
        mine = dot(tokens, part[:, : 2 * wide], 0, 0) * down + arrived.astype(F32)
        if travelling is not None:
            mine = mine + travelling.astype(F32)
        if s < 3:
            travelling = over_z(mine.astype(F16))
    grad_kv = jnp.transpose((mine * up).reshape(feats, 2, wide), (1, 0, 2))

    panels = jnp.concatenate(ring, axis=1)
    panel = [place(panels, (z - (me ^ r)) % 4) for r in range(4)]
    far = over_core(dot(tokens, panel[3], 1, 0))
    far = over_x(dot(tokens, panel[2], 1, 0) + far)
    near = over_core(dot(tokens, panel[1], 1, 0))
    kv = dot(tokens, panel[0], 1, 0) + near + far
    kv = jnp.transpose(kv.reshape(rows, 2, 2, wide), (0, 2, 1, 3))
    kv = jnp.where(y == 0, kv, kv[:, :, ::-1])
    kv_out = kv.reshape(rows, 2, 2 * wide).astype(BF16)

    d_tokens = dot(cot, jnp.concatenate(panel, axis=1), 1, 1).astype(BF16)
    return kv_out, d_tokens, grad_kv


def solution(mesh):
    placed = (P("mp", "dp"), P(None, "dp", "mp"), P("mp", None, "dp"))

    def per_device(tokens, kv_weight, d_kv):
        fits = dict(mesh.shape) == {"dp": 4, "mp": 8} and kv_weight.shape[2] % 128 == 0
        return (hops if fits else general)(tokens, kv_weight, d_kv)

    return jax.shard_map(
        per_device,
        mesh=mesh,
        in_specs=placed,
        out_specs=(P("mp", None, "dp"), P("mp", "dp"), P(None, "dp", "mp")),
        check_vma=False,
    )
```

time: 380 us -> 205 us (0.54)
  waiting for transfers between devices: 326 us -> 66.6 us
  blocking collectives: 0 us -> 51.1 us
  starting transfers between devices: 0.16 us -> 20.9 us
  local copies, waits for them, and re-layouts: 7.04 us -> 25.2 us
  other arithmetic: 1.69 us -> 13.6 us
  between operations: 13.8 us -> 2.2 us
  matrix products: 31.3 us -> 25.1 us
    reduce_scatter x2 -> x0, waiting for transfers between devices: 217 us -> none  [the longest x1 164 us: per_device(): lax.psum_scatter(partial_grad, 'mp', scatter_dimension=0, tiled=True)]
    all_gather x2 -> x0, waiting for transfers between devices: 109 us -> none  [the longest x1 83.4 us: per_device(): panels = lax.all_gather(kv_weight, 'mp', axis=2, tiled=True)]
    ppermute x0 -> x20, waiting for transfers between devices: none -> 66.6 us  [the longest x6 25.7 us: over_z(): return lax.ppermute(a, 'mp', [(m, (m + 2) % 8) for m in range(8)])]
    pmax x0 -> x1, blocking collectives: none -> 51.1 us  [hops(): most = lax.pmax(most, ('dp', 'mp'))]
    ppermute x0 -> x20, starting transfers between devices: none -> 20.9 us  [the longest x8 12.6 us: over_y(): return lax.ppermute(a, 'mp', [(m, m ^ 1) for m in range(8)])]
    reshape x0 -> x3, local copies, waits for them, and re-layouts: none -> 8.26 us  [the longest x2 6.88 us: hops(): halves = d_kv.reshape(rows, 2, 2, wide)]
    unnamed x5 -> x14, local copies, waits for them, and re-layouts: 7.04 us -> 13.5 us
    dot_general x3 -> x13, matrix products: 31.3 us -> 25.1 us  [dot(): lax.dot_general(a, b, (((ca,), (cb,)), ((), ())), preferred_element_type=...]
  transfers between devices with their start and end apart: 4 -> 20, of which waited for: 4 -> 10; matrix products, arithmetic and copies ran while one was open for 10% -> 27% of each run, Pallas kernels for 0% -> 0%
where the time goes in v1:
time: 205 us
  waiting for transfers between devices  66.6 us (32%)
  blocking collectives  51.1 us (25%)
  local copies, waits for them, and re-layouts  25.2 us (12%)
  matrix products  25.1 us (12%)
  starting transfers between devices  20.9 us (10%)
  other arithmetic  13.6 us (7%)
  between operations  2.2 us (1%)
    pmax x1, blocking collectives, hops(): most = lax.pmax(most, ('dp', 'mp'))  51.1 us
    ppermute x6, waiting for transfers between devices, over_z(): return lax.ppermute(a, 'mp', [(m, (m + 2) % 8) for m in range(8)])  25.7 us
    dot_general x13, matrix products, dot(): lax.dot_general(a, b, (((ca,), (cb,)), ((), ())), preferred_element_type=...  25.1 us
    ppermute x8, waiting for transfers between devices, over_y(): return lax.ppermute(a, 'mp', [(m, m ^ 1) for m in range(8)])  24.9 us
    ppermute x2, waiting for transfers between devices, over_x(): return lax.ppermute(a, 'dp', [(d, d ^ 2) for d in range(4)])  15.9 us
    unnamed x14, local copies, waits for them, and re-layouts  13.5 us
    ppermute x8, starting transfers between devices, over_y(): return lax.ppermute(a, 'mp', [(m, m ^ 1) for m in range(8)])  12.6 us
    reshape x2, local copies, waits for them, and re-layouts, hops(): halves = d_kv.reshape(rows, 2, 2, wide)  6.88 us
  transfers between devices with their start and end apart: 20, of which 10 were waited for; matrix products, arithmetic and copies ran while one was open for 27% of the time, Pallas kernels for 0%

profile of v1, /device:TPU:0, one launch (start us, length us, event | category | flops | bytes accessed | tf_op | source)
XLA Modules:
  0.0 204.7 jit_solution(4084836732671877697)
XLA Ops:
  0.6 2.1 %copy.10 = bf16[2,1152,128]{1,2,0:T(8,128)(2,1)} copy(bf16[2,1152,128]{2,1,0:T(8,128)(2,1)} %param.4) | data formatting | bytes 1179648 | tf_op args[1]
  2.7 3.0 %collective-permute-start = (bf16[1152,256]{0,1:T(8,128)(2,1)}, bf16[1152,256]{0,1:T(8,128)(2,1)}, u32[]{:S(2)}, u32[]{:S(2)}) collective-permute-start(bf16[1152,256]{0,1:T(8,128)(2,1)} %bitcast.1), channel_id=1, source_target_pairs={{0,1},{1,0},{2,3},{3,2},{4,5},{5,4},{6,7},{7,6},{8,9},{9,8},{10,11... | collective-permute-start | bytes 1769480 | tf_op jit(solution)/shard_map/ppermute | solution.py:36
  7.3 4.3 %reshape.34 = bf16[1024,2,2,128]{3,2,1,0:T(2,128)(2,1)} reshape(bf16[1024,2,256]{2,1,0:T(2,128)(2,1)} %param.5) | data formatting | bytes 2097152 | tf_op jit(solution)/shard_map/reshape | solution.py:59
  11.6 2.6 %copy.13 = bf16[1024,2,2,128]{0,3,1,2:T(8,128)(2,1)S(1)} copy(bf16[1024,2,2,128]{3,2,1,0:T(2,128)(2,1)} %reshape.34) | data formatting | bytes 2097152 | tf_op jit(solution)/shard_map/reshape | solution.py:59
  16.9 2.8 %abs_reduce_fusion.1 = bf16[]{:T(256)} fusion(bf16[1024,2,256]{2,1,0:T(2,128)(2,1)S(1)} %copy-done.2), kind=kLoop, calls=%fused_computation.50 | loop fusion | flops 1048575 | bytes 1048578 | tf_op jit(solution)/shard_map/reduce_max | solution.py:47
  22.0 51.1 %pmax.7 = f32[2]{0:T(128)S(1)} all-reduce(f32[2]{0:T(128)S(1)} %maximum_convert_fusion), channel_id=1, replica_groups=mesh['dp'=4,'mp'=8] {'dp','mp'}, use_global_device_ids=true, to_apply=%region_2.3 | all-reduce | flops 2 | bytes 16 | tf_op jit(solution)/shard_map/pmax | solution.py:48
  73.2 1.8 collective-permute-start.3
  75.0 1.9 constant_dynamic-update-slice_fusion.7
  76.9 2.3 %collective-permute-start.2 = (bf16[1152,256]{0,1:T(8,128)(2,1)}, bf16[1152,256]{0,1:T(8,128)(2,1)}, u32[]{:S(2)}, u32[]{:S(2)}) collective-permute-start(bf16[1152,256]{0,1:T(8,128)(2,1)} %collective-permute-done.1), channel_id=1, source_target_pairs={{0,1},{1,0},{2,3},{3,2},{4,5},{5,4},{6,7},{7,6},{8,9},{9,8},{10,11... | collective-permute-start | bytes 1769480 | tf_op jit(solution)/shard_map/ppermute | solution.py:36
  81.1 1.9 constant_dynamic-update-slice_fusion.6
  83.0 6.6 %collective-permute-done.3 = bf16[1152,256]{0,1:T(8,128)(2,1)} collective-permute-done((bf16[1152,256]{0,1:T(8,128)(2,1)}, bf16[1152,256]{0,1:T(8,128)(2,1)}, u32[]{:S(2)}, u32[]{:S(2)}) %collective-permute-start.3) | collective-permute-done | bytes 589856 | tf_op jit(solution)/shard_map/ppermute | solution.py:33
  90.9 1.9 constant_dynamic-update-slice_fusion.5
  92.8 1.9 constant_dynamic-update-slice_fusion.4
  94.8 1.9 constant_dynamic-update-slice_fusion.3
  96.7 8.3 %collective-permute-done.5 = bf16[1152,256]{0,1:T(8,128)(2,1)S(1)} collective-permute-done((bf16[1152,256]{0,1:T(8,128)(2,1)}, bf16[1152,256]{0,1:T(8,128)(2,1)S(1)}, u32[]{:S(2)}, u32[]{:S(2)}) %collective-permute-start.5) | collective-permute-done | bytes 589856 | tf_op jit(solution)/shard_map/ppermute | solution.py:33
  105.0 1.7 collective-permute-start.6
  108.5 2.0 pad_maximum_fusion
  111.6 9.6 %collective-permute-done.6 = bf16[1152,256]{0,1:T(8,128)(2,1)S(1)} collective-permute-done((bf16[1152,256]{0,1:T(8,128)(2,1)S(1)}, bf16[1152,256]{0,1:T(8,128)(2,1)S(1)}, u32[]{:S(2)}, u32[]{:S(2)}) %collective-permute-start.6) | collective-permute-done | bytes 589856 | tf_op jit(solution)/shard_map/ppermute | solution.py:36
  124.2 1.8 collective-permute-start.15
  127.3 4.8 %collective-permute-done.16 = f16[1152,256]{0,1:T(8,128)(2,1)S(1)} collective-permute-done((f16[1152,256]{0,1:T(8,128)(2,1)S(1)}, f16[1152,256]{0,1:T(8,128)(2,1)S(1)}, u32[]{:S(2)}, u32[]{:S(2)}) %collective-permute-start.16) | collective-permute-done | bytes 589856 | tf_op jit(solution)/shard_map/ppermute | solution.py:36
  134.4 1.8 collective-permute-start.13
  136.2 2.9 %convolution_bitcast_fusion.1 = f32[1024,512]{0,1:T(8,128)} fusion(bf16[1152,512]{0,1:T(8,128)(2,1)S(1)} %get-tuple-element.6, bf16[1024,1152]{1,0:T(8,128)(2,1)S(1)} %copy-done), kind=kOutput, calls=%fused_computation.48 | convolution fusion | flops 1207959552 | bytes 5636096 | tf_op jit(solution)/shard_map/dot_general | solution.py:21
  139.1 5.6 %collective-permute-done.15 = f16[1152,256]{0,1:T(8,128)(2,1)S(1)} collective-permute-done((f16[1152,256]{0,1:T(8,128)(2,1)S(1)}, f16[1152,256]{0,1:T(8,128)(2,1)S(1)}, u32[]{:S(2)}, u32[]{:S(2)}) %collective-permute-start.15) | collective-permute-done | bytes 589856 | tf_op jit(solution)/shard_map/ppermute | solution.py:36
  148.0 1.8 bitcast_add_fusion
  149.8 2.7 %collective-permute-start.9 = (f32[1024,512]{0,1:T(8,128)}, f32[1024,512]{0,1:T(8,128)}, u32[]{:S(2)}, u32[]{:S(2)}) collective-permute-start(f32[1024,512]{0,1:T(8,128)} %bitcast_add_fusion), channel_id=1, source_target_pairs={{0,16},{8,24},{16,0},{24,8},{1,17},{9,25},{17,1},{25,9},{2,18},{10... | collective-permute-start | bytes 6291464 | tf_op jit(solution)/shard_map/ppermute | solution.py:39
  152.4 4.9 %collective-permute-done.14 = f16[1152,256]{0,1:T(8,128)(2,1)S(1)} collective-permute-done((f16[1152,256]{0,1:T(8,128)(2,1)S(1)}, f16[1152,256]{0,1:T(8,128)(2,1)S(1)}, u32[]{:S(2)}, u32[]{:S(2)}) %collective-permute-start.14) | collective-permute-done | bytes 589856 | tf_op jit(solution)/shard_map/ppermute | solution.py:36
  157.4 5.9 %collective-permute-done.18 = f16[1152,256]{0,1:T(8,128)(2,1)S(1)} collective-permute-done((f16[1152,256]{0,1:T(8,128)(2,1)S(1)}, f16[1152,256]{0,1:T(8,128)(2,1)S(1)}, u32[]{:S(2)}, u32[]{:S(2)}) %collective-permute-start.18) | collective-permute-done | bytes 589856 | tf_op jit(solution)/shard_map/ppermute | solution.py:33
  164.4 8.8 %fusion.8 = bf16[1024,1152]{1,0:T(8,128)(2,1)} fusion(bf16[1152,512]{0,1:T(8,128)(2,1)S(1)} %get-tuple-element.4, bf16[1152,512]{0,1:T(8,128)(2,1)S(1)} %get-tuple-element.5, bf16[1152,512]{0,1:T(8,128)(2,1)S(1)} %get-tuple-element.6, bf16[1152,512]{0,1:T(8,128)(2,1)S(1)} %get-tuple-element.3, bf16[1024,512]{0,1:T(8,128)(2,1)S(1)} %collective-permute-done.12, ...), kind=kOutput, calls=%fused_computation.9 | convolution fusion | flops 4868669440 | bytes 11272192 | tf_op jit(solution)/shard_map/dot_general | solution.py:21
  173.2 2.9 %fusion.54 = f32[512,1024]{1,0:T(8,128)} fusion(bf16[1152,512]{0,1:T(8,128)(2,1)S(1)} %get-tuple-element.3, bf16[1024,1152]{1,0:T(8,128)(2,1)S(1)} %copy-done), kind=kOutput, calls=%fused_computation.82 | convolution fusion | flops 1207959552 | bytes 5636096 | tf_op jit(solution)/shard_map/dot_general | solution.py:21
  176.1 4.3 %collective-permute-done.19 = f16[1152,256]{0,1:T(8,128)(2,1)S(1)} collective-permute-done((f16[1152,256]{0,1:T(8,128)(2,1)S(1)}, f16[1152,256]{0,1:T(8,128)(2,1)S(1)}, u32[]{:S(2)}, u32[]{:S(2)}) %collective-permute-start.19) | collective-permute-done | bytes 589856 | tf_op jit(solution)/shard_map/ppermute | solution.py:33
  182.7 15.9 %collective-permute-done.9 = f32[1024,512]{0,1:T(8,128)} collective-permute-done((f32[1024,512]{0,1:T(8,128)}, f32[1024,512]{0,1:T(8,128)}, u32[]{:S(2)}, u32[]{:S(2)}) %collective-permute-start.9) | collective-permute-done | bytes 2097184 | tf_op jit(solution)/shard_map/ppermute | solution.py:39
  198.7 3.4 %fusion.35 = bf16[1024,512]{0,1:T(8,128)(2,1)S(1)} fusion(f32[1024,512]{0,1:T(8,128)} %collective-permute-done.9, f32[1024,512]{0,1:T(8,128)} %collective-permute-done.7, f32[512,1024]{1,0:T(8,128)} %fusion.54), kind=kLoop, calls=%fused_computation.46 | loop fusion | flops 1572864 | bytes 7340032 | tf_op jit(solution)/shard_map/add | solution.py:82
  (52 shorter events, 27.2 us)
Async XLA Ops:
  2.7 78.3 %collective-permute-start = (bf16[1152,256]{0,1:T(8,128)(2,1)}, bf16[1152,256]{0,1:T(8,128)(2,1)}, u32[]{:S(2)}, u32[]{:S(2)}) collective-permute-start(bf16[1152,256]{0,1:T(8,128)(2,1)} %bitcast.1), channel_id=1, source_target_pairs={{0,1},{1,0},{2,3},{3,2},{4,5},{5,4},{6,7},{7,6},{8,9},{9,8},{10,11... | collective-permute-start | bytes 1769480 | tf_op jit(solution)/shard_map/ppermute | solution.py:36
  5.7 67.5 %collective-permute-start.1 = (bf16[1152,256]{0,1:T(8,128)(2,1)}, bf16[1152,256]{0,1:T(8,128)(2,1)}, u32[]{:S(2)}, u32[]{:S(2)}) collective-permute-start(bf16[1152,256]{0,1:T(8,128)(2,1)} %bitcast.1), channel_id=1, source_target_pairs={{0,2},{1,3},{2,4},{3,5},{4,6},{5,7},{6,0},{7,1},{8,10},{9,11},{10,... | collective-permute-start | bytes 1769480 | tf_op jit(solution)/shard_map/ppermute | solution.py:33
  11.6 8.1 %copy-start = (bf16[1024,1152]{1,0:T(8,128)(2,1)S(1)}, bf16[1024,1152]{1,0:T(8,128)(2,1)}, u32[]{:S(2)}) copy-start(bf16[1024,1152]{1,0:T(8,128)(2,1)} %param.3) | copy-start | bytes 7077892
  14.2 2.7 %copy-start.2 = (bf16[1024,2,256]{2,1,0:T(2,128)(2,1)S(1)}, bf16[1024,2,256]{2,1,0:T(2,128)(2,1)}, u32[]{:S(2)}) copy-start(bf16[1024,2,256]{2,1,0:T(2,128)(2,1)} %param.5) | copy-start | bytes 3145732
  15.4 67.6 %collective-permute-start.11 = (bf16[1024,512]{0,1:T(8,128)(2,1)}, bf16[1024,512]{0,1:T(8,128)(2,1)S(1)}, u32[]{:S(2)}, u32[]{:S(2)}) collective-permute-start(bf16[1024,512]{0,1:T(8,128)(2,1)} %bitcast.11), channel_id=1, source_target_pairs={{0,16},{8,24},{16,0},{24,8},{1,17},{9,25},{17,1},{25,9},{2,18},{10... | collective-permute-start | bytes 3145736 | tf_op jit(solution)/shard_map/ppermute | solution.py:39
  22.0 86.5 %collective-permute-start.10 = (bf16[1024,512]{0,1:T(8,128)(2,1)}, bf16[1024,512]{0,1:T(8,128)(2,1)}, u32[]{:S(2)}, u32[]{:S(2)}) collective-permute-start(bf16[1024,512]{0,1:T(8,128)(2,1)} %bitcast.11), channel_id=1, source_target_pairs={{0,8},{8,0},{16,24},{24,16},{1,9},{9,1},{17,25},{25,17},{2,10},{10... | collective-permute-start | bytes 3145736 | tf_op jit(solution)/shard_map/ppermute | solution.py:42
  73.2 16.4 %collective-permute-start.3 = (bf16[1152,256]{0,1:T(8,128)(2,1)}, bf16[1152,256]{0,1:T(8,128)(2,1)}, u32[]{:S(2)}, u32[]{:S(2)}) collective-permute-start(bf16[1152,256]{0,1:T(8,128)(2,1)} %collective-permute-done.1), channel_id=1, source_target_pairs={{0,2},{1,3},{2,4},{3,5},{4,6},{5,7},{6,0},{7,1},{8,10},{9,11},{10,... | collective-permute-start | bytes 1769480 | tf_op jit(solution)/shard_map/ppermute | solution.py:33
  76.9 15.9 %collective-permute-start.2 = (bf16[1152,256]{0,1:T(8,128)(2,1)}, bf16[1152,256]{0,1:T(8,128)(2,1)}, u32[]{:S(2)}, u32[]{:S(2)}) collective-permute-start(bf16[1152,256]{0,1:T(8,128)(2,1)} %collective-permute-done.1), channel_id=1, source_target_pairs={{0,1},{1,0},{2,3},{3,2},{4,5},{5,4},{6,7},{7,6},{8,9},{9,8},{10,11... | collective-permute-start | bytes 1769480 | tf_op jit(solution)/shard_map/ppermute | solution.py:36
  83.0 25.4 %collective-permute-start.12 = (bf16[1024,512]{0,1:T(8,128)(2,1)S(1)}, bf16[1024,512]{0,1:T(8,128)(2,1)S(1)}, u32[]{:S(2)}, u32[]{:S(2)}) collective-permute-start(bf16[1024,512]{0,1:T(8,128)(2,1)S(1)} %collective-permute-done.11), channel_id=1, source_target_pairs={{0,8},{8,0},{16,24},{24,16},{1,9},{9,1},{17,25},{25,17},{2,10},{10... | collective-permute-start | bytes 3145736 | tf_op jit(solution)/shard_map/ppermute | solution.py:42
  89.6 17.1 %collective-permute-start.4 = (bf16[1152,256]{0,1:T(8,128)(2,1)}, bf16[1152,256]{0,1:T(8,128)(2,1)S(1)}, u32[]{:S(2)}, u32[]{:S(2)}) collective-permute-start(bf16[1152,256]{0,1:T(8,128)(2,1)} %collective-permute-done.3), channel_id=1, source_target_pairs={{0,1},{1,0},{2,3},{3,2},{4,5},{5,4},{6,7},{7,6},{8,9},{9,8},{10,11... | collective-permute-start | bytes 1769480 | tf_op jit(solution)/shard_map/ppermute | solution.py:36
  90.9 14.1 %collective-permute-start.5 = (bf16[1152,256]{0,1:T(8,128)(2,1)}, bf16[1152,256]{0,1:T(8,128)(2,1)S(1)}, u32[]{:S(2)}, u32[]{:S(2)}) collective-permute-start(bf16[1152,256]{0,1:T(8,128)(2,1)} %collective-permute-done.3), channel_id=1, source_target_pairs={{0,2},{1,3},{2,4},{3,5},{4,6},{5,7},{6,0},{7,1},{8,10},{9,11},{10,... | collective-permute-start | bytes 1769480 | tf_op jit(solution)/shard_map/ppermute | solution.py:33
  105.0 16.3 %collective-permute-start.6 = (bf16[1152,256]{0,1:T(8,128)(2,1)S(1)}, bf16[1152,256]{0,1:T(8,128)(2,1)S(1)}, u32[]{:S(2)}, u32[]{:S(2)}) collective-permute-start(bf16[1152,256]{0,1:T(8,128)(2,1)S(1)} %collective-permute-done.5), channel_id=1, source_target_pairs={{0,1},{1,0},{2,3},{3,2},{4,5},{5,4},{6,7},{7,6},{8,9},{9,8},{10,11... | collective-permute-start | bytes 1769480 | tf_op jit(solution)/shard_map/ppermute | solution.py:36
  108.5 12.8 %copy-start.1 = (bf16[1152,2048]{0,1:T(8,128)(2,1)S(1)}, bf16[1152,2048]{0,1:T(8,128)(2,1)}, u32[]{:S(2)}) copy-start(bf16[1152,2048]{0,1:T(8,128)(2,1)} %constant_dynamic-update-slice_fusion.1) | copy-start | bytes 14155780
  111.3 20.8 %collective-permute-start.16 = (f16[1152,256]{0,1:T(8,128)(2,1)S(1)}, f16[1152,256]{0,1:T(8,128)(2,1)S(1)}, u32[]{:S(2)}, u32[]{:S(2)}) collective-permute-start(f16[1152,256]{0,1:T(8,128)(2,1)S(1)} %fusion.30), channel_id=1, source_target_pairs={{0,1},{1,0},{2,3},{3,2},{4,5},{5,4},{6,7},{7,6},{8,9},{9,8},{10,11... | collective-permute-start | bytes 1769480 | tf_op jit(solution)/shard_map/ppermute | solution.py:36
  123.3 24.7 %collective-permute-start.8 = (f32[1024,512]{0,1:T(8,128)S(1)}, f32[1024,512]{0,1:T(8,128)S(1)}, u32[]{:S(2)}, u32[]{:S(2)}) collective-permute-start(f32[1024,512]{0,1:T(8,128)S(1)} %convolution_bitcast_fusion), channel_id=1, source_target_pairs={{0,8},{8,0},{16,24},{24,16},{1,9},{9,1},{17,25},{25,17},{2,10},{10... | collective-permute-start | bytes 6291464 | tf_op jit(solution)/shard_map/ppermute | solution.py:42
  124.2 20.5 %collective-permute-start.15 = (f16[1152,256]{0,1:T(8,128)(2,1)S(1)}, f16[1152,256]{0,1:T(8,128)(2,1)S(1)}, u32[]{:S(2)}, u32[]{:S(2)}) collective-permute-start(f16[1152,256]{0,1:T(8,128)(2,1)S(1)} %fusion.31), channel_id=1, source_target_pairs={{0,1},{1,0},{2,3},{3,2},{4,5},{5,4},{6,7},{7,6},{8,9},{9,8},{10,11... | collective-permute-start | bytes 1769480 | tf_op jit(solution)/shard_map/ppermute | solution.py:36
  126.9 30.4 %collective-permute-start.14 = (f16[1152,256]{0,1:T(8,128)(2,1)S(1)}, f16[1152,256]{0,1:T(8,128)(2,1)S(1)}, u32[]{:S(2)}, u32[]{:S(2)}) collective-permute-start(f16[1152,256]{0,1:T(8,128)(2,1)S(1)} %fusion.32), channel_id=1, source_target_pairs={{0,1},{1,0},{2,3},{3,2},{4,5},{5,4},{6,7},{7,6},{8,9},{9,8},{10,11... | collective-permute-start | bytes 1769480 | tf_op jit(solution)/shard_map/ppermute | solution.py:36
  133.0 12.4 %collective-permute-start.17 = (f16[1152,256]{0,1:T(8,128)(2,1)S(1)}, f16[1152,256]{0,1:T(8,128)(2,1)S(1)}, u32[]{:S(2)}, u32[]{:S(2)}) collective-permute-start(f16[1152,256]{0,1:T(8,128)(2,1)S(1)} %fusion.29), channel_id=1, source_target_pairs={{0,2},{1,3},{2,4},{3,5},{4,6},{5,7},{6,0},{7,1},{8,10},{9,11},{10,... | collective-permute-start | bytes 1769480 | tf_op jit(solution)/shard_map/ppermute | solution.py:33
  134.4 41.7 %collective-permute-start.13 = (f16[1152,256]{0,1:T(8,128)(2,1)S(1)}, f16[1152,256]{0,1:T(8,128)(2,1)S(1)}, u32[]{:S(2)}, u32[]{:S(2)}) collective-permute-start(f16[1152,256]{0,1:T(8,128)(2,1)S(1)} %fusion.33), channel_id=1, source_target_pairs={{0,1},{1,0},{2,3},{3,2},{4,5},{5,4},{6,7},{7,6},{8,9},{9,8},{10,11... | collective-permute-start | bytes 1769480 | tf_op jit(solution)/shard_map/ppermute | solution.py:36
  144.7 38.0 %collective-permute-start.7 = (f32[1024,512]{0,1:T(8,128)}, f32[1024,512]{0,1:T(8,128)}, u32[]{:S(2)}, u32[]{:S(2)}) collective-permute-start(f32[1024,512]{0,1:T(8,128)} %convolution_bitcast_fusion.1), channel_id=1, source_target_pairs={{0,8},{8,0},{16,24},{24,16},{1,9},{9,1},{17,25},{25,17},{2,10},{10... | collective-permute-start | bytes 6291464 | tf_op jit(solution)/shard_map/ppermute | solution.py:42
  146.4 16.9 %collective-permute-start.18 = (f16[1152,256]{0,1:T(8,128)(2,1)S(1)}, f16[1152,256]{0,1:T(8,128)(2,1)S(1)}, u32[]{:S(2)}, u32[]{:S(2)}) collective-permute-start(f16[1152,256]{0,1:T(8,128)(2,1)S(1)} %fusion.23), channel_id=1, source_target_pairs={{0,2},{1,3},{2,4},{3,5},{4,6},{5,7},{6,0},{7,1},{8,10},{9,11},{10,... | collective-permute-start | bytes 1769480 | tf_op jit(solution)/shard_map/ppermute | solution.py:33
  149.8 48.9 %collective-permute-start.9 = (f32[1024,512]{0,1:T(8,128)}, f32[1024,512]{0,1:T(8,128)}, u32[]{:S(2)}, u32[]{:S(2)}) collective-permute-start(f32[1024,512]{0,1:T(8,128)} %bitcast_add_fusion), channel_id=1, source_target_pairs={{0,16},{8,24},{16,0},{24,8},{1,17},{9,25},{17,1},{25,9},{2,18},{10... | collective-permute-start | bytes 6291464 | tf_op jit(solution)/shard_map/ppermute | solution.py:39
  164.3 16.1 %collective-permute-start.19 = (f16[1152,256]{0,1:T(8,128)(2,1)S(1)}, f16[1152,256]{0,1:T(8,128)(2,1)S(1)}, u32[]{:S(2)}, u32[]{:S(2)}) collective-permute-start(f16[1152,256]{0,1:T(8,128)(2,1)S(1)} %fusion.24), channel_id=1, source_target_pairs={{0,2},{1,3},{2,4},{3,5},{4,6},{5,7},{6,0},{7,1},{8,10},{9,11},{10,... | collective-permute-start | bytes 1769480 | tf_op jit(solution)/shard_map/ppermute | solution.py:33

commit v2 on v1

--- a/solution.py
+++ b/solution.py
@@ -44,10 +44,15 @@
     def place(a, index):
         return lax.dynamic_slice(a, (0, index * pair), (a.shape[0], pair))
 
-    most = jnp.stack([jnp.max(jnp.abs(tokens)), jnp.max(jnp.abs(d_kv))]).astype(F32)
-    most = lax.pmax(most, ("dp", "mp"))
+    most = jnp.stack([jnp.max(jnp.abs(a)).astype(F32) for a in (tokens, d_kv, kv_weight)])
+    for flip in (1, 2, 4):
+        most = jnp.maximum(most, lax.ppermute(most, "mp", [(m, m ^ flip) for m in range(8)]))
+    for flip in (1, 2):
+        most = jnp.maximum(most, lax.ppermute(most, "dp", [(d, d ^ flip) for d in range(4)]))
     bound = jnp.maximum(most[0] * most[1] * (rows * 8), 1e-30)
     down, up = 60000.0 / bound, bound / 60000.0
+    kv_bound = jnp.maximum(most[0] * most[2] * (feats * 2), 1e-30)
+    kv_down, kv_up = 60000.0 / kv_bound, kv_bound / 60000.0
 
     block = jnp.transpose(kv_weight, (1, 0, 2)).reshape(feats, 2 * wide)
     ring = []
@@ -56,9 +61,10 @@
         if s < 3:
             block = over_z(block)
 
-    halves = d_kv.reshape(rows, 2, 2, wide)
-    halves = jnp.where(y == 0, halves, halves[:, :, ::-1])
-    own = jnp.transpose(halves, (0, 2, 1, 3)).reshape(rows, pair)
+    both = jnp.transpose(d_kv, (1, 0, 2))
+    low, high = both[:, :, :wide], both[:, :, wide:]
+    first, second = jnp.where(y == 0, low, high), jnp.where(y == 0, high, low)
+    own = jnp.concatenate([first[0], first[1], second[0], second[1]], axis=1)
     across = over_x(own)
     cot = jnp.concatenate([own, over_core(own), across, over_core(across)], axis=1)
 
@@ -77,7 +83,7 @@
     panels = jnp.concatenate(ring, axis=1)
     panel = [place(panels, (z - (me ^ r)) % 4) for r in range(4)]
     far = over_core(dot(tokens, panel[3], 1, 0))
-    far = over_x(dot(tokens, panel[2], 1, 0) + far)
+    far = over_x(((dot(tokens, panel[2], 1, 0) + far) * kv_down).astype(F16)).astype(F32) * kv_up
     near = over_core(dot(tokens, panel[1], 1, 0))
     kv = dot(tokens, panel[0], 1, 0) + near + far
     kv = jnp.transpose(kv.reshape(rows, 2, 2, wide), (0, 2, 1, 3))

time: 205 us -> 173 us (0.84)
  blocking collectives: 51.1 us -> 0 us
  matrix products: 25.1 us -> 34.1 us
  other arithmetic: 13.6 us -> 18.8 us
    pmax x1 -> x0, blocking collectives: 51.1 us -> none  [hops(): most = lax.pmax(most, ('dp', 'mp'))]
    ppermute x2, waiting for transfers between devices: 15.9 us -> 3.35 us  [over_x(): return lax.ppermute(a, 'dp', [(d, d ^ 2) for d in range(4)])]
    dot_general x13, matrix products: 25.1 us -> 34.1 us  [dot(): lax.dot_general(a, b, (((ca,), (cb,)), ((), ())), preferred_element_type=...]
    ppermute x0 -> x5, waiting for transfers between devices: none -> 7.94 us  [the longest x2 4.12 us: hops(): lax.ppermute(most, 'dp', [(d, d ^ flip) for d in range(4)])]
    ppermute x6, waiting for transfers between devices: 25.7 us -> 32.9 us  [over_z(): return lax.ppermute(a, 'mp', [(m, (m + 2) % 8) for m in range(8)])]
    reshape x2 -> x0, local copies, waits for them, and re-layouts: 6.88 us -> none  [hops(): halves = d_kv.reshape(rows, 2, 2, wide)]
    unnamed x14 -> x23, local copies, waits for them, and re-layouts: 13.5 us -> 19.4 us
    ppermute x0 -> x5, starting transfers between devices: none -> 5.23 us  [the longest x3 4.69 us: hops(): lax.ppermute(most, 'mp', [(m, m ^ flip) for m in range(8)])]
  transfers between devices with their start and end apart: 20 -> 25, of which waited for: 10 -> 11; matrix products, arithmetic and copies ran while one was open for 27% -> 41% of each run, Pallas kernels for 0% -> 0%
where the time goes in v2:
time: 173 us; the launch traced here: 172 us
  waiting for transfers between devices  68.4 us (40%)
  matrix products  34.1 us (20%)
  local copies, waits for them, and re-layouts  25.5 us (15%)
  starting transfers between devices  21.7 us (13%)
  other arithmetic  18.8 us (11%)
  between operations  3.39 us (2%)
    dot_general x13, matrix products, dot(): lax.dot_general(a, b, (((ca,), (cb,)), ((), ())), preferred_element_type=...  34.1 us
    ppermute x6, waiting for transfers between devices, over_z(): return lax.ppermute(a, 'mp', [(m, (m + 2) % 8) for m in range(8)])  32.9 us
    ppermute x8, waiting for transfers between devices, over_y(): return lax.ppermute(a, 'mp', [(m, m ^ 1) for m in range(8)])  24.2 us
    unnamed x23, local copies, waits for them, and re-layouts  19.4 us
    ppermute x8, starting transfers between devices, over_y(): return lax.ppermute(a, 'mp', [(m, m ^ 1) for m in range(8)])  9.44 us
    reduce_max x3, other arithmetic, hops(): jnp.max(jnp.abs(a)).astype(F32)  6.75 us
    ppermute x3, starting transfers between devices, hops(): lax.ppermute(most, 'mp', [(m, m ^ flip) for m in range(8)])  4.69 us
    ppermute x2, waiting for transfers between devices, hops(): lax.ppermute(most, 'dp', [(d, d ^ flip) for d in range(4)])  4.12 us
  transfers between devices with their start and end apart: 25, of which 11 were waited for; matrix products, arithmetic and copies ran while one was open for 41% of the time, Pallas kernels for 0%

profile of v2, /device:TPU:0, one launch (start us, length us, event | category | flops | bytes accessed | tf_op | source)
XLA Modules:
  0.0 171.9 jit_solution(2455430556435482041)
XLA Ops:
  3.7 2.5 %collective-permute-start.16 = (bf16[1024,512]{1,0:T(8,128)(2,1)}, bf16[1024,512]{1,0:T(8,128)(2,1)}, u32[]{:S(2)}, u32[]{:S(2)}) collective-permute-start(bf16[1024,512]{1,0:T(8,128)(2,1)} %pad_maximum_fusion), channel_id=1, source_target_pairs={{0,16},{8,24},{16,0},{24,8},{1,17},{9,25},{17,1},{25,9},{2,18},{10... | collective-permute-start | bytes 3145736 | tf_op jit(solution)/shard_map/ppermute | solution.py:39
  6.2 2.1 %copy.13 = bf16[2,1152,128]{1,2,0:T(8,128)(2,1)} copy(bf16[2,1152,128]{2,1,0:T(8,128)(2,1)} %param.4) | data formatting | bytes 1179648 | tf_op args[1]
  11.4 4.1 %abs_reduce_fusion.1 = bf16[]{:T(256)} fusion(bf16[1024,2,256]{2,1,0:T(2,128)(2,1)} %param.5), kind=kLoop, calls=%fused_computation.52 | loop fusion | flops 1048575 | bytes 1048578 | tf_op jit(solution)/shard_map/reduce_max | solution.py:47
  18.2 2.0 %maximum_convert_fusion = f32[3]{0:T(128)S(1)} fusion(bf16[1]{0:T(256)(128)(2,1)} %bitcast.9, bf16[1]{0:T(256)(128)(2,1)} %bitcast.8, bf16[1]{0:T(256)(128)(2,1)} %bitcast.7), kind=kLoop, calls=%fused_computation.95 | loop fusion | flops 18 | bytes 18 | tf_op jit(solution)/shard_map/stack | solution.py:47
  24.7 2.0 %fusion.75 = f32[3]{0:T(128)S(1)} fusion(f32[3]{0:T(128)S(1)} %collective-permute-done.9, bf16[1]{0:T(256)(128)(2,1)} %bitcast.9, bf16[1]{0:T(256)(128)(2,1)} %bitcast.8, bf16[1]{0:T(256)(128)(2,1)} %bitcast.7), kind=kLoop, calls=%fused_computation.100 | loop fusion | flops 21 | bytes 30 | tf_op jit(solution)/shard_map/max | solution.py:49
  28.3 2.0 %collective-permute-done.10 = f32[3]{0:T(128)S(1)} collective-permute-done((f32[3]{0:T(128)S(1)}, f32[3]{0:T(128)S(1)}, u32[]{:S(2)}, u32[]{:S(2)}) %collective-permute-start.10) | collective-permute-done | bytes 44 | tf_op jit(solution)/shard_map/ppermute | solution.py:49
  30.2 2.0 %fusion.76 = f32[3]{0:T(128)S(1)} fusion(f32[3]{0:T(128)S(1)} %collective-permute-done.10, f32[3]{0:T(128)S(1)} %collective-permute-done.9, bf16[1]{0:T(256)(128)(2,1)} %bitcast.9, bf16[1]{0:T(256)(128)(2,1)} %bitcast.8, bf16[1]{0:T(256)(128)(2,1)} %bitcast.7), kind=kLoop, calls=%fused_computation.101 | loop fusion | flops 24 | bytes 42 | tf_op jit(solution)/shard_map/max | solution.py:49
  32.3 2.6 %collective-permute-start.11 = (f32[3]{0:T(128)S(1)}, f32[3]{0:T(128)S(1)}, u32[]{:S(2)}, u32[]{:S(2)}) collective-permute-start(f32[3]{0:T(128)S(1)} %fusion.76), channel_id=1, source_target_pairs={{0,4},{1,5},{2,6},{3,7},{4,0},{5,1},{6,2},{7,3},{8,12},{9,13},{10,... | collective-permute-start | bytes 44 | tf_op jit(solution)/shard_map/ppermute | solution.py:49
  38.4 3.0 %collective-permute-done.13 = f32[3]{0:T(128)S(1)} collective-permute-done((f32[3]{0:T(128)S(1)}, f32[3]{0:T(128)S(1)}, u32[]{:S(2)}, u32[]{:S(2)}) %collective-permute-start.13) | collective-permute-done | bytes 44 | tf_op jit(solution)/shard_map/ppermute | solution.py:51
  47.8 1.9 %constant_dynamic-update-slice_fusion.6 = bf16[1152,2048]{0,1:T(8,128)(2,1)} fusion(bf16[1152,2048]{0,1:T(8,128)(2,1)} %constant_dynamic-update-slice_fusion.7, bf16[1152,256]{0,1:T(8,128)(2,1)} %collective-permute-done), kind=kLoop, calls=%fused_computation.74 | loop fusion | bytes 1179648
  49.7 1.9 %constant_dynamic-update-slice_fusion.5 = bf16[1152,2048]{0,1:T(8,128)(2,1)} fusion(bf16[1152,2048]{0,1:T(8,128)(2,1)} %constant_dynamic-update-slice_fusion.6, bf16[1152,256]{0,1:T(8,128)(2,1)} %collective-permute-done.1), kind=kLoop, calls=%fused_computation.73 | loop fusion | bytes 1179648
  51.6 2.3 %constant_dynamic-update-slice_fusion.10 = bf16[1024,2048]{1,0:T(8,128)(2,1)} fusion(bf16[1024,2048]{1,0:T(8,128)(2,1)} %constant_dynamic-update-slice_fusion.11, bf16[1024,512]{1,0:T(8,128)(2,1)} %collective-permute-done.15), kind=kLoop, calls=%fused_computation.78 | loop fusion | bytes 2097152
  54.0 8.2 %collective-permute-done.3 = bf16[1152,256]{0,1:T(8,128)(2,1)S(1)} collective-permute-done((bf16[1152,256]{0,1:T(8,128)(2,1)}, bf16[1152,256]{0,1:T(8,128)(2,1)S(1)}, u32[]{:S(2)}, u32[]{:S(2)}) %collective-permute-start.3) | collective-permute-done | bytes 589856 | tf_op jit(solution)/shard_map/ppermute | solution.py:33
  62.7 2.3 %constant_dynamic-update-slice_fusion.9 = bf16[1024,2048]{1,0:T(8,128)(2,1)} fusion(bf16[1024,2048]{1,0:T(8,128)(2,1)} %constant_dynamic-update-slice_fusion.10, bf16[1024,512]{1,0:T(8,128)(2,1)} %collective-permute-done.16), kind=kLoop, calls=%fused_computation.77 | loop fusion | bytes 2097152
  66.8 10.5 %collective-permute-done.5 = bf16[1152,256]{0,1:T(8,128)(2,1)S(1)} collective-permute-done((bf16[1152,256]{0,1:T(8,128)(2,1)S(1)}, bf16[1152,256]{0,1:T(8,128)(2,1)S(1)}, u32[]{:S(2)}, u32[]{:S(2)}) %collective-permute-start.5) | collective-permute-done | bytes 589856 | tf_op jit(solution)/shard_map/ppermute | solution.py:33
  81.7 2.4 %fusion.31 = f16[1152,256]{0,1:T(8,128)(2,1)S(1)} fusion(bf16[1024,1152]{1,0:T(8,128)(2,1)S(1)} %copy-done, f32[]{:T(128)} %bitcast.20, bf16[1024,2048]{1,0:T(8,128)(2,1)} %constant_dynamic-update-slice_fusion.8, s32[]{:T(128)S(6)} %add.122), kind=kOutput, calls=%fused_computation.38 | convolution fusion | flops 604569600 | bytes 3473924 | tf_op jit(solution)/shard_map/dot_general | solution.py:21
  84.7 1.9 %fusion.30 = f16[1152,256]{0,1:T(8,128)(2,1)S(1)} fusion(bf16[1024,1152]{1,0:T(8,128)(2,1)S(1)} %copy-done, f32[]{:T(128)} %bitcast.20, bf16[1024,2048]{1,0:T(8,128)(2,1)} %constant_dynamic-update-slice_fusion.8, s32[]{:T(128)S(6)} %add.123), kind=kOutput, calls=%fused_computation.37 | convolution fusion | flops 604569600 | bytes 3473924 | tf_op jit(solution)/shard_map/dot_general | solution.py:21
  88.2 5.4 %collective-permute-done.6 = bf16[1152,256]{0,1:T(8,128)(2,1)S(1)} collective-permute-done((bf16[1152,256]{0,1:T(8,128)(2,1)S(1)}, bf16[1152,256]{0,1:T(8,128)(2,1)S(1)}, u32[]{:S(2)}, u32[]{:S(2)}) %collective-permute-start.6) | collective-permute-done | bytes 589856 | tf_op jit(solution)/shard_map/ppermute | solution.py:36
  95.7 18.8 %collective-permute-done.21 = f16[1152,256]{0,1:T(8,128)(2,1)S(1)} collective-permute-done((f16[1152,256]{0,1:T(8,128)(2,1)S(1)}, f16[1152,256]{0,1:T(8,128)(2,1)S(1)}, u32[]{:S(2)}, u32[]{:S(2)}) %collective-permute-start.21) | collective-permute-done | bytes 589856 | tf_op jit(solution)/shard_map/ppermute | solution.py:36
  114.5 1.9 %fusion.29 = f16[1152,256]{0,1:T(8,128)(2,1)S(1)} fusion(bf16[1024,1152]{1,0:T(8,128)(2,1)S(1)} %copy-done, f16[1152,256]{0,1:T(8,128)(2,1)S(1)} %collective-permute-done.21, f32[]{:T(128)} %bitcast.20, bf16[1024,2048]{1,0:T(8,128)(2,1)} %constant_dynamic-update-slice_fusion.8, s32[]{:T(128)S(6)} %select_n.109), kind=kOutput, calls=%fused_computation.36 | convolution fusion | flops 605159424 | bytes 4063748 | tf_op jit(solution)/shard_map/dot_general | solution.py:21
  116.5 1.9 %fusion.32 = f16[1152,256]{0,1:T(8,128)(2,1)S(1)} fusion(bf16[1024,1152]{1,0:T(8,128)(2,1)S(1)} %copy-done, f32[]{:T(128)} %bitcast.20, bf16[1024,2048]{1,0:T(8,128)(2,1)} %constant_dynamic-update-slice_fusion.8, s32[]{:T(128)S(6)} %add.121), kind=kOutput, calls=%fused_computation.39 | convolution fusion | flops 604569600 | bytes 3473924 | tf_op jit(solution)/shard_map/dot_general | solution.py:21
  120.0 1.9 %fusion.33 = f16[1152,256]{0,1:T(8,128)(2,1)S(1)} fusion(bf16[1024,1152]{1,0:T(8,128)(2,1)S(1)} %copy-done, f32[]{:T(128)} %bitcast.20, bf16[1024,2048]{1,0:T(8,128)(2,1)} %constant_dynamic-update-slice_fusion.8, s32[]{:T(128)S(6)} %add.120), kind=kOutput, calls=%fused_computation.40 | convolution fusion | flops 604569600 | bytes 3473924 | tf_op jit(solution)/shard_map/dot_general | solution.py:21
  122.5 6.7 %collective-permute-done.22 = f16[1152,256]{0,1:T(8,128)(2,1)S(1)} collective-permute-done((f16[1152,256]{0,1:T(8,128)(2,1)S(1)}, f16[1152,256]{0,1:T(8,128)(2,1)S(1)}, u32[]{:S(2)}, u32[]{:S(2)}) %collective-permute-start.22) | collective-permute-done | bytes 589856 | tf_op jit(solution)/shard_map/ppermute | solution.py:33
  129.2 2.0 %fusion.23 = f16[1152,256]{0,1:T(8,128)(2,1)S(1)} fusion(bf16[1024,1152]{1,0:T(8,128)(2,1)S(1)} %copy-done, f16[1152,256]{0,1:T(8,128)(2,1)S(1)} %collective-permute-done.22, f16[1152,256]{0,1:T(8,128)(2,1)S(1)} %collective-permute-done.20, f32[]{:T(128)} %bitcast.20, bf16[1024,2048]{1,0:T(8,128)(2,1)} %constant_dynamic-update-slice_fusion.8, s32[]{:T(128)S(6)} %select_n.107), kind=kOutput, calls=%fused_computation.30 | convolution fusion | flops 605749248 | bytes 4653572 | tf_op jit(solution)/shard_map/dot_general | solution.py:21
  131.5 2.9 %convolution_bitcast_fusion.1 = f32[1024,512]{0,1:T(8,128)} fusion(bf16[1152,512]{0,1:T(8,128)(2,1)S(1)} %get-tuple-element.5, bf16[1024,1152]{1,0:T(8,128)(2,1)S(1)} %copy-done), kind=kOutput, calls=%fused_computation.49 | convolution fusion | flops 1207959552 | bytes 5636096 | tf_op jit(solution)/shard_map/dot_general | solution.py:21
  136.0 7.4 %collective-permute-done.23 = f16[1152,256]{0,1:T(8,128)(2,1)S(1)} collective-permute-done((f16[1152,256]{0,1:T(8,128)(2,1)S(1)}, f16[1152,256]{0,1:T(8,128)(2,1)S(1)}, u32[]{:S(2)}, u32[]{:S(2)}) %collective-permute-start.23) | collective-permute-done | bytes 589856 | tf_op jit(solution)/shard_map/ppermute | solution.py:33
  143.4 2.0 %fusion.24 = f16[1152,256]{0,1:T(8,128)(2,1)S(1)} fusion(bf16[1024,1152]{1,0:T(8,128)(2,1)S(1)} %copy-done, f16[1152,256]{0,1:T(8,128)(2,1)S(1)} %collective-permute-done.23, f16[1152,256]{0,1:T(8,128)(2,1)S(1)} %collective-permute-done.19, f32[]{:T(128)} %bitcast.20, bf16[1024,2048]{1,0:T(8,128)(2,1)} %constant_dynamic-update-slice_fusion.8, s32[]{:T(128)S(6)} %select_n.105), kind=kOutput, calls=%fused_computation.31 | convolution fusion | flops 605749248 | bytes 4653572 | tf_op jit(solution)/shard_map/dot_general | solution.py:21
  147.5 9.2 %fusion.8 = bf16[1024,1152]{1,0:T(8,128)(2,1)} fusion(bf16[1024,2048]{1,0:T(8,128)(2,1)} %constant_dynamic-update-slice_fusion.8, bf16[1152,512]{0,1:T(8,128)(2,1)S(1)} %get-tuple-element.4, bf16[1152,512]{0,1:T(8,128)(2,1)S(1)} %get-tuple-element.3, bf16[1152,512]{0,1:T(8,128)(2,1)S(1)} %get-tuple-element.5, bf16[1152,512]{0,1:T(8,128)(2,1)S(1)} %get-tuple-element.6), kind=kOutput, calls=%fused_computation.8 | convolution fusion | flops 4851892224 | bytes 11272192 | tf_op jit(solution)/shard_map/dot_general | solution.py:21
  156.6 2.9 %fusion.56 = f32[512,1024]{1,0:T(8,128)} fusion(bf16[1152,512]{0,1:T(8,128)(2,1)S(1)} %get-tuple-element.6, bf16[1024,1152]{1,0:T(8,128)(2,1)S(1)} %copy-done), kind=kOutput, calls=%fused_computation.98 | convolution fusion | flops 1207959552 | bytes 5636096 | tf_op jit(solution)/shard_map/dot_general | solution.py:21
  159.5 2.0 %fusion.14 = f32[1152,256]{0,1:T(8,128)S(1)} fusion(bf16[1024,1152]{1,0:T(8,128)(2,1)S(1)} %copy-done, f16[1152,256]{0,1:T(8,128)(2,1)S(1)} %collective-permute-done.24, f16[1152,256]{0,1:T(8,128)(2,1)S(1)} %collective-permute-done.18, f32[]{:T(128)} %bitcast.29, f32[]{:T(128)} %bitcast.20, bf16[1024,2048]{1,0:T(8,128)(2,1)} %constant_dynamic-update-slice_fusion.8, ...), kind=kOutput, calls=%fused_computation.21 | convolution fusion | flops 605749248 | bytes 5243908 | tf_op jit(solution)/shard_map/dot_general | solution.py:21
  162.9 3.3 %collective-permute-done.14 = f16[1024,512]{0,1:T(8,128)(2,1)} collective-permute-done((f16[1024,512]{0,1:T(8,128)(2,1)}, f16[1024,512]{0,1:T(8,128)(2,1)}, u32[]{:S(2)}, u32[]{:S(2)}) %collective-permute-start.14) | collective-permute-done | bytes 1048608 | tf_op jit(solution)/shard_map/ppermute | solution.py:39
  166.2 3.1 %fusion.37 = bf16[1024,512]{0,1:T(8,128)(2,1)S(1)} fusion(f32[1024,512]{0,1:T(8,128)} %collective-permute-done.7, f32[512,1024]{1,0:T(8,128)} %fusion.56, f16[1024,512]{0,1:T(8,128)(2,1)} %collective-permute-done.14, f32[]{:T(128)} %bitcast.11), kind=kLoop, calls=%fused_computation.47 | loop fusion | flops 2621440 | bytes 6291460 | tf_op jit(solution)/shard_map/add | solution.py:88
  (77 shorter events, 43.1 us)
Async XLA Ops:
  2.2 15.1 %copy-start = (bf16[1024,1152]{1,0:T(8,128)(2,1)S(1)}, bf16[1024,1152]{1,0:T(8,128)(2,1)}, u32[]{:S(2)}) copy-start(bf16[1024,1152]{1,0:T(8,128)(2,1)} %param.3) | copy-start | bytes 7077892
  3.3 48.4 %collective-permute-start.15 = (bf16[1024,512]{1,0:T(8,128)(2,1)}, bf16[1024,512]{1,0:T(8,128)(2,1)}, u32[]{:S(2)}, u32[]{:S(2)}) collective-permute-start(bf16[1024,512]{1,0:T(8,128)(2,1)} %pad_maximum_fusion), channel_id=1, source_target_pairs={{0,8},{8,0},{16,24},{24,16},{1,9},{9,1},{17,25},{25,17},{2,10},{10... | collective-permute-start | bytes 3145736 | tf_op jit(solution)/shard_map/ppermute | solution.py:42
  3.7 47.9 %collective-permute-start.16 = (bf16[1024,512]{1,0:T(8,128)(2,1)}, bf16[1024,512]{1,0:T(8,128)(2,1)}, u32[]{:S(2)}, u32[]{:S(2)}) collective-permute-start(bf16[1024,512]{1,0:T(8,128)(2,1)} %pad_maximum_fusion), channel_id=1, source_target_pairs={{0,16},{8,24},{16,0},{24,8},{1,17},{9,25},{17,1},{25,9},{2,18},{10... | collective-permute-start | bytes 3145736 | tf_op jit(solution)/shard_map/ppermute | solution.py:39
  8.3 13.1 %copy-start.1 = (bf16[2,1152,128]{1,2,0:T(8,128)(2,1)S(1)}, bf16[2,1152,128]{1,2,0:T(8,128)(2,1)}, u32[]{:S(2)}) copy-start(bf16[2,1152,128]{1,2,0:T(8,128)(2,1)} %copy.13) | copy-start | bytes 1769476
  8.3 39.4 %collective-permute-start = (bf16[1152,256]{0,1:T(8,128)(2,1)}, bf16[1152,256]{0,1:T(8,128)(2,1)}, u32[]{:S(2)}, u32[]{:S(2)}) collective-permute-start(bf16[1152,256]{0,1:T(8,128)(2,1)} %bitcast.108), channel_id=1, source_target_pairs={{0,1},{1,0},{2,3},{3,2},{4,5},{5,4},{6,7},{7,6},{8,9},{9,8},{10,11... | collective-permute-start | bytes 1769480 | tf_op jit(solution)/shard_map/ppermute | solution.py:36
  9.9 34.7 %collective-permute-start.1 = (bf16[1152,256]{0,1:T(8,128)(2,1)}, bf16[1152,256]{0,1:T(8,128)(2,1)}, u32[]{:S(2)}, u32[]{:S(2)}) collective-permute-start(bf16[1152,256]{0,1:T(8,128)(2,1)} %bitcast.109), channel_id=1, source_target_pairs={{0,2},{1,3},{2,4},{3,5},{4,6},{5,7},{6,0},{7,1},{8,10},{9,11},{10,... | collective-permute-start | bytes 1769480 | tf_op jit(solution)/shard_map/ppermute | solution.py:33
  20.2 4.4 %collective-permute-start.9 = (f32[3]{0:T(128)S(1)}, f32[3]{0:T(128)S(1)}, u32[]{:S(2)}, u32[]{:S(2)}) collective-permute-start(f32[3]{0:T(128)S(1)} %maximum_convert_fusion), channel_id=1, source_target_pairs={{0,1},{1,0},{2,3},{3,2},{4,5},{5,4},{6,7},{7,6},{8,9},{9,8},{10,11... | collective-permute-start | bytes 44 | tf_op jit(solution)/shard_map/ppermute | solution.py:49
  26.7 3.5 %collective-permute-start.10 = (f32[3]{0:T(128)S(1)}, f32[3]{0:T(128)S(1)}, u32[]{:S(2)}, u32[]{:S(2)}) collective-permute-start(f32[3]{0:T(128)S(1)} %fusion.75), channel_id=1, source_target_pairs={{0,2},{1,3},{2,0},{3,1},{4,6},{5,7},{6,4},{7,5},{8,10},{9,11},{10,... | collective-permute-start | bytes 44 | tf_op jit(solution)/shard_map/ppermute | solution.py:49
  32.3 4.4 %collective-permute-start.11 = (f32[3]{0:T(128)S(1)}, f32[3]{0:T(128)S(1)}, u32[]{:S(2)}, u32[]{:S(2)}) collective-permute-start(f32[3]{0:T(128)S(1)} %fusion.76), channel_id=1, source_target_pairs={{0,4},{1,5},{2,6},{3,7},{4,0},{5,1},{6,2},{7,3},{8,12},{9,13},{10,... | collective-permute-start | bytes 44 | tf_op jit(solution)/shard_map/ppermute | solution.py:49
  36.7 1.1 collective-permute-start.12
  37.9 3.5 %collective-permute-start.13 = (f32[3]{0:T(128)S(1)}, f32[3]{0:T(128)S(1)}, u32[]{:S(2)}, u32[]{:S(2)}) collective-permute-start(f32[3]{0:T(128)S(1)} %max.26), channel_id=1, source_target_pairs={{0,16},{8,24},{16,0},{24,8},{1,17},{9,25},{17,1},{25,9},{2,18},{10... | collective-permute-start | bytes 44 | tf_op jit(solution)/shard_map/ppermute | solution.py:51
  44.6 20.5 %collective-permute-start.2 = (bf16[1152,256]{0,1:T(8,128)(2,1)}, bf16[1152,256]{0,1:T(8,128)(2,1)S(1)}, u32[]{:S(2)}, u32[]{:S(2)}) collective-permute-start(bf16[1152,256]{0,1:T(8,128)(2,1)} %collective-permute-done.1), channel_id=1, source_target_pairs={{0,1},{1,0},{2,3},{3,2},{4,5},{5,4},{6,7},{7,6},{8,9},{9,8},{10,11... | collective-permute-start | bytes 1769480 | tf_op jit(solution)/shard_map/ppermute | solution.py:36
  46.2 16.0 %collective-permute-start.3 = (bf16[1152,256]{0,1:T(8,128)(2,1)}, bf16[1152,256]{0,1:T(8,128)(2,1)S(1)}, u32[]{:S(2)}, u32[]{:S(2)}) collective-permute-start(bf16[1152,256]{0,1:T(8,128)(2,1)} %collective-permute-done.1), channel_id=1, source_target_pairs={{0,2},{1,3},{2,4},{3,5},{4,6},{5,7},{6,0},{7,1},{8,10},{9,11},{10,... | collective-permute-start | bytes 1769480 | tf_op jit(solution)/shard_map/ppermute | solution.py:33
  51.6 28.9 %collective-permute-start.17 = (bf16[1024,512]{1,0:T(8,128)(2,1)}, bf16[1024,512]{1,0:T(8,128)(2,1)S(1)}, u32[]{:S(2)}, u32[]{:S(2)}) collective-permute-start(bf16[1024,512]{1,0:T(8,128)(2,1)} %collective-permute-done.16), channel_id=1, source_target_pairs={{0,8},{8,0},{16,24},{24,16},{1,9},{9,1},{17,25},{25,17},{2,10},{10... | collective-permute-start | bytes 3145736 | tf_op jit(solution)/shard_map/ppermute | solution.py:42
  62.2 16.6 %collective-permute-start.4 = (bf16[1152,256]{0,1:T(8,128)(2,1)S(1)}, bf16[1152,256]{0,1:T(8,128)(2,1)S(1)}, u32[]{:S(2)}, u32[]{:S(2)}) collective-permute-start(bf16[1152,256]{0,1:T(8,128)(2,1)S(1)} %collective-permute-done.3), channel_id=1, source_target_pairs={{0,1},{1,0},{2,3},{3,2},{4,5},{5,4},{6,7},{7,6},{8,9},{9,8},{10,11... | collective-permute-start | bytes 1769480 | tf_op jit(solution)/shard_map/ppermute | solution.py:36
  62.7 14.6 %collective-permute-start.5 = (bf16[1152,256]{0,1:T(8,128)(2,1)S(1)}, bf16[1152,256]{0,1:T(8,128)(2,1)S(1)}, u32[]{:S(2)}, u32[]{:S(2)}) collective-permute-start(bf16[1152,256]{0,1:T(8,128)(2,1)S(1)} %collective-permute-done.3), channel_id=1, source_target_pairs={{0,2},{1,3},{2,4},{3,5},{4,6},{5,7},{6,0},{7,1},{8,10},{9,11},{10,... | collective-permute-start | bytes 1769480 | tf_op jit(solution)/shard_map/ppermute | solution.py:33
  77.3 16.3 %collective-permute-start.6 = (bf16[1152,256]{0,1:T(8,128)(2,1)S(1)}, bf16[1152,256]{0,1:T(8,128)(2,1)S(1)}, u32[]{:S(2)}, u32[]{:S(2)}) collective-permute-start(bf16[1152,256]{0,1:T(8,128)(2,1)S(1)} %collective-permute-done.5), channel_id=1, source_target_pairs={{0,1},{1,0},{2,3},{3,2},{4,5},{5,4},{6,7},{7,6},{8,9},{9,8},{10,11... | collective-permute-start | bytes 1769480 | tf_op jit(solution)/shard_map/ppermute | solution.py:36
  80.6 13.0 %slice-start = ((s8[4718592]{0:T(1024)(128)(4,1)}), s8[4194304]{0:T(1024)(128)(4,1)S(1)}, s32[]{:S(2)}) async-start(s8[4718592]{0:T(1024)(128)(4,1)} %bitcast.103), calls=%async_computation | async-start | bytes 8388608
  81.7 11.9 %slice-start.1 = ((s8[4718592]{0:T(1024)(128)(4,1)}), s8[524288]{0:T(1024)(128)(4,1)S(1)}, s32[]{:S(2)}) async-start(s8[4718592]{0:T(1024)(128)(4,1)} %bitcast.103), calls=%async_computation.1 | async-start | bytes 1048576
  84.1 38.4 %collective-permute-start.20 = (f16[1152,256]{0,1:T(8,128)(2,1)S(1)}, f16[1152,256]{0,1:T(8,128)(2,1)S(1)}, u32[]{:S(2)}, u32[]{:S(2)}) collective-permute-start(f16[1152,256]{0,1:T(8,128)(2,1)S(1)} %fusion.31), channel_id=1, source_target_pairs={{0,1},{1,0},{2,3},{3,2},{4,5},{5,4},{6,7},{7,6},{8,9},{9,8},{10,11... | collective-permute-start | bytes 1769480 | tf_op jit(solution)/shard_map/ppermute | solution.py:36
  86.6 27.9 %collective-permute-start.21 = (f16[1152,256]{0,1:T(8,128)(2,1)S(1)}, f16[1152,256]{0,1:T(8,128)(2,1)S(1)}, u32[]{:S(2)}, u32[]{:S(2)}) collective-permute-start(f16[1152,256]{0,1:T(8,128)(2,1)S(1)} %fusion.30), channel_id=1, source_target_pairs={{0,1},{1,0},{2,3},{3,2},{4,5},{5,4},{6,7},{7,6},{8,9},{9,8},{10,11... | collective-permute-start | bytes 1769480 | tf_op jit(solution)/shard_map/ppermute | solution.py:36
  95.6 49.9 %collective-permute-start.8 = (f32[1024,512]{0,1:T(8,128)S(1)}, f32[1024,512]{0,1:T(8,128)S(1)}, u32[]{:S(2)}, u32[]{:S(2)}) collective-permute-start(f32[1024,512]{0,1:T(8,128)S(1)} %convolution_bitcast_fusion), channel_id=1, source_target_pairs={{0,8},{8,0},{16,24},{24,16},{1,9},{9,1},{17,25},{25,17},{2,10},{10... | collective-permute-start | bytes 6291464 | tf_op jit(solution)/shard_map/ppermute | solution.py:42
  116.4 12.8 %collective-permute-start.22 = (f16[1152,256]{0,1:T(8,128)(2,1)S(1)}, f16[1152,256]{0,1:T(8,128)(2,1)S(1)}, u32[]{:S(2)}, u32[]{:S(2)}) collective-permute-start(f16[1152,256]{0,1:T(8,128)(2,1)S(1)} %fusion.29), channel_id=1, source_target_pairs={{0,2},{1,3},{2,4},{3,5},{4,6},{5,7},{6,0},{7,1},{8,10},{9,11},{10,... | collective-permute-start | bytes 1769480 | tf_op jit(solution)/shard_map/ppermute | solution.py:33
  118.4 17.6 %collective-permute-start.19 = (f16[1152,256]{0,1:T(8,128)(2,1)S(1)}, f16[1152,256]{0,1:T(8,128)(2,1)S(1)}, u32[]{:S(2)}, u32[]{:S(2)}) collective-permute-start(f16[1152,256]{0,1:T(8,128)(2,1)S(1)} %fusion.32), channel_id=1, source_target_pairs={{0,1},{1,0},{2,3},{3,2},{4,5},{5,4},{6,7},{7,6},{8,9},{9,8},{10,11... | collective-permute-start | bytes 1769480 | tf_op jit(solution)/shard_map/ppermute | solution.py:36
  121.9 37.6 %collective-permute-start.18 = (f16[1152,256]{0,1:T(8,128)(2,1)S(1)}, f16[1152,256]{0,1:T(8,128)(2,1)S(1)}, u32[]{:S(2)}, u32[]{:S(2)}) collective-permute-start(f16[1152,256]{0,1:T(8,128)(2,1)S(1)} %fusion.33), channel_id=1, source_target_pairs={{0,1},{1,0},{2,3},{3,2},{4,5},{5,4},{6,7},{7,6},{8,9},{9,8},{10,11... | collective-permute-start | bytes 1769480 | tf_op jit(solution)/shard_map/ppermute | solution.py:36
  131.3 12.1 %collective-permute-start.23 = (f16[1152,256]{0,1:T(8,128)(2,1)S(1)}, f16[1152,256]{0,1:T(8,128)(2,1)S(1)}, u32[]{:S(2)}, u32[]{:S(2)}) collective-permute-start(f16[1152,256]{0,1:T(8,128)(2,1)S(1)} %fusion.23), channel_id=1, source_target_pairs={{0,2},{1,3},{2,4},{3,5},{4,6},{5,7},{6,0},{7,1},{8,10},{9,11},{10,... | collective-permute-start | bytes 1769480 | tf_op jit(solution)/shard_map/ppermute | solution.py:33
  134.4 28.5 %collective-permute-start.7 = (f32[1024,512]{0,1:T(8,128)}, f32[1024,512]{0,1:T(8,128)}, u32[]{:S(2)}, u32[]{:S(2)}) collective-permute-start(f32[1024,512]{0,1:T(8,128)} %convolution_bitcast_fusion.1), channel_id=1, source_target_pairs={{0,8},{8,0},{16,24},{24,16},{1,9},{9,1},{17,25},{25,17},{2,10},{10... | collective-permute-start | bytes 6291464 | tf_op jit(solution)/shard_map/ppermute | solution.py:42
  145.4 14.1 %collective-permute-start.24 = (f16[1152,256]{0,1:T(8,128)(2,1)S(1)}, f16[1152,256]{0,1:T(8,128)(2,1)S(1)}, u32[]{:S(2)}, u32[]{:S(2)}) collective-permute-start(f16[1152,256]{0,1:T(8,128)(2,1)S(1)} %fusion.24), channel_id=1, source_target_pairs={{0,2},{1,3},{2,4},{3,5},{4,6},{5,7},{6,0},{7,1},{8,10},{9,11},{10,... | collective-permute-start | bytes 1769480 | tf_op jit(solution)/shard_map/ppermute | solution.py:33
  146.9 19.3 %collective-permute-start.14 = (f16[1024,512]{0,1:T(8,128)(2,1)}, f16[1024,512]{0,1:T(8,128)(2,1)}, u32[]{:S(2)}, u32[]{:S(2)}) collective-permute-start(f16[1024,512]{0,1:T(8,128)(2,1)} %fusion.36), channel_id=1, source_target_pairs={{0,16},{8,24},{16,0},{24,8},{1,17},{9,25},{17,1},{25,9},{2,18},{10... | collective-permute-start | bytes 3145736 | tf_op jit(solution)/shard_map/ppermute | solution.py:39

commit v3 on v2

--- a/solution.py
+++ b/solution.py
@@ -19,6 +19,12 @@
 
 def dot(a, b, ca, cb):
     return lax.dot_general(a, b, (((ca,), (cb,)), ((), ())), preferred_element_type=F32)
+
+
+def after(value, *arrays):
+    for a in arrays:
+        value = value + 0.0 * a[0, 0].astype(F32)
+    return value
 
 
 def hops(tokens, kv_weight, d_kv):
@@ -44,21 +50,12 @@
     def place(a, index):
         return lax.dynamic_slice(a, (0, index * pair), (a.shape[0], pair))
 
-    most = jnp.stack([jnp.max(jnp.abs(a)).astype(F32) for a in (tokens, d_kv, kv_weight)])
-    for flip in (1, 2, 4):
-        most = jnp.maximum(most, lax.ppermute(most, "mp", [(m, m ^ flip) for m in range(8)]))
-    for flip in (1, 2):
-        most = jnp.maximum(most, lax.ppermute(most, "dp", [(d, d ^ flip) for d in range(4)]))
-    bound = jnp.maximum(most[0] * most[1] * (rows * 8), 1e-30)
-    down, up = 60000.0 / bound, bound / 60000.0
-    kv_bound = jnp.maximum(most[0] * most[2] * (feats * 2), 1e-30)
-    kv_down, kv_up = 60000.0 / kv_bound, kv_bound / 60000.0
-
     block = jnp.transpose(kv_weight, (1, 0, 2)).reshape(feats, 2 * wide)
     ring = []
     for s in range(4):
-        ring += [block, over_y(block)]
+        ring += [block]
         if s < 3:
+            ring += [over_y(block)]
             block = over_z(block)
 
     both = jnp.transpose(d_kv, (1, 0, 2))
@@ -68,22 +65,40 @@
     across = over_x(own)
     cot = jnp.concatenate([own, over_core(own), across, over_core(across)], axis=1)
 
+    most = jnp.stack([jnp.max(jnp.abs(a)).astype(F32) for a in (tokens, own, ring[0])])
+    for flip in (1, 2):
+        most = jnp.maximum(most, lax.ppermute(most, "dp", [(d, d ^ flip) for d in range(4)]))
+    for flip in (1, 2, 4):
+        if flip == 2:
+            most = after(most, ring[2], across)
+        most = jnp.maximum(most, lax.ppermute(most, "mp", [(m, m ^ flip) for m in range(8)]))
+    bound = jnp.maximum(most[0] * most[1] * (rows * 8), 1e-30)
+    down, up = 60000.0 / bound, bound / 60000.0
+    kv_bound = jnp.maximum(most[0] * most[2] * (feats * 2), 1e-30)
+    kv_down, kv_up = 60000.0 / kv_bound, kv_bound / 60000.0
+
+    parts = [place(cot, me ^ ((z - 1 - s) % 4)) for s in range(4)]
+    away = [(dot(tokens, p[:, 2 * wide :], 0, 0) * down).astype(F16) for p in parts]
+    arrived = [over_y(a) for a in away]
+    ring += [over_y(after(block.astype(F32), away[0], away[1]).astype(BF16))]
+
+    panels = jnp.concatenate(ring, axis=1)
+    panel = [place(panels, (z - (me ^ r)) % 4) for r in range(4)]
+    far = over_core(dot(tokens, panel[3], 1, 0))
+    far = ((dot(tokens, panel[2], 1, 0) + far) * kv_down).astype(F16)
+
     travelling = None
-    for s in range(4):
-        part = place(cot, me ^ ((z - 1 - s) % 4))
-        away = dot(tokens, part[:, 2 * wide :], 0, 0)
-        arrived = over_y((away * down).astype(F16))
-        mine = dot(tokens, part[:, : 2 * wide], 0, 0) * down + arrived.astype(F32)
+    for s, part in enumerate(parts):
+        if s == 1:
+            down = after(down, far)
+        mine = dot(tokens, part[:, : 2 * wide], 0, 0) * down + arrived[s].astype(F32)
         if travelling is not None:
             mine = mine + travelling.astype(F32)
         if s < 3:
             travelling = over_z(mine.astype(F16))
     grad_kv = jnp.transpose((mine * up).reshape(feats, 2, wide), (1, 0, 2))
 
-    panels = jnp.concatenate(ring, axis=1)
-    panel = [place(panels, (z - (me ^ r)) % 4) for r in range(4)]
-    far = over_core(dot(tokens, panel[3], 1, 0))
-    far = over_x(((dot(tokens, panel[2], 1, 0) + far) * kv_down).astype(F16)).astype(F32) * kv_up
+    far = over_x(far).astype(F32) * kv_up
     near = over_core(dot(tokens, panel[1], 1, 0))
     kv = dot(tokens, panel[0], 1, 0) + near + far
     kv = jnp.transpose(kv.reshape(rows, 2, 2, wide), (0, 2, 1, 3))

time: 173 us -> 173 us (level)
  waiting for transfers between devices: 68.4 us -> 51.7 us
  local copies, waits for them, and re-layouts: 25.5 us -> 34.2 us
  matrix products: 34.1 us -> 38.5 us
  other arithmetic: 18.8 us -> 15.1 us
  starting transfers between devices: 21.7 us -> 25.3 us
  between operations: 3.39 us -> 6.82 us
    ppermute x6, waiting for transfers between devices: 32.9 us -> 17.8 us  [over_z(): return lax.ppermute(a, 'mp', [(m, (m + 2) % 8) for m in range(8)])]
    dot_general x13, matrix products: 34.1 us -> 38.5 us  [dot(): lax.dot_general(a, b, (((ca,), (cb,)), ((), ())), preferred_element_type=...]
    max x3 -> x2, other arithmetic: 4.07 us -> 0.01 us  [hops(): jnp.maximum(most, lax.ppermute(most, 'mp', [(m, m ^ flip) for m in range(...]
    convert_element_type x2, local copies, waits for them, and re-layouts: 2.35 us -> 6.32 us  [hops(): kv_out = kv.reshape(rows, 2, 2 * wide).astype(BF16)]
    slice x1 -> x6, local copies, waits for them, and re-layouts: 0.66 us -> 4.62 us  [the longest x5 4 us: after(): value = value + 0.0 * a[0, 0].astype(F32)]
    max x2, other arithmetic: 0.01 us -> 3.94 us  [hops(): jnp.maximum(most, lax.ppermute(most, 'dp', [(d, d ^ flip) for d in range(...]
    ppermute x2, waiting for transfers between devices: 4.12 us -> 8.02 us  [hops(): lax.ppermute(most, 'dp', [(d, d ^ flip) for d in range(4)])]
    ppermute x2, waiting for transfers between devices: 3.35 us -> 0.01 us  [over_x(): return lax.ppermute(a, 'dp', [(d, d ^ 2) for d in range(4)])]
  transfers between devices with their start and end apart: 25 -> 25, of which waited for: 11 -> 10; matrix products, arithmetic and copies ran while one was open for 41% -> 43% of each run, Pallas kernels for 0% -> 0%
where the time goes in v3:
time: 173 us; the launch traced here: 172 us
  waiting for transfers between devices  51.7 us (30%)
  matrix products  38.5 us (22%)
  local copies, waits for them, and re-layouts  34.2 us (20%)
  starting transfers between devices  25.3 us (15%)
  other arithmetic  15.1 us (9%)
  between operations  6.82 us (4%)
    dot_general x13, matrix products, dot(): lax.dot_general(a, b, (((ca,), (cb,)), ((), ())), preferred_element_type=...  38.5 us
    ppermute x8, waiting for transfers between devices, over_y(): return lax.ppermute(a, 'mp', [(m, m ^ 1) for m in range(8)])  24.3 us
    ppermute x6, waiting for transfers between devices, over_z(): return lax.ppermute(a, 'mp', [(m, (m + 2) % 8) for m in range(8)])  17.8 us
    unnamed x40, local copies, waits for them, and re-layouts  16.7 us
    ppermute x8, starting transfers between devices, over_y(): return lax.ppermute(a, 'mp', [(m, m ^ 1) for m in range(8)])  8.23 us
    ppermute x2, waiting for transfers between devices, hops(): lax.ppermute(most, 'dp', [(d, d ^ flip) for d in range(4)])  8.02 us
    ppermute x3, starting transfers between devices, hops(): lax.ppermute(most, 'mp', [(m, m ^ flip) for m in range(8)])  6.62 us
    convert_element_type x2, local copies, waits for them, and re-layouts, hops(): kv_out = kv.reshape(rows, 2, 2 * wide).astype(BF16)  6.32 us
  transfers between devices with their start and end apart: 25, of which 10 were waited for; matrix products, arithmetic and copies ran while one was open for 43% of the time, Pallas kernels for 0%

profile of v3, /device:TPU:0, one launch (start us, length us, event | category | flops | bytes accessed | tf_op | source)
XLA Modules:
  0.0 171.7 jit_solution(18203527439574167108)
XLA Ops:
  0.6 2.5 %copy.7 = bf16[1024,2,256]{0,2,1:T(8,128)(2,1)S(1)} copy(bf16[1024,2,256]{2,1,0:T(2,128)(2,1)} %param.5) | data formatting | bytes 2097152 | tf_op args[2]
  5.5 2.5 %collective-permute-start.7 = (bf16[1024,512]{0,1:T(8,128)(2,1)}, bf16[1024,512]{0,1:T(8,128)(2,1)}, u32[]{:S(2)}, u32[]{:S(2)}) collective-permute-start(bf16[1024,512]{0,1:T(8,128)(2,1)} %get-tuple-element.4), channel_id=1, source_target_pairs={{0,16},{8,24},{16,0},{24,8},{1,17},{9,25},{17,1},{25,9},{2,18},{10... | collective-permute-start | bytes 3145736 | tf_op jit(solution)/shard_map/ppermute | solution.py:45
  8.0 2.1 %copy.6 = bf16[1152,2,128]{0,2,1:T(8,128)(2,1)} copy(bf16[1152,2,128]{2,0,1:T(8,128)(2,1)} %bitcast.111) | data formatting | bytes 1179648 | tf_op jit(solution)/shard_map/transpose | solution.py:53
  15.9 2.0 %maximum_convert_fusion = f32[3]{0:T(128)S(1)} fusion(bf16[1]{0:T(256)(128)(2,1)} %bitcast.9, bf16[1]{0:T(256)(128)(2,1)} %bitcast.8, bf16[1]{0:T(256)(128)(2,1)} %bitcast.7), kind=kLoop, calls=%fused_computation.95 | loop fusion | flops 18 | bytes 18 | tf_op jit(solution)/shard_map/stack | solution.py:68
  21.6 2.0 %fusion.75 = f32[3]{0:T(128)S(1)} fusion(f32[3]{0:T(128)S(1)} %collective-permute-done.9, bf16[1]{0:T(256)(128)(2,1)} %bitcast.9, bf16[1]{0:T(256)(128)(2,1)} %bitcast.8, bf16[1]{0:T(256)(128)(2,1)} %bitcast.7), kind=kLoop, calls=%fused_computation.101 | loop fusion | flops 21 | bytes 30 | tf_op jit(solution)/shard_map/max | solution.py:70
  24.1 8.0 %collective-permute-done.10 = f32[3]{0:T(128)S(1)} collective-permute-done((f32[3]{0:T(128)S(1)}, f32[3]{0:T(128)S(1)}, u32[]{:S(2)}, u32[]{:S(2)}) %collective-permute-start.10) | collective-permute-done | bytes 44 | tf_op jit(solution)/shard_map/ppermute | solution.py:70
  32.2 2.0 %fusion.76 = f32[3]{0:T(128)S(1)} fusion(f32[3]{0:T(128)S(1)} %collective-permute-done.10, f32[3]{0:T(128)S(1)} %collective-permute-done.9, bf16[1]{0:T(256)(128)(2,1)} %bitcast.9, bf16[1]{0:T(256)(128)(2,1)} %bitcast.8, bf16[1]{0:T(256)(128)(2,1)} %bitcast.7), kind=kLoop, calls=%fused_computation.102 | loop fusion | flops 24 | bytes 42 | tf_op jit(solution)/shard_map/max | solution.py:70
  39.9 1.9 %constant_dynamic-update-slice_fusion.13 = bf16[1152,2048]{0,1:T(8,128)(2,1)} fusion(bf16[1152,2048]{0,1:T(8,128)(2,1)} %constant_dynamic-update-slice_fusion.14, bf16[1152,256]{0,1:T(8,128)(2,1)} %collective-permute-done), kind=kLoop, calls=%fused_computation.81 | loop fusion | bytes 1179648
  47.3 2.2 %constant_dynamic-update-slice_fusion.2 = bf16[1024,2048]{0,1:T(8,128)(2,1)} fusion(bf16[1024,2048]{0,1:T(8,128)(2,1)} %constant_dynamic-update-slice_fusion.3, bf16[1024,512]{0,1:T(8,128)(2,1)} %collective-permute-done.6), kind=kLoop, calls=%fused_computation.70 | loop fusion | bytes 2097152
  49.5 2.3 %constant_dynamic-update-slice_fusion.1 = bf16[1024,2048]{0,1:T(8,128)(2,1)} fusion(bf16[1024,2048]{0,1:T(8,128)(2,1)} %constant_dynamic-update-slice_fusion.2, bf16[1024,512]{0,1:T(8,128)(2,1)} %collective-permute-done.7), kind=kLoop, calls=%fused_computation.69 | loop fusion | bytes 2097152
  51.9 3.2 %collective-permute-start.13 = (f32[3]{0:T(128)S(1)}, f32[3]{0:T(128)S(1)}, u32[]{:S(2)}, u32[]{:S(2)}) collective-permute-start(f32[3]{0:T(128)S(1)} %max.26), channel_id=1, source_target_pairs={{0,4},{1,5},{2,6},{3,7},{4,0},{5,1},{6,2},{7,3},{8,12},{9,13},{10,... | collective-permute-start | bytes 44 | tf_op jit(solution)/shard_map/ppermute | solution.py:74
  58.6 2.2 %collective-permute-start.5 = (bf16[1152,256]{0,1:T(8,128)(2,1)S(1)}, bf16[1152,256]{0,1:T(8,128)(2,1)S(1)}, u32[]{:S(2)}, u32[]{:S(2)}) collective-permute-start(bf16[1152,256]{0,1:T(8,128)(2,1)S(1)} %collective-permute-done.3), channel_id=1, source_target_pairs={{0,2},{1,3},{2,4},{3,5},{4,6},{5,7},{6,0},{7,1},{8,10},{9,11},{10,... | collective-permute-start | bytes 1769480 | tf_op jit(solution)/shard_map/ppermute | solution.py:39
  63.2 2.5 %fusion.33 = f16[1152,256]{0,1:T(8,128)(2,1)S(1)} fusion(bf16[1024,1152]{1,0:T(8,128)(2,1)S(1)} %copy-done, f32[]{:T(128)} %bitcast.12, bf16[1024,2048]{0,1:T(8,128)(2,1)} %constant_dynamic-update-slice_fusion, s32[]{:T(128)S(6)} %add.156), kind=kOutput, calls=%fused_computation.40 | convolution fusion | flops 604569600 | bytes 3473924 | tf_op jit(solution)/shard_map/dot_general | solution.py:21
  70.1 4.3 %collective-permute-done.5 = bf16[1152,256]{0,1:T(8,128)(2,1)S(1)} collective-permute-done((bf16[1152,256]{0,1:T(8,128)(2,1)S(1)}, bf16[1152,256]{0,1:T(8,128)(2,1)S(1)}, u32[]{:S(2)}, u32[]{:S(2)}) %collective-permute-start.5) | collective-permute-done | bytes 589856 | tf_op jit(solution)/shard_map/ppermute | solution.py:39
  76.3 11.4 %collective-permute-done.14 = bf16[1152,256]{0,1:T(8,128)(2,1)S(1)} collective-permute-done((bf16[1152,256]{0,1:T(8,128)(2,1)S(1)}, bf16[1152,256]{0,1:T(8,128)(2,1)S(1)}, u32[]{:S(2)}, u32[]{:S(2)}) %collective-permute-start.14) | collective-permute-done | bytes 589856 | tf_op jit(solution)/shard_map/ppermute | solution.py:42
  89.7 2.9 %convolution_bitcast_fusion = f32[1024,512]{0,1:T(8,128)} fusion(bf16[1152,512]{0,1:T(8,128)(2,1)S(1)} %get-tuple-element.6, bf16[1024,1152]{1,0:T(8,128)(2,1)S(1)} %copy-done), kind=kOutput, calls=%fused_computation.48 | convolution fusion | flops 1207959552 | bytes 5636096 | tf_op jit(solution)/shard_map/dot_general | solution.py:21
  95.9 2.7 %fusion.31 = f16[1152,256]{0,1:T(8,128)(2,1)} fusion(bf16[1024,1152]{1,0:T(8,128)(2,1)S(1)} %copy-done, f32[]{:T(128)} %bitcast.12, bf16[1024,2048]{0,1:T(8,128)(2,1)} %constant_dynamic-update-slice_fusion, s32[]{:T(128)S(6)} %add.158), kind=kOutput, calls=%fused_computation.38 | convolution fusion | flops 604569600 | bytes 3473924 | tf_op jit(solution)/shard_map/dot_general | solution.py:21
  100.3 2.7 %fusion.30 = f16[1152,256]{0,1:T(8,128)(2,1)} fusion(bf16[1024,1152]{1,0:T(8,128)(2,1)S(1)} %copy-done, f32[]{:T(128)} %bitcast.12, bf16[1024,2048]{0,1:T(8,128)(2,1)} %constant_dynamic-update-slice_fusion, s32[]{:T(128)S(6)} %add.159), kind=kOutput, calls=%fused_computation.37 | convolution fusion | flops 604569600 | bytes 3473924 | tf_op jit(solution)/shard_map/dot_general | solution.py:21
  103.4 6.8 %collective-permute-done.21 = f16[1152,256]{0,1:T(8,128)(2,1)S(1)} collective-permute-done((f16[1152,256]{0,1:T(8,128)(2,1)}, f16[1152,256]{0,1:T(8,128)(2,1)S(1)}, u32[]{:S(2)}, u32[]{:S(2)}) %collective-permute-start.21) | collective-permute-done | bytes 589856 | tf_op jit(solution)/shard_map/ppermute | solution.py:42
  110.2 2.8 %fusion.29 = f16[1152,256]{0,1:T(8,128)(2,1)} fusion(bf16[1024,1152]{1,0:T(8,128)(2,1)S(1)} %copy-done, f16[1152,256]{0,1:T(8,128)(2,1)S(1)} %collective-permute-done.21, f32[]{:T(128)} %bitcast.12, bf16[1024,2048]{0,1:T(8,128)(2,1)} %constant_dynamic-update-slice_fusion, s32[]{:T(128)S(6)} %select_n.94), kind=kOutput, calls=%fused_computation.36 | convolution fusion | flops 605159424 | bytes 4063748 | tf_op jit(solution)/shard_map/dot_general | solution.py:21
  114.5 3.0 %convolution_bitcast_fusion.1 = f32[1024,512]{0,1:T(8,128)} fusion(bf16[1152,512]{0,1:T(8,128)(2,1)S(1)} %copy-done.6, bf16[1024,1152]{1,0:T(8,128)(2,1)S(1)} %copy-done), kind=kOutput, calls=%fused_computation.49 | convolution fusion | flops 1207959552 | bytes 5636096 | tf_op jit(solution)/shard_map/dot_general | solution.py:21
  117.6 2.1 %fusion.36 = f16[1024,512]{0,1:T(8,128)(2,1)S(1)} fusion(f32[1024,512]{0,1:T(8,128)} %collective-permute-done.16, f32[512,1024]{1,0:T(8,128)S(1)} %fusion.57, f32[]{:T(128)} %bitcast.21), kind=kLoop, calls=%fused_computation.45 | loop fusion | flops 1572864 | bytes 5242884 | tf_op jit(solution)/shard_map/convert_element_type | solution.py:88
  124.4 5.2 %collective-permute-done.22 = f16[1152,256]{0,1:T(8,128)(2,1)} collective-permute-done((f16[1152,256]{0,1:T(8,128)(2,1)}, f16[1152,256]{0,1:T(8,128)(2,1)}, u32[]{:S(2)}, u32[]{:S(2)}) %collective-permute-start.22) | collective-permute-done | bytes 589856 | tf_op jit(solution)/shard_map/ppermute | solution.py:39
  129.7 2.3 %fusion.23 = f16[1152,256]{0,1:T(8,128)(2,1)S(1)} fusion(bf16[1024,1152]{1,0:T(8,128)(2,1)S(1)} %copy-done, f16[1152,256]{0,1:T(8,128)(2,1)} %collective-permute-done.22, f16[1152,256]{0,1:T(8,128)(2,1)} %collective-permute-done.20, f32[]{:T(128)S(6)} %add.146, bf16[1024,2048]{0,1:T(8,128)(2,1)} %constant_dynamic-update-slice_fusion, s32[]{:T(128)S(6)} %select_n.96), kind=kOutput, calls=%fused_computation.30 | convolution fusion | flops 605749248 | bytes 4653064 | tf_op jit(solution)/shard_map/dot_general | solution.py:21
  132.1 9.3 %fusion.8 = bf16[1024,1152]{1,0:T(8,128)(2,1)} fusion(bf16[1024,2048]{0,1:T(8,128)(2,1)} %constant_dynamic-update-slice_fusion, bf16[1152,512]{0,1:T(8,128)(2,1)S(1)} %copy-done.5, bf16[1152,512]{0,1:T(8,128)(2,1)S(1)} %copy-done.3, bf16[1152,512]{0,1:T(8,128)(2,1)S(1)} %copy-done.7, bf16[1152,512]{0,1:T(8,128)(2,1)S(1)} %get-tuple-element.8), kind=kOutput, calls=%fused_computation.8 | convolution fusion | flops 4851892224 | bytes 11272192 | tf_op jit(solution)/shard_map/dot_general | solution.py:21
  142.9 4.9 %collective-permute-done.19 = f16[1152,256]{0,1:T(8,128)(2,1)} collective-permute-done((f16[1152,256]{0,1:T(8,128)(2,1)}, f16[1152,256]{0,1:T(8,128)(2,1)}, u32[]{:S(2)}, u32[]{:S(2)}) %collective-permute-start.19) | collective-permute-done | bytes 589856 | tf_op jit(solution)/shard_map/ppermute | solution.py:42
  147.9 3.0 %fusion.24 = f16[1152,256]{0,1:T(8,128)(2,1)} fusion(bf16[1024,1152]{1,0:T(8,128)(2,1)S(1)} %copy-done, f16[1152,256]{0,1:T(8,128)(2,1)S(1)} %collective-permute-done.23, f16[1152,256]{0,1:T(8,128)(2,1)} %collective-permute-done.19, f32[]{:T(128)S(6)} %add.146, bf16[1024,2048]{0,1:T(8,128)(2,1)} %constant_dynamic-update-slice_fusion, s32[]{:T(128)S(6)} %select_n.109), kind=kOutput, calls=%fused_computation.31 | convolution fusion | flops 605749248 | bytes 4653064 | tf_op jit(solution)/shard_map/dot_general | solution.py:21
  150.9 2.2 %fusion.37 = bf16[1024,512]{0,1:T(8,128)(2,1)S(1)} fusion(f32[1024,512]{0,1:T(8,128)} %collective-permute-done.15, f32[512,1024]{1,0:T(8,128)S(1)} %fusion.56, f16[1024,512]{0,1:T(8,128)(2,1)S(1)} %collective-permute-done.17, f32[]{:T(128)} %bitcast.22), kind=kLoop, calls=%fused_computation.47 | loop fusion | flops 2621440 | bytes 6291460 | tf_op jit(solution)/shard_map/add | solution.py:103
  153.3 2.0 %copy.8 = bf16[1024,2,2,128]{3,2,1,0:T(2,128)(2,1)} copy(bf16[1024,2,2,128]{0,3,1,2:T(8,128)(2,1)S(1)} %fusion.34) | data formatting | bytes 2097152 | tf_op jit(solution)/shard_map/convert_element_type | solution.py:106
  155.4 4.3 %convert_element_type.111 = bf16[1024,2,256]{2,1,0:T(2,128)(2,1)} reshape(bf16[1024,2,2,128]{3,2,1,0:T(2,128)(2,1)} %copy.8) | data formatting | bytes 2097152 | tf_op jit(solution)/shard_map/convert_element_type | solution.py:106
  159.7 8.3 %collective-permute-done.24 = f16[1152,256]{0,1:T(8,128)(2,1)} collective-permute-done((f16[1152,256]{0,1:T(8,128)(2,1)}, f16[1152,256]{0,1:T(8,128)(2,1)}, u32[]{:S(2)}, u32[]{:S(2)}) %collective-permute-start.24) | collective-permute-done | bytes 589856 | tf_op jit(solution)/shard_map/ppermute | solution.py:39
  167.9 2.3 %fusion.14 = f32[1152,256]{0,1:T(8,128)S(1)} fusion(bf16[1024,1152]{1,0:T(8,128)(2,1)S(1)} %copy-done, f16[1152,256]{0,1:T(8,128)(2,1)} %collective-permute-done.24, f16[1152,256]{0,1:T(8,128)(2,1)} %collective-permute-done.18, f32[]{:T(128)} %bitcast.33, f32[]{:T(128)S(6)} %add.146, bf16[1024,2048]{0,1:T(8,128)(2,1)} %constant_dynamic-update-slice_fusion, ...), kind=kOutput, calls=%fused_computation.21 | convolution fusion | flops 605749248 | bytes 5243400 | tf_op jit(solution)/shard_map/dot_general | solution.py:21
  (100 shorter events, 46.9 us)
Async XLA Ops:
  3.3 11.7 %copy-start = (bf16[1024,1152]{1,0:T(8,128)(2,1)S(1)}, bf16[1024,1152]{1,0:T(8,128)(2,1)}, u32[]{:S(2)}) copy-start(bf16[1024,1152]{1,0:T(8,128)(2,1)} %param.3) | copy-start | bytes 7077892
  5.1 42.2 %collective-permute-start.6 = (bf16[1024,512]{0,1:T(8,128)(2,1)}, bf16[1024,512]{0,1:T(8,128)(2,1)}, u32[]{:S(2)}, u32[]{:S(2)}) collective-permute-start(bf16[1024,512]{0,1:T(8,128)(2,1)} %get-tuple-element.4), channel_id=1, source_target_pairs={{0,8},{8,0},{16,24},{24,16},{1,9},{9,1},{17,25},{25,17},{2,10},{10... | collective-permute-start | bytes 3145736 | tf_op jit(solution)/shard_map/ppermute | solution.py:48
  5.5 36.3 %collective-permute-start.7 = (bf16[1024,512]{0,1:T(8,128)(2,1)}, bf16[1024,512]{0,1:T(8,128)(2,1)}, u32[]{:S(2)}, u32[]{:S(2)}) collective-permute-start(bf16[1024,512]{0,1:T(8,128)(2,1)} %get-tuple-element.4), channel_id=1, source_target_pairs={{0,16},{8,24},{16,0},{24,8},{1,17},{9,25},{17,1},{25,9},{2,18},{10... | collective-permute-start | bytes 3145736 | tf_op jit(solution)/shard_map/ppermute | solution.py:45
  10.1 25.8 %collective-permute-start.1 = (bf16[1152,256]{0,1:T(8,128)(2,1)}, bf16[1152,256]{0,1:T(8,128)(2,1)}, u32[]{:S(2)}, u32[]{:S(2)}) collective-permute-start(bf16[1152,256]{0,1:T(8,128)(2,1)} %bitcast.112), channel_id=1, source_target_pairs={{0,2},{1,3},{2,4},{3,5},{4,6},{5,7},{6,0},{7,1},{8,10},{9,11},{10,... | collective-permute-start | bytes 1769480 | tf_op jit(solution)/shard_map/ppermute | solution.py:39
  11.7 27.7 %collective-permute-start = (bf16[1152,256]{0,1:T(8,128)(2,1)}, bf16[1152,256]{0,1:T(8,128)(2,1)}, u32[]{:S(2)}, u32[]{:S(2)}) collective-permute-start(bf16[1152,256]{0,1:T(8,128)(2,1)} %bitcast.113), channel_id=1, source_target_pairs={{0,1},{1,0},{2,3},{3,2},{4,5},{5,4},{6,7},{7,6},{8,9},{9,8},{10,11... | collective-permute-start | bytes 1769480 | tf_op jit(solution)/shard_map/ppermute | solution.py:42
  17.8 3.8 %collective-permute-start.9 = (f32[3]{0:T(128)S(1)}, f32[3]{0:T(128)S(1)}, u32[]{:S(2)}, u32[]{:S(2)}) collective-permute-start(f32[3]{0:T(128)S(1)} %maximum_convert_fusion), channel_id=1, source_target_pairs={{0,8},{8,0},{16,24},{24,16},{1,9},{9,1},{17,25},{25,17},{2,10},{10... | collective-permute-start | bytes 44 | tf_op jit(solution)/shard_map/ppermute | solution.py:70
  23.6 8.6 %collective-permute-start.10 = (f32[3]{0:T(128)S(1)}, f32[3]{0:T(128)S(1)}, u32[]{:S(2)}, u32[]{:S(2)}) collective-permute-start(f32[3]{0:T(128)S(1)} %fusion.75), channel_id=1, source_target_pairs={{0,16},{8,24},{16,0},{24,8},{1,17},{9,25},{17,1},{25,9},{2,18},{10... | collective-permute-start | bytes 44 | tf_op jit(solution)/shard_map/ppermute | solution.py:70
  34.1 11.5 %collective-permute-start.11 = (f32[3]{0:T(128)S(1)}, f32[3]{0:T(128)S(1)}, u32[]{:S(2)}, u32[]{:S(2)}) collective-permute-start(f32[3]{0:T(128)S(1)} %fusion.76), channel_id=1, source_target_pairs={{0,1},{1,0},{2,3},{3,2},{4,5},{5,4},{6,7},{7,6},{8,9},{9,8},{10,11... | collective-permute-start | bytes 44 | tf_op jit(solution)/shard_map/ppermute | solution.py:74
  37.8 20.8 %collective-permute-start.3 = (bf16[1152,256]{0,1:T(8,128)(2,1)}, bf16[1152,256]{0,1:T(8,128)(2,1)S(1)}, u32[]{:S(2)}, u32[]{:S(2)}) collective-permute-start(bf16[1152,256]{0,1:T(8,128)(2,1)} %collective-permute-done.1), channel_id=1, source_target_pairs={{0,2},{1,3},{2,4},{3,5},{4,6},{5,7},{6,0},{7,1},{8,10},{9,11},{10,... | collective-permute-start | bytes 1769480 | tf_op jit(solution)/shard_map/ppermute | solution.py:39
  39.4 21.9 %collective-permute-start.2 = (bf16[1152,256]{0,1:T(8,128)(2,1)}, bf16[1152,256]{0,1:T(8,128)(2,1)S(1)}, u32[]{:S(2)}, u32[]{:S(2)}) collective-permute-start(bf16[1152,256]{0,1:T(8,128)(2,1)} %collective-permute-done.1), channel_id=1, source_target_pairs={{0,1},{1,0},{2,3},{3,2},{4,5},{5,4},{6,7},{7,6},{8,9},{9,8},{10,11... | collective-permute-start | bytes 1769480 | tf_op jit(solution)/shard_map/ppermute | solution.py:42
  41.8 20.4 %collective-permute-start.8 = (bf16[1024,512]{0,1:T(8,128)(2,1)}, bf16[1024,512]{0,1:T(8,128)(2,1)S(1)}, u32[]{:S(2)}, u32[]{:S(2)}) collective-permute-start(bf16[1024,512]{0,1:T(8,128)(2,1)} %collective-permute-done.7), channel_id=1, source_target_pairs={{0,8},{8,0},{16,24},{24,16},{1,9},{9,1},{17,25},{25,17},{2,10},{10... | collective-permute-start | bytes 3145736 | tf_op jit(solution)/shard_map/ppermute | solution.py:48
  45.6 6.3 %collective-permute-start.12 = (f32[3]{0:T(128)S(1)}, f32[3]{0:T(128)S(1)}, u32[]{:S(2)}, u32[]{:S(2)}) collective-permute-start(f32[3]{0:T(128)S(1)} %add_add_fusion), channel_id=1, source_target_pairs={{0,2},{1,3},{2,0},{3,1},{4,6},{5,7},{6,4},{7,5},{8,10},{9,11},{10,... | collective-permute-start | bytes 44 | tf_op jit(solution)/shard_map/ppermute | solution.py:74
  51.9 4.7 %collective-permute-start.13 = (f32[3]{0:T(128)S(1)}, f32[3]{0:T(128)S(1)}, u32[]{:S(2)}, u32[]{:S(2)}) collective-permute-start(f32[3]{0:T(128)S(1)} %max.26), channel_id=1, source_target_pairs={{0,4},{1,5},{2,6},{3,7},{4,0},{5,1},{6,2},{7,3},{8,12},{9,13},{10,... | collective-permute-start | bytes 44 | tf_op jit(solution)/shard_map/ppermute | solution.py:74
  58.6 15.8 %collective-permute-start.5 = (bf16[1152,256]{0,1:T(8,128)(2,1)S(1)}, bf16[1152,256]{0,1:T(8,128)(2,1)S(1)}, u32[]{:S(2)}, u32[]{:S(2)}) collective-permute-start(bf16[1152,256]{0,1:T(8,128)(2,1)S(1)} %collective-permute-done.3), channel_id=1, source_target_pairs={{0,2},{1,3},{2,4},{3,5},{4,6},{5,7},{6,0},{7,1},{8,10},{9,11},{10,... | collective-permute-start | bytes 1769480 | tf_op jit(solution)/shard_map/ppermute | solution.py:39
  60.8 15.4 %collective-permute-start.4 = (bf16[1152,256]{0,1:T(8,128)(2,1)S(1)}, bf16[1152,256]{0,1:T(8,128)(2,1)S(1)}, u32[]{:S(2)}, u32[]{:S(2)}) collective-permute-start(bf16[1152,256]{0,1:T(8,128)(2,1)S(1)} %collective-permute-done.3), channel_id=1, source_target_pairs={{0,1},{1,0},{2,3},{3,2},{4,5},{5,4},{6,7},{7,6},{8,9},{9,8},{10,11... | collective-permute-start | bytes 1769480 | tf_op jit(solution)/shard_map/ppermute | solution.py:42
  62.2 13.9 %slice-start = ((s8[4718592]{0:T(1024)(128)(4,1)}), s8[4194304]{0:T(1024)(128)(4,1)S(1)}, s32[]{:S(2)}) async-start(s8[4718592]{0:T(1024)(128)(4,1)} %bitcast.106), calls=%async_computation | async-start | bytes 8388608
  63.2 12.8 %slice-start.1 = ((s8[4718592]{0:T(1024)(128)(4,1)}), s8[524288]{0:T(1024)(128)(4,1)S(1)}, s32[]{:S(2)}) async-start(s8[4718592]{0:T(1024)(128)(4,1)} %bitcast.106), calls=%async_computation.1 | async-start | bytes 1048576
  74.5 13.2 %collective-permute-start.14 = (bf16[1152,256]{0,1:T(8,128)(2,1)S(1)}, bf16[1152,256]{0,1:T(8,128)(2,1)S(1)}, u32[]{:S(2)}, u32[]{:S(2)}) collective-permute-start(bf16[1152,256]{0,1:T(8,128)(2,1)S(1)} %add_convert_fusion), channel_id=1, source_target_pairs={{0,1},{1,0},{2,3},{3,2},{4,5},{5,4},{6,7},{7,6},{8,9},{9,8},{10,11... | collective-permute-start | bytes 1769480 | tf_op jit(solution)/shard_map/ppermute | solution.py:42
  92.5 25.0 %collective-permute-start.16 = (f32[1024,512]{0,1:T(8,128)}, f32[1024,512]{0,1:T(8,128)}, u32[]{:S(2)}, u32[]{:S(2)}) collective-permute-start(f32[1024,512]{0,1:T(8,128)} %convolution_bitcast_fusion), channel_id=1, source_target_pairs={{0,8},{8,0},{16,24},{24,16},{1,9},{9,1},{17,25},{25,17},{2,10},{10... | collective-permute-start | bytes 6291464 | tf_op jit(solution)/shard_map/ppermute | solution.py:48
  93.8 16.4 %collective-permute-start.21 = (f16[1152,256]{0,1:T(8,128)(2,1)}, f16[1152,256]{0,1:T(8,128)(2,1)S(1)}, u32[]{:S(2)}, u32[]{:S(2)}) collective-permute-start(f16[1152,256]{0,1:T(8,128)(2,1)} %copy-done.10), channel_id=1, source_target_pairs={{0,1},{1,0},{2,3},{3,2},{4,5},{5,4},{6,7},{7,6},{8,9},{9,8},{10,11... | collective-permute-start | bytes 1769480 | tf_op jit(solution)/shard_map/ppermute | solution.py:42
  95.6 27.3 %collective-permute-start.20 = (f16[1152,256]{0,1:T(8,128)(2,1)}, f16[1152,256]{0,1:T(8,128)(2,1)}, u32[]{:S(2)}, u32[]{:S(2)}) collective-permute-start(f16[1152,256]{0,1:T(8,128)(2,1)} %copy-done.9), channel_id=1, source_target_pairs={{0,1},{1,0},{2,3},{3,2},{4,5},{5,4},{6,7},{7,6},{8,9},{9,8},{10,11... | collective-permute-start | bytes 1769480 | tf_op jit(solution)/shard_map/ppermute | solution.py:42
  98.6 61.1 %collective-permute-start.18 = (f16[1152,256]{0,1:T(8,128)(2,1)}, f16[1152,256]{0,1:T(8,128)(2,1)}, u32[]{:S(2)}, u32[]{:S(2)}) collective-permute-start(f16[1152,256]{0,1:T(8,128)(2,1)} %fusion.31), channel_id=1, source_target_pairs={{0,1},{1,0},{2,3},{3,2},{4,5},{5,4},{6,7},{7,6},{8,9},{9,8},{10,11... | collective-permute-start | bytes 1769480 | tf_op jit(solution)/shard_map/ppermute | solution.py:42
  103.1 9.9 %copy-start.2 = (bf16[1152,512]{0,1:T(8,128)(2,1)S(1)}, bf16[1152,512]{0,1:T(8,128)(2,1)}, u32[]{:S(2)}) copy-start(bf16[1152,512]{0,1:T(8,128)(2,1)} %get-tuple-element.5) | copy-start | bytes 3538948
  103.1 44.8 %collective-permute-start.19 = (f16[1152,256]{0,1:T(8,128)(2,1)}, f16[1152,256]{0,1:T(8,128)(2,1)}, u32[]{:S(2)}, u32[]{:S(2)}) collective-permute-start(f16[1152,256]{0,1:T(8,128)(2,1)} %fusion.30), channel_id=1, source_target_pairs={{0,1},{1,0},{2,3},{3,2},{4,5},{5,4},{6,7},{7,6},{8,9},{9,8},{10,11... | collective-permute-start | bytes 1769480 | tf_op jit(solution)/shard_map/ppermute | solution.py:42
  113.0 16.7 %collective-permute-start.22 = (f16[1152,256]{0,1:T(8,128)(2,1)}, f16[1152,256]{0,1:T(8,128)(2,1)}, u32[]{:S(2)}, u32[]{:S(2)}) collective-permute-start(f16[1152,256]{0,1:T(8,128)(2,1)} %fusion.29), channel_id=1, source_target_pairs={{0,2},{1,3},{2,4},{3,5},{4,6},{5,7},{6,0},{7,1},{8,10},{9,11},{10,... | collective-permute-start | bytes 1769480 | tf_op jit(solution)/shard_map/ppermute | solution.py:39
  117.6 33.3 %collective-permute-start.15 = (f32[1024,512]{0,1:T(8,128)}, f32[1024,512]{0,1:T(8,128)}, u32[]{:S(2)}, u32[]{:S(2)}) collective-permute-start(f32[1024,512]{0,1:T(8,128)} %convolution_bitcast_fusion.1), channel_id=1, source_target_pairs={{0,8},{8,0},{16,24},{24,16},{1,9},{9,1},{17,25},{25,17},{2,10},{10... | collective-permute-start | bytes 6291464 | tf_op jit(solution)/shard_map/ppermute | solution.py:48
  121.8 10.3 %copy-start.3 = (bf16[1152,512]{0,1:T(8,128)(2,1)S(1)}, bf16[1152,512]{0,1:T(8,128)(2,1)}, u32[]{:S(2)}) copy-start(bf16[1152,512]{0,1:T(8,128)(2,1)} %get-tuple-element.5) | copy-start | bytes 3538948
  121.8 10.3 %copy-start.5 = (bf16[1152,512]{0,1:T(8,128)(2,1)S(1)}, bf16[1152,512]{0,1:T(8,128)(2,1)}, u32[]{:S(2)}) copy-start(bf16[1152,512]{0,1:T(8,128)(2,1)} %copy-done.4) | copy-start | bytes 3538948
  121.8 10.3 %copy-start.7 = (bf16[1152,512]{0,1:T(8,128)(2,1)S(1)}, bf16[1152,512]{0,1:T(8,128)(2,1)}, u32[]{:S(2)}) copy-start(bf16[1152,512]{0,1:T(8,128)(2,1)} %get-tuple-element.7) | copy-start | bytes 3538948
  122.9 27.9 %collective-permute-start.17 = (f16[1024,512]{0,1:T(8,128)(2,1)}, f16[1024,512]{0,1:T(8,128)(2,1)S(1)}, u32[]{:S(2)}, u32[]{:S(2)}) collective-permute-start(f16[1024,512]{0,1:T(8,128)(2,1)} %copy-done.8), channel_id=1, source_target_pairs={{0,16},{8,24},{16,0},{24,8},{1,17},{9,25},{17,1},{25,9},{2,18},{10... | collective-permute-start | bytes 3145736 | tf_op jit(solution)/shard_map/ppermute | solution.py:45
  132.0 15.8 %collective-permute-start.23 = (f16[1152,256]{0,1:T(8,128)(2,1)S(1)}, f16[1152,256]{0,1:T(8,128)(2,1)S(1)}, u32[]{:S(2)}, u32[]{:S(2)}) collective-permute-start(f16[1152,256]{0,1:T(8,128)(2,1)S(1)} %fusion.23), channel_id=1, source_target_pairs={{0,2},{1,3},{2,4},{3,5},{4,6},{5,7},{6,0},{7,1},{8,10},{9,11},{10,... | collective-permute-start | bytes 1769480 | tf_op jit(solution)/shard_map/ppermute | solution.py:39
  150.9 17.1 %collective-permute-start.24 = (f16[1152,256]{0,1:T(8,128)(2,1)}, f16[1152,256]{0,1:T(8,128)(2,1)}, u32[]{:S(2)}, u32[]{:S(2)}) collective-permute-start(f16[1152,256]{0,1:T(8,128)(2,1)} %fusion.24), channel_id=1, source_target_pairs={{0,2},{1,3},{2,4},{3,5},{4,6},{5,7},{6,0},{7,1},{8,10},{9,11},{10,... | collective-permute-start | bytes 1769480 | tf_op jit(solution)/shard_map/ppermute | solution.py:39
  (6 other events, 20.6 us)

commit v4 on v3

--- a/solution.py
+++ b/solution.py
@@ -4,6 +4,7 @@
 from jax.sharding import PartitionSpec as P
 
 F32, BF16, F16 = jnp.float32, jnp.bfloat16, jnp.float16
+SPAN = 60000.0
 
 
 def general(tokens, kv_weight, d_kv):
@@ -65,40 +66,39 @@
     across = over_x(own)
     cot = jnp.concatenate([own, over_core(own), across, over_core(across)], axis=1)
 
-    most = jnp.stack([jnp.max(jnp.abs(a)).astype(F32) for a in (tokens, own, ring[0])])
-    for flip in (1, 2):
-        most = jnp.maximum(most, lax.ppermute(most, "dp", [(d, d ^ flip) for d in range(4)]))
-    for flip in (1, 2, 4):
-        if flip == 2:
-            most = after(most, ring[2], across)
-        most = jnp.maximum(most, lax.ppermute(most, "mp", [(m, m ^ flip) for m in range(8)]))
-    bound = jnp.maximum(most[0] * most[1] * (rows * 8), 1e-30)
-    down, up = 60000.0 / bound, bound / 60000.0
-    kv_bound = jnp.maximum(most[0] * most[2] * (feats * 2), 1e-30)
-    kv_down, kv_up = 60000.0 / kv_bound, kv_bound / 60000.0
-
-    parts = [place(cot, me ^ ((z - 1 - s) % 4)) for s in range(4)]
-    away = [(dot(tokens, p[:, 2 * wide :], 0, 0) * down).astype(F16) for p in parts]
+    most = [jnp.max(jnp.abs(a)).astype(F32) for a in (tokens, cot)]
+    bound = jnp.maximum(most[0] * most[1] * rows, 1e-30)[None]
+    beside = over_y(bound)
+    shifts = (2, 1, 3, 0)
+    parts = [place(cot, me ^ ((z + r) % 4)) for r in shifts]
+    away = [(dot(tokens, p[:, 2 * wide :], 0, 0) * (SPAN / bound)).astype(F16) for p in parts]
     arrived = [over_y(a) for a in away]
-    ring += [over_y(after(block.astype(F32), away[0], away[1]).astype(BF16))]
+    total = bound + beside
+    for flip in (2, 4):
+        total = total + lax.ppermute(total, "mp", [(m, m ^ flip) for m in range(8)])
+    ring += [over_y(after(block.astype(F32), away[0], away[1], total[None]).astype(BF16))]
 
     panels = jnp.concatenate(ring, axis=1)
     panel = [place(panels, (z - (me ^ r)) % 4) for r in range(4)]
-    far = over_core(dot(tokens, panel[3], 1, 0))
-    far = ((dot(tokens, panel[2], 1, 0) + far) * kv_down).astype(F16)
+    far = over_core(after(dot(tokens, panel[3], 1, 0), arrived[0], arrived[1]))
+    far = dot(tokens, panel[2], 1, 0) + far
+    far_most = jnp.maximum(jnp.max(jnp.abs(far)), 1e-30)[None]
+    far = (far * (SPAN / far_most)).astype(F16)
 
-    travelling = None
-    for s, part in enumerate(parts):
-        if s == 1:
-            down = after(down, far)
-        mine = dot(tokens, part[:, : 2 * wide], 0, 0) * down + arrived[s].astype(F32)
-        if travelling is not None:
-            mine = mine + travelling.astype(F32)
-        if s < 3:
-            travelling = over_z(mine.astype(F16))
-    grad_kv = jnp.transpose((mine * up).reshape(feats, 2, wide), (1, 0, 2))
+    far_beside = over_x(far_most)
+    landed = []
+    for r, part, other in zip(shifts, parts, arrived):
+        if r == 0:
+            beside = after(beside, far_beside[None])
+        mine = dot(tokens, part[:, : 2 * wide], 0, 0) + other.astype(F32) * (beside / SPAN)
+        if r:
+            sent = (mine * (SPAN / total)).astype(F16)
+            landed += [lax.ppermute(sent, "mp", [(m, (m + 2 * r) % 8) for m in range(8)])]
+    for share in landed:
+        mine = mine + share.astype(F32) * (total / SPAN)
+    grad_kv = jnp.transpose(mine.reshape(feats, 2, wide), (1, 0, 2))
 
-    far = over_x(far).astype(F32) * kv_up
+    far = over_x(far).astype(F32) * (far_beside / SPAN)
     near = over_core(dot(tokens, panel[1], 1, 0))
     kv = dot(tokens, panel[0], 1, 0) + near + far
     kv = jnp.transpose(kv.reshape(rows, 2, 2, wide), (0, 2, 1, 3))

time: 173 us -> 196 us (1.13)
  starting transfers between devices: 25.3 us -> 37.4 us
  waiting for transfers between devices: 51.7 us -> 61.3 us
  matrix products: 38.5 us -> 42.7 us
  local copies, waits for them, and re-layouts: 34.2 us -> 30.4 us
  between operations: 6.82 us -> 9.92 us
  other arithmetic: 15.1 us -> 13.1 us
    ppermute x2 -> x3, waiting for transfers between devices: 0.01 us -> 19.9 us  [over_x(): return lax.ppermute(a, 'dp', [(d, d ^ 2) for d in range(4)])]
    ppermute x6 -> x3, waiting for transfers between devices: 17.8 us -> 6.31 us  [over_z(): return lax.ppermute(a, 'mp', [(m, (m + 2) % 8) for m in range(8)])]
    ppermute x8 -> x9, waiting for transfers between devices: 24.3 us -> 32.8 us  [over_y(): return lax.ppermute(a, 'mp', [(m, m ^ 1) for m in range(8)])]
    ppermute x5, waiting for transfers between devices: 9.65 us -> 2.29 us  [the longest x2 2.29 us: hops(): total = total + lax.ppermute(total, 'mp', [(m, m ^ flip) for m in range(8)])]
    ppermute x8 -> x9, starting transfers between devices: 8.23 us -> 14.1 us  [over_y(): return lax.ppermute(a, 'mp', [(m, m ^ 1) for m in range(8)])]
    ppermute x5, starting transfers between devices: 7.17 us -> 12.7 us  [the longest x3 7.01 us: hops(): lax.ppermute(sent, 'mp', [(m, (m + 2 * r) % 8) for m in range(8)])]
    dot_general x13, matrix products: 38.5 us -> 42.7 us  [dot(): lax.dot_general(a, b, (((ca,), (cb,)), ((), ())), preferred_element_type=...]
    convert_element_type x2, local copies, waits for them, and re-layouts: 6.32 us -> 2.35 us  [hops(): kv_out = kv.reshape(rows, 2, 2 * wide).astype(BF16)]
  transfers between devices with their start and end apart: 25 -> 24, of which waited for: 10 -> 9; matrix products, arithmetic and copies ran while one was open for 43% -> 37% of each run, Pallas kernels for 0% -> 0%
where the time goes in v4:
time: 196 us; the launch traced here: 195 us
  waiting for transfers between devices  61.3 us (31%)
  matrix products  42.7 us (22%)
  starting transfers between devices  37.4 us (19%)
  local copies, waits for them, and re-layouts  30.4 us (16%)
  other arithmetic  13.1 us (7%)
  between operations  9.92 us (5%)
    dot_general x13, matrix products, dot(): lax.dot_general(a, b, (((ca,), (cb,)), ((), ())), preferred_element_type=...  42.7 us
    ppermute x9, waiting for transfers between devices, over_y(): return lax.ppermute(a, 'mp', [(m, m ^ 1) for m in range(8)])  32.8 us
    unnamed x41, local copies, waits for them, and re-layouts  20.1 us
    ppermute x3, waiting for transfers between devices, over_x(): return lax.ppermute(a, 'dp', [(d, d ^ 2) for d in range(4)])  19.9 us
    ppermute x9, starting transfers between devices, over_y(): return lax.ppermute(a, 'mp', [(m, m ^ 1) for m in range(8)])  14.1 us
    ppermute x3, starting transfers between devices, hops(): lax.ppermute(sent, 'mp', [(m, (m + 2 * r) % 8) for m in range(8)])  7.01 us
    ppermute x3, starting transfers between devices, over_x(): return lax.ppermute(a, 'dp', [(d, d ^ 2) for d in range(4)])  6.76 us
    ppermute x3, waiting for transfers between devices, over_z(): return lax.ppermute(a, 'mp', [(m, (m + 2) % 8) for m in range(8)])  6.31 us
  transfers between devices with their start and end apart: 24, of which 9 were waited for; matrix products, arithmetic and copies ran while one was open for 37% of the time, Pallas kernels for 0%

profile of v4, /device:TPU:0, one launch (start us, length us, event | category | flops | bytes accessed | tf_op | source)
XLA Modules:
  0.0 194.8 jit_solution(3636042539746500794)
XLA Ops:
  3.7 2.5 %collective-permute-start.7 = (bf16[1024,512]{1,0:T(8,128)(2,1)}, bf16[1024,512]{1,0:T(8,128)(2,1)}, u32[]{:S(2)}, u32[]{:S(2)}) collective-permute-start(bf16[1024,512]{1,0:T(8,128)(2,1)} %pad_maximum_fusion), channel_id=1, source_target_pairs={{0,16},{8,24},{16,0},{24,8},{1,17},{9,25},{17,1},{25,9},{2,18},{10... | collective-permute-start | bytes 3145736 | tf_op jit(solution)/shard_map/ppermute | solution.py:46
  6.2 2.1 %copy.13 = bf16[2,1152,128]{1,2,0:T(8,128)(2,1)} copy(bf16[2,1152,128]{2,1,0:T(8,128)(2,1)} %param.4) | data formatting | bytes 1179648 | tf_op args[1]
  16.5 13.9 %collective-permute-done.7 = bf16[1024,512]{1,0:T(8,128)(2,1)} collective-permute-done((bf16[1024,512]{1,0:T(8,128)(2,1)}, bf16[1024,512]{1,0:T(8,128)(2,1)}, u32[]{:S(2)}, u32[]{:S(2)}) %collective-permute-start.7) | collective-permute-done | bytes 1048608 | tf_op jit(solution)/shard_map/ppermute | solution.py:46
  34.5 2.0 %constant_dynamic-update-slice_fusion.13 = bf16[1152,2048]{0,1:T(8,128)(2,1)} fusion(bf16[1152,2048]{0,1:T(8,128)(2,1)} %constant_dynamic-update-slice_fusion.14, bf16[1152,256]{0,1:T(8,128)(2,1)} %collective-permute-done), kind=kLoop, calls=%fused_computation.79 | loop fusion | bytes 1179648
  38.4 2.3 %constant_dynamic-update-slice_fusion.2 = bf16[1024,2048]{1,0:T(8,128)(2,1)} fusion(bf16[1024,2048]{1,0:T(8,128)(2,1)} %constant_dynamic-update-slice_fusion.3, bf16[1024,512]{1,0:T(8,128)(2,1)} %collective-permute-done.6), kind=kLoop, calls=%fused_computation.68 | loop fusion | bytes 2097152
  40.7 2.3 %constant_dynamic-update-slice_fusion.1 = bf16[1024,2048]{1,0:T(8,128)(2,1)} fusion(bf16[1024,2048]{1,0:T(8,128)(2,1)} %constant_dynamic-update-slice_fusion.2, bf16[1024,512]{1,0:T(8,128)(2,1)} %collective-permute-done.7), kind=kLoop, calls=%fused_computation.67 | loop fusion | bytes 2097152
  43.0 6.3 %collective-permute-done.3 = bf16[1152,256]{0,1:T(8,128)(2,1)} collective-permute-done((bf16[1152,256]{0,1:T(8,128)(2,1)}, bf16[1152,256]{0,1:T(8,128)(2,1)}, u32[]{:S(2)}, u32[]{:S(2)}) %collective-permute-start.3) | collective-permute-done | bytes 589856 | tf_op jit(solution)/shard_map/ppermute | solution.py:40
  51.7 2.3 %constant_dynamic-update-slice_fusion = bf16[1024,2048]{1,0:T(8,128)(2,1)} fusion(bf16[1024,2048]{1,0:T(8,128)(2,1)} %constant_dynamic-update-slice_fusion.1, bf16[1024,512]{1,0:T(8,128)(2,1)} %collective-permute-done.8), kind=kLoop, calls=%fused_computation.66 | loop fusion | bytes 2097152 | tf_op jit(solution)/shard_map/concatenate | solution.py:67
  54.0 3.7 %abs_reduce_fusion = bf16[]{:T(256)} fusion(bf16[1024,2048]{1,0:T(8,128)(2,1)} %constant_dynamic-update-slice_fusion), kind=kLoop, calls=%fused_computation.8 | loop fusion | flops 4194303 | bytes 4194306 | tf_op jit(solution)/shard_map/reduce_max | solution.py:69
  59.0 4.7 %collective-permute-start.9 = (f32[1]{0:T(128)}, f32[1]{0:T(128)}, u32[]{:S(2)}, u32[]{:S(2)}) collective-permute-start(f32[1]{0:T(128)} %bitcast.8), channel_id=1, source_target_pairs={{0,1},{1,0},{2,3},{3,2},{4,5},{5,4},{6,7},{7,6},{8,9},{9,8},{10,11... | collective-permute-start | bytes 20 | tf_op jit(solution)/shard_map/ppermute | solution.py:43
  63.7 2.1 %fusion.31 = f16[1152,256]{0,1:T(8,128)(2,1)S(1)} fusion(bf16[1024,1152]{1,0:T(8,128)(2,1)S(1)} %copy-done, f32[]{:T(128)} %bitcast.9, bf16[1024,2048]{1,0:T(8,128)(2,1)} %constant_dynamic-update-slice_fusion, s32[]{:T(128)S(6)} %add.184), kind=kOutput, calls=%fused_computation.39 | convolution fusion | flops 604569600 | bytes 3473924 | tf_op jit(solution)/shard_map/dot_general | solution.py:22
  72.7 2.3 %collective-permute-start.10 = (f32[1]{0:T(128)}, f32[1]{0:T(128)}, u32[]{:S(2)}, u32[]{:S(2)}) collective-permute-start(f32[1]{0:T(128)} %add.150), channel_id=1, source_target_pairs={{0,2},{1,3},{2,0},{3,1},{4,6},{5,7},{6,4},{7,5},{8,10},{9,11},{10,... | collective-permute-start | bytes 20 | tf_op jit(solution)/shard_map/ppermute | solution.py:78
  76.8 3.4 %collective-permute-start.11 = (f32[1]{0:T(128)}, f32[1]{0:T(128)}, u32[]{:S(2)}, u32[]{:S(2)}) collective-permute-start(f32[1]{0:T(128)} %add.151), channel_id=1, source_target_pairs={{0,4},{1,5},{2,6},{3,7},{4,0},{5,1},{6,2},{7,3},{8,12},{9,13},{10,... | collective-permute-start | bytes 20 | tf_op jit(solution)/shard_map/ppermute | solution.py:78
  86.4 8.8 %collective-permute-done.15 = f16[1152,256]{0,1:T(8,128)(2,1)S(1)} collective-permute-done((f16[1152,256]{0,1:T(8,128)(2,1)S(1)}, f16[1152,256]{0,1:T(8,128)(2,1)S(1)}, u32[]{:S(2)}, u32[]{:S(2)}) %collective-permute-start.15) | collective-permute-done | bytes 589856 | tf_op jit(solution)/shard_map/ppermute | solution.py:43
  96.4 9.3 %collective-permute-done.12 = bf16[1152,256]{0,1:T(8,128)(2,1)S(1)} collective-permute-done((bf16[1152,256]{0,1:T(8,128)(2,1)S(1)}, bf16[1152,256]{0,1:T(8,128)(2,1)S(1)}, u32[]{:S(2)}, u32[]{:S(2)}) %collective-permute-start.12) | collective-permute-done | bytes 589856 | tf_op jit(solution)/shard_map/ppermute | solution.py:43
  107.7 2.9 %add_bitcast_fusion = f32[1024,512]{0,1:T(8,128)} fusion(f32[]{:T(128)} %bitcast.19, f32[]{:T(128)} %bitcast.18, bf16[1152,512]{0,1:T(8,128)(2,1)S(1)} %get-tuple-element.4, bf16[1024,1152]{1,0:T(8,128)(2,1)S(1)} %copy-done), kind=kOutput, calls=%fused_computation.47 | convolution fusion | flops 1209008128 | bytes 5636104 | tf_op jit(solution)/shard_map/dot_general | solution.py:22
  110.6 2.7 %fusion.29 = f16[1152,256]{0,1:T(8,128)(2,1)} fusion(bf16[1024,1152]{1,0:T(8,128)(2,1)S(1)} %copy-done, f32[]{:T(128)} %bitcast.9, bf16[1024,2048]{1,0:T(8,128)(2,1)} %constant_dynamic-update-slice_fusion, s32[]{:T(128)S(6)} %add.186), kind=kOutput, calls=%fused_computation.37 | convolution fusion | flops 604569600 | bytes 3473924 | tf_op jit(solution)/shard_map/dot_general | solution.py:22
  118.0 2.8 %fusion.25 = f16[1152,256]{0,1:T(8,128)(2,1)} fusion(bf16[1024,1152]{1,0:T(8,128)(2,1)S(1)} %copy-done, f16[1152,256]{0,1:T(8,128)(2,1)S(1)} %copy-done.8, f32[]{:T(128)} %bitcast.32, f32[]{:T(128)} %bitcast.31, bf16[1024,2048]{1,0:T(8,128)(2,1)} %constant_dynamic-update-slice_fusion, s32[]{:T(128)S(6)} %select_n.94), kind=kOutput, calls=%fused_computation.33 | convolution fusion | flops 605454336 | bytes 4064260 | tf_op jit(solution)/shard_map/dot_general | solution.py:22
  122.3 2.8 %fusion.26 = f16[1152,256]{0,1:T(8,128)(2,1)} fusion(bf16[1024,1152]{1,0:T(8,128)(2,1)S(1)} %copy-done, f16[1152,256]{0,1:T(8,128)(2,1)S(1)} %copy-done.10, f32[]{:T(128)} %bitcast.32, f32[]{:T(128)} %bitcast.31, bf16[1024,2048]{1,0:T(8,128)(2,1)} %constant_dynamic-update-slice_fusion, s32[]{:T(128)S(6)} %select_n.96), kind=kOutput, calls=%fused_computation.34 | convolution fusion | flops 605454336 | bytes 4064260 | tf_op jit(solution)/shard_map/dot_general | solution.py:22
  125.1 2.2 %collective-permute-start.21 = (f16[1152,256]{0,1:T(8,128)(2,1)}, f16[1152,256]{0,1:T(8,128)(2,1)}, u32[]{:S(2)}, u32[]{:S(2)}) collective-permute-start(f16[1152,256]{0,1:T(8,128)(2,1)} %fusion.26), channel_id=1, source_target_pairs={{0,2},{1,3},{2,4},{3,5},{4,6},{5,7},{6,0},{7,1},{8,10},{9,11},{10,... | collective-permute-start | bytes 1769480 | tf_op jit(solution)/shard_map/ppermute | solution.py:96
  127.3 14.6 %collective-permute-done.22 = f16[1152,256]{0,1:T(8,128)(2,1)S(1)} collective-permute-done((f16[1152,256]{0,1:T(8,128)(2,1)S(1)}, f16[1152,256]{0,1:T(8,128)(2,1)S(1)}, u32[]{:S(2)}, u32[]{:S(2)}) %collective-permute-start.22) | collective-permute-done | bytes 589856 | tf_op jit(solution)/shard_map/ppermute | solution.py:43
  141.9 2.7 %fusion.27 = f16[1152,256]{0,1:T(8,128)(2,1)} fusion(bf16[1024,1152]{1,0:T(8,128)(2,1)S(1)} %copy-done, f16[1152,256]{0,1:T(8,128)(2,1)S(1)} %collective-permute-done.22, f32[]{:T(128)} %bitcast.32, f32[]{:T(128)} %bitcast.31, bf16[1024,2048]{1,0:T(8,128)(2,1)} %constant_dynamic-update-slice_fusion, s32[]{:T(128)S(6)} %select_n.109), kind=kOutput, calls=%fused_computation.35 | convolution fusion | flops 605454336 | bytes 4064260 | tf_op jit(solution)/shard_map/dot_general | solution.py:22
  144.7 3.2 %collective-permute-start.23 = (f16[1152,256]{0,1:T(8,128)(2,1)}, f16[1152,256]{0,1:T(8,128)(2,1)}, u32[]{:S(2)}, u32[]{:S(2)}) collective-permute-start(f16[1152,256]{0,1:T(8,128)(2,1)} %fusion.27), channel_id=1, source_target_pairs={{0,6},{1,7},{2,0},{3,1},{4,2},{5,3},{6,4},{7,5},{8,14},{9,15},{10,... | collective-permute-start | bytes 1769480 | tf_op jit(solution)/shard_map/ppermute | solution.py:96
  147.9 2.9 %convolution_bitcast_fusion.4 = f32[1024,512]{0,1:T(8,128)} fusion(bf16[1152,512]{0,1:T(8,128)(2,1)S(1)} %copy-done.5, bf16[1024,1152]{1,0:T(8,128)(2,1)S(1)} %copy-done), kind=kOutput, calls=%fused_computation.48 | convolution fusion | flops 1207959552 | bytes 5636096 | tf_op jit(solution)/shard_map/dot_general | solution.py:22
  150.8 5.1 %abs_reduce_fusion.2 = (f32[]{:T(128)}, f32[512,1024]{1,0:T(8,128)}) fusion(f32[1024,512]{0,1:T(8,128)} %collective-permute-done.16, bf16[1152,512]{0,1:T(8,128)(2,1)S(1)} %copy-done.2, bf16[1024,1152]{1,0:T(8,128)(2,1)S(1)} %copy-done), kind=kOutput, calls=%fused_computation.46 | convolution fusion | flops 1209532416 | bytes 7733252 | tf_op jit(solution)/shard_map/dot_general | solution.py:22
  156.6 3.9 %multiply_convert_fusion = f16[1024,512]{0,1:T(8,128)(2,1)} fusion(f32[]{:T(128)} %bitcast.22, f32[1024,512]{0,1:T(8,128)} %collective-permute-done.16, f32[512,1024]{1,0:T(8,128)} %get-tuple-element.14), kind=kLoop, calls=%fused_computation.45 | loop fusion | flops 1572864 | bytes 5242884 | tf_op jit(solution)/shard_map/convert_element_type | solution.py:86
  160.5 2.8 %collective-permute-start.18 = (f32[1]{0:T(128)}, f32[1]{0:T(128)}, u32[]{:S(2)}, u32[]{:S(2)}) collective-permute-start(f32[1]{0:T(128)} %bitcast.21), channel_id=1, source_target_pairs={{0,16},{8,24},{16,0},{24,8},{1,17},{9,25},{17,1},{25,9},{2,18},{10... | collective-permute-start | bytes 20 | tf_op jit(solution)/shard_map/ppermute | solution.py:46
  165.5 9.2 %fusion.8 = bf16[1024,1152]{1,0:T(8,128)(2,1)} fusion(bf16[1024,2048]{1,0:T(8,128)(2,1)} %constant_dynamic-update-slice_fusion, bf16[1152,512]{0,1:T(8,128)(2,1)S(1)} %copy-done.4, bf16[1152,512]{0,1:T(8,128)(2,1)S(1)} %copy-done.2, bf16[1152,512]{0,1:T(8,128)(2,1)S(1)} %copy-done.6, bf16[1152,512]{0,1:T(8,128)(2,1)S(1)} %copy-done.1), kind=kOutput, calls=%fused_computation.9 | convolution fusion | flops 4851892224 | bytes 11272192 | tf_op jit(solution)/shard_map/dot_general | solution.py:22
  174.6 2.9 %fusion.51 = f32[512,1024]{1,0:T(8,128)} fusion(bf16[1152,512]{0,1:T(8,128)(2,1)S(1)} %copy-done.1, bf16[1024,1152]{1,0:T(8,128)(2,1)S(1)} %copy-done), kind=kOutput, calls=%fused_computation.94 | convolution fusion | flops 1207959552 | bytes 5636096 | tf_op jit(solution)/shard_map/dot_general | solution.py:22
  178.8 2.9 %fusion.20 = f32[1152,256]{0,1:T(8,128)S(1)} fusion(bf16[1024,1152]{1,0:T(8,128)(2,1)S(1)} %copy-done, f16[1152,256]{0,1:T(8,128)(2,1)} %collective-permute-done.23, f16[1152,256]{0,1:T(8,128)(2,1)} %collective-permute-done.21, f16[1152,256]{0,1:T(8,128)(2,1)} %collective-permute-done.20, f16[1152,256]{0,1:T(8,128)(2,1)} %collective-permute-done.19, ...), kind=kOutput, calls=%fused_computation.28 | convolution fusion | flops 607518720 | bytes 6423556 | tf_op jit(solution)/shard_map/dot_general | solution.py:22
  183.8 5.3 %collective-permute-done.17 = f16[1024,512]{0,1:T(8,128)(2,1)} collective-permute-done((f16[1024,512]{0,1:T(8,128)(2,1)}, f16[1024,512]{0,1:T(8,128)(2,1)}, u32[]{:S(2)}, u32[]{:S(2)}) %collective-permute-start.17) | collective-permute-done | bytes 1048608 | tf_op jit(solution)/shard_map/ppermute | solution.py:46
  189.1 3.1 %fusion.33 = bf16[1024,512]{0,1:T(8,128)(2,1)S(1)} fusion(f32[1024,512]{0,1:T(8,128)} %collective-permute-done.13, f32[512,1024]{1,0:T(8,128)} %fusion.51, f16[1024,512]{0,1:T(8,128)(2,1)} %collective-permute-done.17, f32[]{:T(128)} %bitcast.23), kind=kLoop, calls=%fused_computation.44 | loop fusion | flops 2621440 | bytes 6291460 | tf_op jit(solution)/shard_map/add | solution.py:103
  (90 shorter events, 45.0 us)
Async XLA Ops:
  3.3 12.3 %copy-start = (bf16[1024,1152]{1,0:T(8,128)(2,1)S(1)}, bf16[1024,1152]{1,0:T(8,128)(2,1)}, u32[]{:S(2)}) copy-start(bf16[1024,1152]{1,0:T(8,128)(2,1)} %param.3) | copy-start | bytes 7077892
  3.3 35.1 %collective-permute-start.6 = (bf16[1024,512]{1,0:T(8,128)(2,1)}, bf16[1024,512]{1,0:T(8,128)(2,1)}, u32[]{:S(2)}, u32[]{:S(2)}) collective-permute-start(bf16[1024,512]{1,0:T(8,128)(2,1)} %pad_maximum_fusion), channel_id=1, source_target_pairs={{0,8},{8,0},{16,24},{24,16},{1,9},{9,1},{17,25},{25,17},{2,10},{10... | collective-permute-start | bytes 3145736 | tf_op jit(solution)/shard_map/ppermute | solution.py:49
  3.7 26.6 %collective-permute-start.7 = (bf16[1024,512]{1,0:T(8,128)(2,1)}, bf16[1024,512]{1,0:T(8,128)(2,1)}, u32[]{:S(2)}, u32[]{:S(2)}) collective-permute-start(bf16[1024,512]{1,0:T(8,128)(2,1)} %pad_maximum_fusion), channel_id=1, source_target_pairs={{0,16},{8,24},{16,0},{24,8},{1,17},{9,25},{17,1},{25,9},{2,18},{10... | collective-permute-start | bytes 3145736 | tf_op jit(solution)/shard_map/ppermute | solution.py:46
  8.3 22.8 %collective-permute-start.1 = (bf16[1152,256]{0,1:T(8,128)(2,1)}, bf16[1152,256]{0,1:T(8,128)(2,1)}, u32[]{:S(2)}, u32[]{:S(2)}) collective-permute-start(bf16[1152,256]{0,1:T(8,128)(2,1)} %bitcast.119), channel_id=1, source_target_pairs={{0,2},{1,3},{2,4},{3,5},{4,6},{5,7},{6,0},{7,1},{8,10},{9,11},{10,... | collective-permute-start | bytes 1769480 | tf_op jit(solution)/shard_map/ppermute | solution.py:40
  9.9 24.6 %collective-permute-start = (bf16[1152,256]{0,1:T(8,128)(2,1)}, bf16[1152,256]{0,1:T(8,128)(2,1)}, u32[]{:S(2)}, u32[]{:S(2)}) collective-permute-start(bf16[1152,256]{0,1:T(8,128)(2,1)} %bitcast.120), channel_id=1, source_target_pairs={{0,1},{1,0},{2,3},{3,2},{4,5},{5,4},{6,7},{7,6},{8,9},{9,8},{10,11... | collective-permute-start | bytes 1769480 | tf_op jit(solution)/shard_map/ppermute | solution.py:43
  30.3 21.3 %collective-permute-start.8 = (bf16[1024,512]{1,0:T(8,128)(2,1)}, bf16[1024,512]{1,0:T(8,128)(2,1)}, u32[]{:S(2)}, u32[]{:S(2)}) collective-permute-start(bf16[1024,512]{1,0:T(8,128)(2,1)} %collective-permute-done.7), channel_id=1, source_target_pairs={{0,8},{8,0},{16,24},{24,16},{1,9},{9,1},{17,25},{25,17},{2,10},{10... | collective-permute-start | bytes 3145736 | tf_op jit(solution)/shard_map/ppermute | solution.py:49
  31.1 18.2 %collective-permute-start.3 = (bf16[1152,256]{0,1:T(8,128)(2,1)}, bf16[1152,256]{0,1:T(8,128)(2,1)}, u32[]{:S(2)}, u32[]{:S(2)}) collective-permute-start(bf16[1152,256]{0,1:T(8,128)(2,1)} %collective-permute-done.1), channel_id=1, source_target_pairs={{0,2},{1,3},{2,4},{3,5},{4,6},{5,7},{6,0},{7,1},{8,10},{9,11},{10,... | collective-permute-start | bytes 1769480 | tf_op jit(solution)/shard_map/ppermute | solution.py:40
  32.9 17.9 %collective-permute-start.2 = (bf16[1152,256]{0,1:T(8,128)(2,1)}, bf16[1152,256]{0,1:T(8,128)(2,1)S(1)}, u32[]{:S(2)}, u32[]{:S(2)}) collective-permute-start(bf16[1152,256]{0,1:T(8,128)(2,1)} %collective-permute-done.1), channel_id=1, source_target_pairs={{0,1},{1,0},{2,3},{3,2},{4,5},{5,4},{6,7},{7,6},{8,9},{9,8},{10,11... | collective-permute-start | bytes 1769480 | tf_op jit(solution)/shard_map/ppermute | solution.py:43
  49.3 32.6 %collective-permute-start.5 = (bf16[1152,256]{0,1:T(8,128)(2,1)}, bf16[1152,256]{0,1:T(8,128)(2,1)S(1)}, u32[]{:S(2)}, u32[]{:S(2)}) collective-permute-start(bf16[1152,256]{0,1:T(8,128)(2,1)} %collective-permute-done.3), channel_id=1, source_target_pairs={{0,2},{1,3},{2,4},{3,5},{4,6},{5,7},{6,0},{7,1},{8,10},{9,11},{10,... | collective-permute-start | bytes 1769480 | tf_op jit(solution)/shard_map/ppermute | solution.py:40
  49.3 34.7 %collective-permute-start.4 = (bf16[1152,256]{0,1:T(8,128)(2,1)}, bf16[1152,256]{0,1:T(8,128)(2,1)}, u32[]{:S(2)}, u32[]{:S(2)}) collective-permute-start(bf16[1152,256]{0,1:T(8,128)(2,1)} %collective-permute-done.3), channel_id=1, source_target_pairs={{0,1},{1,0},{2,3},{3,2},{4,5},{5,4},{6,7},{7,6},{8,9},{9,8},{10,11... | collective-permute-start | bytes 1769480 | tf_op jit(solution)/shard_map/ppermute | solution.py:43
  54.0 28.8 %slice-start = ((s8[4718592]{0:T(1024)(128)(4,1)}), s8[524288]{0:T(1024)(128)(4,1)S(1)}, s32[]{:S(2)}) async-start(s8[4718592]{0:T(1024)(128)(4,1)} %bitcast.114), calls=%async_computation | async-start | bytes 1048576
  59.0 13.1 %collective-permute-start.9 = (f32[1]{0:T(128)}, f32[1]{0:T(128)}, u32[]{:S(2)}, u32[]{:S(2)}) collective-permute-start(f32[1]{0:T(128)} %bitcast.8), channel_id=1, source_target_pairs={{0,1},{1,0},{2,3},{3,2},{4,5},{5,4},{6,7},{7,6},{8,9},{9,8},{10,11... | collective-permute-start | bytes 20 | tf_op jit(solution)/shard_map/ppermute | solution.py:43
  63.7 19.1 %slice-start.1 = ((s8[4718592]{0:T(1024)(128)(4,1)}), s8[4194304]{0:T(1024)(128)(4,1)S(1)}, s32[]{:S(2)}) async-start(s8[4718592]{0:T(1024)(128)(4,1)} %bitcast.114), calls=%async_computation.1 | async-start | bytes 8388608
  66.3 18.8 %collective-permute-start.14 = (f16[1152,256]{0,1:T(8,128)(2,1)S(1)}, f16[1152,256]{0,1:T(8,128)(2,1)S(1)}, u32[]{:S(2)}, u32[]{:S(2)}) collective-permute-start(f16[1152,256]{0,1:T(8,128)(2,1)S(1)} %fusion.31), channel_id=1, source_target_pairs={{0,1},{1,0},{2,3},{3,2},{4,5},{5,4},{6,7},{7,6},{8,9},{9,8},{10,11... | collective-permute-start | bytes 1769480 | tf_op jit(solution)/shard_map/ppermute | solution.py:43
  69.4 25.8 %collective-permute-start.15 = (f16[1152,256]{0,1:T(8,128)(2,1)S(1)}, f16[1152,256]{0,1:T(8,128)(2,1)S(1)}, u32[]{:S(2)}, u32[]{:S(2)}) collective-permute-start(f16[1152,256]{0,1:T(8,128)(2,1)S(1)} %fusion.30), channel_id=1, source_target_pairs={{0,1},{1,0},{2,3},{3,2},{4,5},{5,4},{6,7},{7,6},{8,9},{9,8},{10,11... | collective-permute-start | bytes 1769480 | tf_op jit(solution)/shard_map/ppermute | solution.py:43
  72.7 3.6 %collective-permute-start.10 = (f32[1]{0:T(128)}, f32[1]{0:T(128)}, u32[]{:S(2)}, u32[]{:S(2)}) collective-permute-start(f32[1]{0:T(128)} %add.150), channel_id=1, source_target_pairs={{0,2},{1,3},{2,0},{3,1},{4,6},{5,7},{6,4},{7,5},{8,10},{9,11},{10,... | collective-permute-start | bytes 20 | tf_op jit(solution)/shard_map/ppermute | solution.py:78
  76.8 4.5 %collective-permute-start.11 = (f32[1]{0:T(128)}, f32[1]{0:T(128)}, u32[]{:S(2)}, u32[]{:S(2)}) collective-permute-start(f32[1]{0:T(128)} %add.151), channel_id=1, source_target_pairs={{0,4},{1,5},{2,6},{3,7},{4,0},{5,1},{6,2},{7,3},{8,12},{9,13},{10,... | collective-permute-start | bytes 20 | tf_op jit(solution)/shard_map/ppermute | solution.py:78
  82.1 23.6 %collective-permute-start.12 = (bf16[1152,256]{0,1:T(8,128)(2,1)S(1)}, bf16[1152,256]{0,1:T(8,128)(2,1)S(1)}, u32[]{:S(2)}, u32[]{:S(2)}) collective-permute-start(bf16[1152,256]{0,1:T(8,128)(2,1)S(1)} %add_convert_fusion), channel_id=1, source_target_pairs={{0,1},{1,0},{2,3},{3,2},{4,5},{5,4},{6,7},{7,6},{8,9},{9,8},{10,11... | collective-permute-start | bytes 1769480 | tf_op jit(solution)/shard_map/ppermute | solution.py:43
  85.2 20.6 %copy-start.7 = (f16[1152,256]{0,1:T(8,128)(2,1)}, f16[1152,256]{0,1:T(8,128)(2,1)S(1)}, u32[]{:S(2)}) copy-start(f16[1152,256]{0,1:T(8,128)(2,1)S(1)} %collective-permute-done.14) | copy-start | bytes 1769476
  95.2 10.5 %copy-start.9 = (f16[1152,256]{0,1:T(8,128)(2,1)}, f16[1152,256]{0,1:T(8,128)(2,1)S(1)}, u32[]{:S(2)}) copy-start(f16[1152,256]{0,1:T(8,128)(2,1)S(1)} %collective-permute-done.15) | copy-start | bytes 1769476
  110.6 40.2 %collective-permute-start.16 = (f32[1024,512]{0,1:T(8,128)}, f32[1024,512]{0,1:T(8,128)}, u32[]{:S(2)}, u32[]{:S(2)}) collective-permute-start(f32[1024,512]{0,1:T(8,128)} %add_bitcast_fusion), channel_id=1, source_target_pairs={{0,8},{8,0},{16,24},{24,16},{1,9},{9,1},{17,25},{25,17},{2,10},{10... | collective-permute-start | bytes 6291464 | tf_op jit(solution)/shard_map/ppermute | solution.py:49
  113.3 47.1 %collective-permute-start.19 = (f16[1152,256]{0,1:T(8,128)(2,1)}, f16[1152,256]{0,1:T(8,128)(2,1)}, u32[]{:S(2)}, u32[]{:S(2)}) collective-permute-start(f16[1152,256]{0,1:T(8,128)(2,1)} %fusion.29), channel_id=1, source_target_pairs={{0,1},{1,0},{2,3},{3,2},{4,5},{5,4},{6,7},{7,6},{8,9},{9,8},{10,11... | collective-permute-start | bytes 1769480 | tf_op jit(solution)/shard_map/ppermute | solution.py:43
  116.0 25.9 %collective-permute-start.22 = (f16[1152,256]{0,1:T(8,128)(2,1)S(1)}, f16[1152,256]{0,1:T(8,128)(2,1)S(1)}, u32[]{:S(2)}, u32[]{:S(2)}) collective-permute-start(f16[1152,256]{0,1:T(8,128)(2,1)S(1)} %fusion.28), channel_id=1, source_target_pairs={{0,1},{1,0},{2,3},{3,2},{4,5},{5,4},{6,7},{7,6},{8,9},{9,8},{10,11... | collective-permute-start | bytes 1769480 | tf_op jit(solution)/shard_map/ppermute | solution.py:43
  120.7 58.0 %collective-permute-start.20 = (f16[1152,256]{0,1:T(8,128)(2,1)}, f16[1152,256]{0,1:T(8,128)(2,1)}, u32[]{:S(2)}, u32[]{:S(2)}) collective-permute-start(f16[1152,256]{0,1:T(8,128)(2,1)} %fusion.25), channel_id=1, source_target_pairs={{0,4},{1,5},{2,6},{3,7},{4,0},{5,1},{6,2},{7,3},{8,12},{9,13},{10,... | collective-permute-start | bytes 1769480 | tf_op jit(solution)/shard_map/ppermute | solution.py:96
  125.1 22.8 %copy-start.5 = (bf16[1152,512]{0,1:T(8,128)(2,1)S(1)}, bf16[1152,512]{0,1:T(8,128)(2,1)}, u32[]{:S(2)}) copy-start(bf16[1152,512]{0,1:T(8,128)(2,1)} %get-tuple-element.5) | copy-start | bytes 3538948
  125.1 53.7 %collective-permute-start.21 = (f16[1152,256]{0,1:T(8,128)(2,1)}, f16[1152,256]{0,1:T(8,128)(2,1)}, u32[]{:S(2)}, u32[]{:S(2)}) collective-permute-start(f16[1152,256]{0,1:T(8,128)(2,1)} %fusion.26), channel_id=1, source_target_pairs={{0,2},{1,3},{2,4},{3,5},{4,6},{5,7},{6,0},{7,1},{8,10},{9,11},{10,... | collective-permute-start | bytes 1769480 | tf_op jit(solution)/shard_map/ppermute | solution.py:96
  144.7 34.1 %collective-permute-start.23 = (f16[1152,256]{0,1:T(8,128)(2,1)}, f16[1152,256]{0,1:T(8,128)(2,1)}, u32[]{:S(2)}, u32[]{:S(2)}) collective-permute-start(f16[1152,256]{0,1:T(8,128)(2,1)} %fusion.27), channel_id=1, source_target_pairs={{0,6},{1,7},{2,0},{3,1},{4,2},{5,3},{6,4},{7,5},{8,14},{9,15},{10,... | collective-permute-start | bytes 1769480 | tf_op jit(solution)/shard_map/ppermute | solution.py:96
  150.8 33.0 %collective-permute-start.13 = (f32[1024,512]{0,1:T(8,128)}, f32[1024,512]{0,1:T(8,128)}, u32[]{:S(2)}, u32[]{:S(2)}) collective-permute-start(f32[1024,512]{0,1:T(8,128)} %convolution_bitcast_fusion.4), channel_id=1, source_target_pairs={{0,8},{8,0},{16,24},{24,16},{1,9},{9,1},{17,25},{25,17},{2,10},{10... | collective-permute-start | bytes 6291464 | tf_op jit(solution)/shard_map/ppermute | solution.py:49
  156.6 8.9 %copy-start.1 = (bf16[1152,512]{0,1:T(8,128)(2,1)S(1)}, bf16[1152,512]{0,1:T(8,128)(2,1)}, u32[]{:S(2)}) copy-start(bf16[1152,512]{0,1:T(8,128)(2,1)} %get-tuple-element.6) | copy-start | bytes 3538948
  156.6 8.9 %copy-start.4 = (bf16[1152,512]{0,1:T(8,128)(2,1)S(1)}, bf16[1152,512]{0,1:T(8,128)(2,1)}, u32[]{:S(2)}) copy-start(bf16[1152,512]{0,1:T(8,128)(2,1)} %copy-done.3) | copy-start | bytes 3538948
  160.5 3.5 %collective-permute-start.18 = (f32[1]{0:T(128)}, f32[1]{0:T(128)}, u32[]{:S(2)}, u32[]{:S(2)}) collective-permute-start(f32[1]{0:T(128)} %bitcast.21), channel_id=1, source_target_pairs={{0,16},{8,24},{16,0},{24,8},{1,17},{9,25},{17,1},{25,9},{2,18},{10... | collective-permute-start | bytes 20 | tf_op jit(solution)/shard_map/ppermute | solution.py:46
  164.0 25.2 %collective-permute-start.17 = (f16[1024,512]{0,1:T(8,128)(2,1)}, f16[1024,512]{0,1:T(8,128)(2,1)}, u32[]{:S(2)}, u32[]{:S(2)}) collective-permute-start(f16[1024,512]{0,1:T(8,128)(2,1)} %multiply_convert_fusion), channel_id=1, source_target_pairs={{0,16},{8,24},{16,0},{24,8},{1,17},{9,25},{17,1},{25,9},{2,18},{10... | collective-permute-start | bytes 3145736 | tf_op jit(solution)/shard_map/ppermute | solution.py:46
  (5 other events, 25.5 us)

commit v5 on v4

--- a/solution.py
+++ b/solution.py
@@ -76,20 +76,22 @@
     total = bound + beside
     for flip in (2, 4):
         total = total + lax.ppermute(total, "mp", [(m, m ^ flip) for m in range(8)])
-    ring += [over_y(after(block.astype(F32), away[0], away[1], total[None]).astype(BF16))]
+    ring += [over_y(block)]
 
     panels = jnp.concatenate(ring, axis=1)
     panel = [place(panels, (z - (me ^ r)) % 4) for r in range(4)]
-    far = over_core(after(dot(tokens, panel[3], 1, 0), arrived[0], arrived[1]))
+    far = over_core(dot(tokens, panel[3], 1, 0))
     far = dot(tokens, panel[2], 1, 0) + far
-    far_most = jnp.maximum(jnp.max(jnp.abs(far)), 1e-30)[None]
+    share_most = jnp.max(jnp.abs(panels)).astype(F32) * most[0] * feats
+    share_most = jnp.maximum(share_most, 1e-30)[None]
+    far_most = share_most + over_core(share_most)
     far = (far * (SPAN / far_most)).astype(F16)
 
     far_beside = over_x(far_most)
     landed = []
     for r, part, other in zip(shifts, parts, arrived):
-        if r == 0:
-            beside = after(beside, far_beside[None])
+        if r == 1:
+            beside = after(beside, far, far_beside[None])
         mine = dot(tokens, part[:, : 2 * wide], 0, 0) + other.astype(F32) * (beside / SPAN)
         if r:
             sent = (mine * (SPAN / total)).astype(F16)

time: 196 us -> 183 us (0.934)
  waiting for transfers between devices: 61.3 us -> 54.4 us
  starting transfers between devices: 37.4 us -> 31.8 us
  matrix products: 42.7 us -> 40.1 us
  other arithmetic: 13.1 us -> 15.1 us
    ppermute x9, waiting for transfers between devices: 32.8 us -> 0.02 us  [over_y(): return lax.ppermute(a, 'mp', [(m, m ^ 1) for m in range(8)])]
    ppermute x3, waiting for transfers between devices: 0.01 us -> 23.2 us  [hops(): lax.ppermute(sent, 'mp', [(m, (m + 2 * r) % 8) for m in range(8)])]
    ppermute x3, waiting for transfers between devices: 6.31 us -> 18 us  [over_z(): return lax.ppermute(a, 'mp', [(m, (m + 2) % 8) for m in range(8)])]
    ppermute x3, waiting for transfers between devices: 19.9 us -> 10.5 us  [over_x(): return lax.ppermute(a, 'dp', [(d, d ^ 2) for d in range(4)])]
    reduce_max x0 -> x1, other arithmetic: none -> 3.61 us  [hops(): share_most = jnp.max(jnp.abs(panels)).astype(F32) * most[0] * feats]
    ppermute x3, starting transfers between devices: 7.01 us -> 3.67 us  [hops(): lax.ppermute(sent, 'mp', [(m, (m + 2 * r) % 8) for m in range(8)])]
    dot_general x13, matrix products: 42.7 us -> 40.1 us  [dot(): lax.dot_general(a, b, (((ca,), (cb,)), ((), ())), preferred_element_type=...]
    unnamed x41 -> x31, local copies, waits for them, and re-layouts: 20.1 us -> 18.3 us
  transfers between devices with their start and end apart: 24 -> 25, of which waited for: 9 -> 9; matrix products, arithmetic and copies ran while one was open for 37% -> 43% of each run, Pallas kernels for 0% -> 0%
where the time goes in v5:
time: 183 us; the launch traced here: 180 us
  waiting for transfers between devices  54.4 us (30%)
  matrix products  40.1 us (22%)
  starting transfers between devices  31.8 us (17%)
  local copies, waits for them, and re-layouts  29 us (16%)
  other arithmetic  15.1 us (8%)
  between operations  9.72 us (5%)
    dot_general x13, matrix products, dot(): lax.dot_general(a, b, (((ca,), (cb,)), ((), ())), preferred_element_type=...  40.1 us
    ppermute x3, waiting for transfers between devices, hops(): lax.ppermute(sent, 'mp', [(m, (m + 2 * r) % 8) for m in range(8)])  23.2 us
    unnamed x31, local copies, waits for them, and re-layouts  18.3 us
    ppermute x3, waiting for transfers between devices, over_z(): return lax.ppermute(a, 'mp', [(m, (m + 2) % 8) for m in range(8)])  18 us
    ppermute x9, starting transfers between devices, over_y(): return lax.ppermute(a, 'mp', [(m, m ^ 1) for m in range(8)])  14.3 us
    ppermute x3, waiting for transfers between devices, over_x(): return lax.ppermute(a, 'dp', [(d, d ^ 2) for d in range(4)])  10.5 us
    ppermute x3, starting transfers between devices, over_x(): return lax.ppermute(a, 'dp', [(d, d ^ 2) for d in range(4)])  6.19 us
    ppermute x2, starting transfers between devices, hops(): total = total + lax.ppermute(total, 'mp', [(m, m ^ flip) for m in range(8)])  4.71 us
  transfers between devices with their start and end apart: 25, of which 9 were waited for; matrix products, arithmetic and copies ran while one was open for 43% of the time, Pallas kernels for 0%

profile of v5, /device:TPU:0, one launch (start us, length us, event | category | flops | bytes accessed | tf_op | source)
XLA Modules:
  0.0 180.1 jit_solution(15162438424658113567)
XLA Ops:
  2.0 3.0 %collective-permute-start = (bf16[1152,256]{0,1:T(8,128)(2,1)S(1)}, bf16[1152,256]{0,1:T(8,128)(2,1)}, u32[]{:S(2)}, u32[]{:S(2)}) collective-permute-start(bf16[1152,256]{0,1:T(8,128)(2,1)S(1)} %bitcast.113), channel_id=1, source_target_pairs={{0,1},{1,0},{2,3},{3,2},{4,5},{5,4},{6,7},{7,6},{8,9},{9,8},{10,11... | collective-permute-start | bytes 1769480 | tf_op jit(solution)/shard_map/ppermute | solution.py:43
  15.7 6.0 %collective-permute-done.1 = bf16[1152,256]{0,1:T(8,128)(2,1)S(1)} collective-permute-done((bf16[1152,256]{0,1:T(8,128)(2,1)S(1)}, bf16[1152,256]{0,1:T(8,128)(2,1)S(1)}, u32[]{:S(2)}, u32[]{:S(2)}) %collective-permute-start.1) | collective-permute-done | bytes 589856 | tf_op jit(solution)/shard_map/ppermute | solution.py:40
  22.2 1.9 %constant_dynamic-update-slice_fusion.6 = bf16[1152,2048]{0,1:T(8,128)(2,1)} fusion(bf16[1152,2048]{0,1:T(8,128)(2,1)} %constant_dynamic-update-slice_fusion.7, bf16[1152,256]{0,1:T(8,128)(2,1)} %collective-permute-done), kind=kLoop, calls=%fused_computation.72 | loop fusion | bytes 1179648
  25.0 10.1 %collective-permute-done.13 = bf16[1024,512]{1,0:T(8,128)(2,1)} collective-permute-done((bf16[1024,512]{1,0:T(8,128)(2,1)}, bf16[1024,512]{1,0:T(8,128)(2,1)}, u32[]{:S(2)}, u32[]{:S(2)}) %collective-permute-start.13) | collective-permute-done | bytes 1048608 | tf_op jit(solution)/shard_map/ppermute | solution.py:46
  35.1 2.3 %constant_dynamic-update-slice_fusion.10 = bf16[1024,2048]{1,0:T(8,128)(2,1)} fusion(bf16[1024,2048]{1,0:T(8,128)(2,1)} %constant_dynamic-update-slice_fusion.11, bf16[1024,512]{1,0:T(8,128)(2,1)} %collective-permute-done.12), kind=kLoop, calls=%fused_computation.76 | loop fusion | bytes 2097152
  39.5 2.4 %constant_dynamic-update-slice_fusion.9 = bf16[1024,2048]{1,0:T(8,128)(2,1)} fusion(bf16[1024,2048]{1,0:T(8,128)(2,1)} %constant_dynamic-update-slice_fusion.10, bf16[1024,512]{1,0:T(8,128)(2,1)} %collective-permute-done.13), kind=kLoop, calls=%fused_computation.75 | loop fusion | bytes 2097152
  43.7 11.6 %collective-permute-done.5 = bf16[1152,256]{0,1:T(8,128)(2,1)S(1)} collective-permute-done((bf16[1152,256]{0,1:T(8,128)(2,1)S(1)}, bf16[1152,256]{0,1:T(8,128)(2,1)S(1)}, u32[]{:S(2)}, u32[]{:S(2)}) %collective-permute-start.5) | collective-permute-done | bytes 589856 | tf_op jit(solution)/shard_map/ppermute | solution.py:40
  59.6 3.6 %abs_reduce_fusion.1 = bf16[]{:T(256)} fusion(bf16[1024,2048]{1,0:T(8,128)(2,1)} %constant_dynamic-update-slice_fusion.8), kind=kLoop, calls=%fused_computation.9 | loop fusion | flops 4194303 | bytes 4194306 | tf_op jit(solution)/shard_map/reduce_max | solution.py:69
  64.6 3.9 %collective-permute-start.16 = (f32[1]{0:T(128)}, f32[1]{0:T(128)}, u32[]{:S(2)}, u32[]{:S(2)}) collective-permute-start(f32[1]{0:T(128)} %bitcast.19), channel_id=1, source_target_pairs={{0,1},{1,0},{2,3},{3,2},{4,5},{5,4},{6,7},{7,6},{8,9},{9,8},{10,11... | collective-permute-start | bytes 20 | tf_op jit(solution)/shard_map/ppermute | solution.py:43
  68.5 2.7 %fusion.28 = f16[1152,256]{0,1:T(8,128)(2,1)} fusion(bf16[1024,1152]{1,0:T(8,128)(2,1)S(1)} %copy-done, f32[]{:T(128)} %bitcast.20, bf16[1024,2048]{1,0:T(8,128)(2,1)} %constant_dynamic-update-slice_fusion.8, s32[]{:T(128)S(6)} %add.154), kind=kOutput, calls=%fused_computation.37 | convolution fusion | flops 604569600 | bytes 3473924 | tf_op jit(solution)/shard_map/dot_general | solution.py:22
  71.6 2.7 %fusion.29 = f16[1152,256]{0,1:T(8,128)(2,1)} fusion(bf16[1024,1152]{1,0:T(8,128)(2,1)S(1)} %copy-done, f32[]{:T(128)} %bitcast.20, bf16[1024,2048]{1,0:T(8,128)(2,1)} %constant_dynamic-update-slice_fusion.8, s32[]{:T(128)S(6)} %add.153), kind=kOutput, calls=%fused_computation.38 | convolution fusion | flops 604569600 | bytes 3473924 | tf_op jit(solution)/shard_map/dot_general | solution.py:22
  76.9 3.7 %constant_dynamic-slice_fusion.1 = (bf16[1152,512]{0,1:T(8,128)(2,1)}, bf16[1152,512]{0,1:T(8,128)(2,1)S(1)}, bf16[1152,512]{0,1:T(8,128)(2,1)S(1)}, bf16[1152,512]{0,1:T(8,128)(2,1)S(1)}) fusion(bf16[1152,2048]{0,1:T(8,128)(2,1)} %constant_dynamic-update-slice_fusion, s32[]{:T(128)S(6)} %select_n.95, s32[]{:T(128)S(6)} %select_n.97, s32[]{:T(128)S(6)} %select_n.93, ...), kind=kLoop, calls=%fused_computation.90 | loop fusion | bytes 9437200 | tf_op jit(solution)/shard_map/dynamic_slice | solution.py:52
  80.6 2.9 %convolution_bitcast_fusion.4 = f32[1024,512]{0,1:T(8,128)} fusion(bf16[1152,512]{0,1:T(8,128)(2,1)S(1)} %get-tuple-element.4, bf16[1024,1152]{1,0:T(8,128)(2,1)S(1)} %copy-done), kind=kOutput, calls=%fused_computation.48 | convolution fusion | flops 1207959552 | bytes 5636096 | tf_op jit(solution)/shard_map/dot_general | solution.py:22
  83.5 2.7 %fusion.30 = f16[1152,256]{0,1:T(8,128)(2,1)} fusion(bf16[1024,1152]{1,0:T(8,128)(2,1)S(1)} %copy-done, f32[]{:T(128)} %bitcast.20, bf16[1024,2048]{1,0:T(8,128)(2,1)} %constant_dynamic-update-slice_fusion.8, s32[]{:T(128)S(6)} %add.152), kind=kOutput, calls=%fused_computation.39 | convolution fusion | flops 604569600 | bytes 3473924 | tf_op jit(solution)/shard_map/dot_general | solution.py:22
  86.5 2.7 %fusion.31 = f16[1152,256]{0,1:T(8,128)(2,1)} fusion(bf16[1024,1152]{1,0:T(8,128)(2,1)S(1)} %copy-done, f32[]{:T(128)} %bitcast.20, bf16[1024,2048]{1,0:T(8,128)(2,1)} %constant_dynamic-update-slice_fusion.8, s32[]{:T(128)S(6)} %add.151), kind=kOutput, calls=%fused_computation.40 | convolution fusion | flops 604569600 | bytes 3473924 | tf_op jit(solution)/shard_map/dot_general | solution.py:22
  89.9 1.8 %collective-permute-start.18 = (f32[1]{0:T(128)}, f32[1]{0:T(128)}, u32[]{:S(2)}, u32[]{:S(2)}) collective-permute-start(f32[1]{0:T(128)} %add.137), channel_id=1, source_target_pairs={{0,2},{1,3},{2,0},{3,1},{4,6},{5,7},{6,4},{7,5},{8,10},{9,11},{10,... | collective-permute-start | bytes 20 | tf_op jit(solution)/shard_map/ppermute | solution.py:78
  94.1 2.9 %collective-permute-start.19 = (f32[1]{0:T(128)}, f32[1]{0:T(128)}, u32[]{:S(2)}, u32[]{:S(2)}) collective-permute-start(f32[1]{0:T(128)} %add.138), channel_id=1, source_target_pairs={{0,4},{1,5},{2,6},{3,7},{4,0},{5,1},{6,2},{7,3},{8,12},{9,13},{10,... | collective-permute-start | bytes 20 | tf_op jit(solution)/shard_map/ppermute | solution.py:78
  99.3 2.9 %convolution_bitcast_fusion.5 = f32[1024,512]{0,1:T(8,128)} fusion(bf16[1152,512]{0,1:T(8,128)(2,1)S(1)} %get-tuple-element.5, bf16[1024,1152]{1,0:T(8,128)(2,1)S(1)} %copy-done), kind=kOutput, calls=%fused_computation.49 | convolution fusion | flops 1207959552 | bytes 5636096 | tf_op jit(solution)/shard_map/dot_general | solution.py:22
  102.1 3.6 %abs_reduce_fusion = bf16[]{:T(256)} fusion(bf16[1152,2048]{0,1:T(8,128)(2,1)} %constant_dynamic-update-slice_fusion), kind=kLoop, calls=%fused_computation.8 | loop fusion | flops 4718591 | bytes 4718594 | tf_op jit(solution)/shard_map/reduce_max | solution.py:85
  108.0 2.9 %fusion.54 = f32[512,1024]{1,0:T(8,128)S(1)} fusion(bf16[1152,512]{0,1:T(8,128)(2,1)} %get-tuple-element.3, bf16[1024,1152]{1,0:T(8,128)(2,1)S(1)} %copy-done), kind=kOutput, calls=%fused_computation.95 | convolution fusion | flops 1207959552 | bytes 5636096 | tf_op jit(solution)/shard_map/dot_general | solution.py:22
  111.6 3.1 %collective-permute-start.11 = (f32[1]{0:T(128)}, f32[1]{0:T(128)}, u32[]{:S(2)}, u32[]{:S(2)}) collective-permute-start(f32[1]{0:T(128)} %add.125), channel_id=1, source_target_pairs={{0,16},{8,24},{16,0},{24,8},{1,17},{9,25},{17,1},{25,9},{2,18},{10... | collective-permute-start | bytes 20 | tf_op jit(solution)/shard_map/ppermute | solution.py:46
  117.7 2.1 %fusion.25 = f16[1152,256]{0,1:T(8,128)(2,1)S(1)} fusion(bf16[1024,1152]{1,0:T(8,128)(2,1)S(1)} %copy-done, f16[1152,256]{0,1:T(8,128)(2,1)} %collective-permute-done.17, f32[]{:T(128)} %bitcast.27, f32[]{:T(128)} %bitcast.26, bf16[1024,2048]{1,0:T(8,128)(2,1)} %constant_dynamic-update-slice_fusion.8, s32[]{:T(128)S(6)} %select_n.105), kind=kOutput, calls=%fused_computation.34 | convolution fusion | flops 605454336 | bytes 4064260 | tf_op jit(solution)/shard_map/dot_general | solution.py:22
  121.2 3.1 %fusion.34 = f16[1024,512]{0,1:T(8,128)(2,1)} fusion(f32[1024,512]{0,1:T(8,128)} %collective-permute-done.8, f32[512,1024]{1,0:T(8,128)S(1)} %fusion.54, f32[]{:T(128)} %bitcast.8), kind=kLoop, calls=%fused_computation.45 | loop fusion | flops 1572864 | bytes 5242884 | tf_op jit(solution)/shard_map/convert_element_type | solution.py:88
  128.3 2.1 %fusion.27 = f16[1152,256]{0,1:T(8,128)(2,1)S(1)} fusion(bf16[1024,1152]{1,0:T(8,128)(2,1)S(1)} %copy-done, f16[1152,256]{0,1:T(8,128)(2,1)} %collective-permute-done.23, f32[]{:T(128)} %bitcast.27, f32[]{:T(128)} %bitcast.23, bf16[1024,2048]{1,0:T(8,128)(2,1)} %constant_dynamic-update-slice_fusion.8, s32[]{:T(128)S(6)} %select_n.109), kind=kOutput, calls=%fused_computation.36 | convolution fusion | flops 605454336 | bytes 4064260 | tf_op jit(solution)/shard_map/dot_general | solution.py:22
  130.5 2.0 %collective-permute-start.24 = (f16[1152,256]{0,1:T(8,128)(2,1)S(1)}, f16[1152,256]{0,1:T(8,128)(2,1)S(1)}, u32[]{:S(2)}, u32[]{:S(2)}) collective-permute-start(f16[1152,256]{0,1:T(8,128)(2,1)S(1)} %fusion.27), channel_id=1, source_target_pairs={{0,6},{1,7},{2,0},{3,1},{4,2},{5,3},{6,4},{7,5},{8,14},{9,15},{10,... | collective-permute-start | bytes 1769480 | tf_op jit(solution)/shard_map/ppermute | solution.py:98
  132.5 2.1 %fusion.26 = f16[1152,256]{0,1:T(8,128)(2,1)S(1)} fusion(bf16[1024,1152]{1,0:T(8,128)(2,1)S(1)} %copy-done, f16[1152,256]{0,1:T(8,128)(2,1)} %collective-permute-done.21, f32[]{:T(128)} %bitcast.27, f32[]{:T(128)} %bitcast.23, bf16[1024,2048]{1,0:T(8,128)(2,1)} %constant_dynamic-update-slice_fusion.8, s32[]{:T(128)S(6)} %select_n.107), kind=kOutput, calls=%fused_computation.35 | convolution fusion | flops 605454336 | bytes 4064260 | tf_op jit(solution)/shard_map/dot_general | solution.py:22
  135.0 9.2 %fusion.8 = bf16[1024,1152]{1,0:T(8,128)(2,1)} fusion(bf16[1024,2048]{1,0:T(8,128)(2,1)} %constant_dynamic-update-slice_fusion.8, bf16[1152,512]{0,1:T(8,128)(2,1)S(1)} %copy-done.4, bf16[1152,512]{0,1:T(8,128)(2,1)S(1)} %copy-done.2, bf16[1152,512]{0,1:T(8,128)(2,1)S(1)} %copy-done.6, bf16[1152,512]{0,1:T(8,128)(2,1)S(1)} %get-tuple-element.6), kind=kOutput, calls=%fused_computation.10 | convolution fusion | flops 4851892224 | bytes 11272192 | tf_op jit(solution)/shard_map/dot_general | solution.py:22
  144.2 2.8 %fusion.53 = f32[512,1024]{1,0:T(8,128)} fusion(bf16[1152,512]{0,1:T(8,128)(2,1)S(1)} %get-tuple-element.6, bf16[1024,1152]{1,0:T(8,128)(2,1)S(1)} %copy-done), kind=kOutput, calls=%fused_computation.94 | convolution fusion | flops 1207959552 | bytes 5636096 | tf_op jit(solution)/shard_map/dot_general | solution.py:22
  147.7 2.0 %collective-permute-done.20 = f16[1152,256]{0,1:T(8,128)(2,1)S(1)} collective-permute-done((f16[1152,256]{0,1:T(8,128)(2,1)S(1)}, f16[1152,256]{0,1:T(8,128)(2,1)S(1)}, u32[]{:S(2)}, u32[]{:S(2)}) %collective-permute-start.20) | collective-permute-done | bytes 589856 | tf_op jit(solution)/shard_map/ppermute | solution.py:98
  149.7 21.2 %collective-permute-done.24 = f16[1152,256]{0,1:T(8,128)(2,1)S(1)} collective-permute-done((f16[1152,256]{0,1:T(8,128)(2,1)S(1)}, f16[1152,256]{0,1:T(8,128)(2,1)S(1)}, u32[]{:S(2)}, u32[]{:S(2)}) %collective-permute-start.24) | collective-permute-done | bytes 589856 | tf_op jit(solution)/shard_map/ppermute | solution.py:98
  170.9 2.1 %fusion.20 = f32[1152,256]{0,1:T(8,128)S(1)} fusion(bf16[1024,1152]{1,0:T(8,128)(2,1)S(1)} %copy-done, f16[1152,256]{0,1:T(8,128)(2,1)S(1)} %collective-permute-done.24, f16[1152,256]{0,1:T(8,128)(2,1)S(1)} %collective-permute-done.22, f16[1152,256]{0,1:T(8,128)(2,1)S(1)} %collective-permute-done.20, f16[1152,256]{0,1:T(8,128)(2,1)S(1)} %collective-permute-done.15, ...), kind=kOutput, calls=%fused_computation.29 | convolution fusion | flops 607518720 | bytes 6423556 | tf_op jit(solution)/shard_map/dot_general | solution.py:22
  175.1 2.4 %fusion.35 = bf16[1024,512]{0,1:T(8,128)(2,1)S(1)} fusion(f32[1024,512]{0,1:T(8,128)} %collective-permute-done.7, f32[512,1024]{1,0:T(8,128)S(1)} %copy-done.1, f16[1024,512]{0,1:T(8,128)(2,1)} %collective-permute-done.10, f32[]{:T(128)} %bitcast.9), kind=kLoop, calls=%fused_computation.47 | loop fusion | flops 2621440 | bytes 6291460 | tf_op jit(solution)/shard_map/add | solution.py:105
  (78 shorter events, 39.6 us)
Async XLA Ops:
  2.0 20.2 %collective-permute-start = (bf16[1152,256]{0,1:T(8,128)(2,1)S(1)}, bf16[1152,256]{0,1:T(8,128)(2,1)}, u32[]{:S(2)}, u32[]{:S(2)}) collective-permute-start(bf16[1152,256]{0,1:T(8,128)(2,1)S(1)} %bitcast.113), channel_id=1, source_target_pairs={{0,1},{1,0},{2,3},{3,2},{4,5},{5,4},{6,7},{7,6},{8,9},{9,8},{10,11... | collective-permute-start | bytes 1769480 | tf_op jit(solution)/shard_map/ppermute | solution.py:43
  5.0 16.6 %collective-permute-start.1 = (bf16[1152,256]{0,1:T(8,128)(2,1)S(1)}, bf16[1152,256]{0,1:T(8,128)(2,1)S(1)}, u32[]{:S(2)}, u32[]{:S(2)}) collective-permute-start(bf16[1152,256]{0,1:T(8,128)(2,1)S(1)} %bitcast.114), channel_id=1, source_target_pairs={{0,2},{1,3},{2,4},{3,5},{4,6},{5,7},{6,0},{7,1},{8,10},{9,11},{10,... | collective-permute-start | bytes 1769480 | tf_op jit(solution)/shard_map/ppermute | solution.py:40
  8.1 6.6 %copy-start = (bf16[1024,1152]{1,0:T(8,128)(2,1)S(1)}, bf16[1024,1152]{1,0:T(8,128)(2,1)}, u32[]{:S(2)}) copy-start(bf16[1024,1152]{1,0:T(8,128)(2,1)} %param.3) | copy-start | bytes 7077892
  9.2 25.9 %collective-permute-start.12 = (bf16[1024,512]{1,0:T(8,128)(2,1)}, bf16[1024,512]{1,0:T(8,128)(2,1)}, u32[]{:S(2)}, u32[]{:S(2)}) collective-permute-start(bf16[1024,512]{1,0:T(8,128)(2,1)} %pad_maximum_fusion), channel_id=1, source_target_pairs={{0,8},{8,0},{16,24},{24,16},{1,9},{9,1},{17,25},{25,17},{2,10},{10... | collective-permute-start | bytes 3145736 | tf_op jit(solution)/shard_map/ppermute | solution.py:49
  9.2 25.9 %collective-permute-start.13 = (bf16[1024,512]{1,0:T(8,128)(2,1)}, bf16[1024,512]{1,0:T(8,128)(2,1)}, u32[]{:S(2)}, u32[]{:S(2)}) collective-permute-start(bf16[1024,512]{1,0:T(8,128)(2,1)} %pad_maximum_fusion), channel_id=1, source_target_pairs={{0,16},{8,24},{16,0},{24,8},{1,17},{9,25},{17,1},{25,9},{2,18},{10... | collective-permute-start | bytes 3145736 | tf_op jit(solution)/shard_map/ppermute | solution.py:46
  21.7 20.2 %collective-permute-start.2 = (bf16[1152,256]{0,1:T(8,128)(2,1)S(1)}, bf16[1152,256]{0,1:T(8,128)(2,1)S(1)}, u32[]{:S(2)}, u32[]{:S(2)}) collective-permute-start(bf16[1152,256]{0,1:T(8,128)(2,1)S(1)} %collective-permute-done.1), channel_id=1, source_target_pairs={{0,1},{1,0},{2,3},{3,2},{4,5},{5,4},{6,7},{7,6},{8,9},{9,8},{10,11... | collective-permute-start | bytes 1769480 | tf_op jit(solution)/shard_map/ppermute | solution.py:43
  22.2 15.7 %collective-permute-start.3 = (bf16[1152,256]{0,1:T(8,128)(2,1)S(1)}, bf16[1152,256]{0,1:T(8,128)(2,1)S(1)}, u32[]{:S(2)}, u32[]{:S(2)}) collective-permute-start(bf16[1152,256]{0,1:T(8,128)(2,1)S(1)} %collective-permute-done.1), channel_id=1, source_target_pairs={{0,2},{1,3},{2,4},{3,5},{4,6},{5,7},{6,0},{7,1},{8,10},{9,11},{10,... | collective-permute-start | bytes 1769480 | tf_op jit(solution)/shard_map/ppermute | solution.py:40
  35.1 23.4 %collective-permute-start.14 = (bf16[1024,512]{1,0:T(8,128)(2,1)}, bf16[1024,512]{1,0:T(8,128)(2,1)S(1)}, u32[]{:S(2)}, u32[]{:S(2)}) collective-permute-start(bf16[1024,512]{1,0:T(8,128)(2,1)} %collective-permute-done.13), channel_id=1, source_target_pairs={{0,8},{8,0},{16,24},{24,16},{1,9},{9,1},{17,25},{25,17},{2,10},{10... | collective-permute-start | bytes 3145736 | tf_op jit(solution)/shard_map/ppermute | solution.py:49
  37.9 18.9 %collective-permute-start.4 = (bf16[1152,256]{0,1:T(8,128)(2,1)S(1)}, bf16[1152,256]{0,1:T(8,128)(2,1)S(1)}, u32[]{:S(2)}, u32[]{:S(2)}) collective-permute-start(bf16[1152,256]{0,1:T(8,128)(2,1)S(1)} %collective-permute-done.3), channel_id=1, source_target_pairs={{0,1},{1,0},{2,3},{3,2},{4,5},{5,4},{6,7},{7,6},{8,9},{9,8},{10,11... | collective-permute-start | bytes 1769480 | tf_op jit(solution)/shard_map/ppermute | solution.py:43
  39.2 16.1 %collective-permute-start.5 = (bf16[1152,256]{0,1:T(8,128)(2,1)S(1)}, bf16[1152,256]{0,1:T(8,128)(2,1)S(1)}, u32[]{:S(2)}, u32[]{:S(2)}) collective-permute-start(bf16[1152,256]{0,1:T(8,128)(2,1)S(1)} %collective-permute-done.3), channel_id=1, source_target_pairs={{0,2},{1,3},{2,4},{3,5},{4,6},{5,7},{6,0},{7,1},{8,10},{9,11},{10,... | collective-permute-start | bytes 1769480 | tf_op jit(solution)/shard_map/ppermute | solution.py:40
  55.2 20.8 %collective-permute-start.6 = (bf16[1152,256]{0,1:T(8,128)(2,1)S(1)}, bf16[1152,256]{0,1:T(8,128)(2,1)S(1)}, u32[]{:S(2)}, u32[]{:S(2)}) collective-permute-start(bf16[1152,256]{0,1:T(8,128)(2,1)S(1)} %collective-permute-done.5), channel_id=1, source_target_pairs={{0,1},{1,0},{2,3},{3,2},{4,5},{5,4},{6,7},{7,6},{8,9},{9,8},{10,11... | collective-permute-start | bytes 1769480 | tf_op jit(solution)/shard_map/ppermute | solution.py:43
  64.6 24.7 %collective-permute-start.16 = (f32[1]{0:T(128)}, f32[1]{0:T(128)}, u32[]{:S(2)}, u32[]{:S(2)}) collective-permute-start(f32[1]{0:T(128)} %bitcast.19), channel_id=1, source_target_pairs={{0,1},{1,0},{2,3},{3,2},{4,5},{5,4},{6,7},{7,6},{8,9},{9,8},{10,11... | collective-permute-start | bytes 20 | tf_op jit(solution)/shard_map/ppermute | solution.py:43
  71.3 55.5 %collective-permute-start.23 = (f16[1152,256]{0,1:T(8,128)(2,1)}, f16[1152,256]{0,1:T(8,128)(2,1)}, u32[]{:S(2)}, u32[]{:S(2)}) collective-permute-start(f16[1152,256]{0,1:T(8,128)(2,1)} %fusion.28), channel_id=1, source_target_pairs={{0,1},{1,0},{2,3},{3,2},{4,5},{5,4},{6,7},{7,6},{8,9},{9,8},{10,11... | collective-permute-start | bytes 1769480 | tf_op jit(solution)/shard_map/ppermute | solution.py:43
  74.3 56.2 %collective-permute-start.21 = (f16[1152,256]{0,1:T(8,128)(2,1)}, f16[1152,256]{0,1:T(8,128)(2,1)}, u32[]{:S(2)}, u32[]{:S(2)}) collective-permute-start(f16[1152,256]{0,1:T(8,128)(2,1)} %fusion.29), channel_id=1, source_target_pairs={{0,1},{1,0},{2,3},{3,2},{4,5},{5,4},{6,7},{7,6},{8,9},{9,8},{10,11... | collective-permute-start | bytes 1769480 | tf_op jit(solution)/shard_map/ppermute | solution.py:43
  80.6 2.9 %copy-start.3 = (bf16[1152,512]{0,1:T(8,128)(2,1)}, bf16[1152,512]{0,1:T(8,128)(2,1)S(1)}, u32[]{:S(2)}) copy-start(bf16[1152,512]{0,1:T(8,128)(2,1)S(1)} %get-tuple-element.4) | copy-start | bytes 3538948
  80.6 18.6 %copy-start.5 = (bf16[1152,512]{0,1:T(8,128)(2,1)}, bf16[1152,512]{0,1:T(8,128)(2,1)S(1)}, u32[]{:S(2)}) copy-start(bf16[1152,512]{0,1:T(8,128)(2,1)S(1)} %get-tuple-element.5) | copy-start | bytes 3538948
  83.5 36.3 %collective-permute-start.8 = (f32[1024,512]{0,1:T(8,128)}, f32[1024,512]{0,1:T(8,128)}, u32[]{:S(2)}, u32[]{:S(2)}) collective-permute-start(f32[1024,512]{0,1:T(8,128)} %convolution_bitcast_fusion.4), channel_id=1, source_target_pairs={{0,8},{8,0},{16,24},{24,16},{1,9},{9,1},{17,25},{25,17},{2,10},{10... | collective-permute-start | bytes 6291464 | tf_op jit(solution)/shard_map/ppermute | solution.py:49
  86.2 31.4 %collective-permute-start.17 = (f16[1152,256]{0,1:T(8,128)(2,1)}, f16[1152,256]{0,1:T(8,128)(2,1)}, u32[]{:S(2)}, u32[]{:S(2)}) collective-permute-start(f16[1152,256]{0,1:T(8,128)(2,1)} %fusion.30), channel_id=1, source_target_pairs={{0,1},{1,0},{2,3},{3,2},{4,5},{5,4},{6,7},{7,6},{8,9},{9,8},{10,11... | collective-permute-start | bytes 1769480 | tf_op jit(solution)/shard_map/ppermute | solution.py:43
  89.9 3.6 %collective-permute-start.18 = (f32[1]{0:T(128)}, f32[1]{0:T(128)}, u32[]{:S(2)}, u32[]{:S(2)}) collective-permute-start(f32[1]{0:T(128)} %add.137), channel_id=1, source_target_pairs={{0,2},{1,3},{2,0},{3,1},{4,6},{5,7},{6,4},{7,5},{8,10},{9,11},{10,... | collective-permute-start | bytes 20 | tf_op jit(solution)/shard_map/ppermute | solution.py:78
  94.1 4.5 %collective-permute-start.19 = (f32[1]{0:T(128)}, f32[1]{0:T(128)}, u32[]{:S(2)}, u32[]{:S(2)}) collective-permute-start(f32[1]{0:T(128)} %add.138), channel_id=1, source_target_pairs={{0,4},{1,5},{2,6},{3,7},{4,0},{5,1},{6,2},{7,3},{8,12},{9,13},{10,... | collective-permute-start | bytes 20 | tf_op jit(solution)/shard_map/ppermute | solution.py:78
  107.1 3.8 %collective-permute-start.9 = (f32[1]{0:T(128)}, f32[1]{0:T(128)}, u32[]{:S(2)}, u32[]{:S(2)}) collective-permute-start(f32[1]{0:T(128)} %bitcast.7), channel_id=1, source_target_pairs={{0,8},{8,0},{16,24},{24,16},{1,9},{9,1},{17,25},{25,17},{2,10},{10... | collective-permute-start | bytes 20 | tf_op jit(solution)/shard_map/ppermute | solution.py:49
  108.0 7.2 %copy-start.7 = (f16[1152,256]{0,1:T(8,128)(2,1)S(1)}, f16[1152,256]{0,1:T(8,128)(2,1)}, u32[]{:S(2)}) copy-start(f16[1152,256]{0,1:T(8,128)(2,1)} %fusion.31) | copy-start | bytes 1769476
  111.6 3.6 %collective-permute-start.11 = (f32[1]{0:T(128)}, f32[1]{0:T(128)}, u32[]{:S(2)}, u32[]{:S(2)}) collective-permute-start(f32[1]{0:T(128)} %add.125), channel_id=1, source_target_pairs={{0,16},{8,24},{16,0},{24,8},{1,17},{9,25},{17,1},{25,9},{2,18},{10... | collective-permute-start | bytes 20 | tf_op jit(solution)/shard_map/ppermute | solution.py:46
  115.2 19.4 %collective-permute-start.15 = (f16[1152,256]{0,1:T(8,128)(2,1)S(1)}, f16[1152,256]{0,1:T(8,128)(2,1)S(1)}, u32[]{:S(2)}, u32[]{:S(2)}) collective-permute-start(f16[1152,256]{0,1:T(8,128)(2,1)S(1)} %copy-done.7), channel_id=1, source_target_pairs={{0,1},{1,0},{2,3},{3,2},{4,5},{5,4},{6,7},{7,6},{8,9},{9,8},{10,11... | collective-permute-start | bytes 1769480 | tf_op jit(solution)/shard_map/ppermute | solution.py:43
  117.6 56.8 %collective-permute-start.7 = (f32[1024,512]{0,1:T(8,128)}, f32[1024,512]{0,1:T(8,128)}, u32[]{:S(2)}, u32[]{:S(2)}) collective-permute-start(f32[1024,512]{0,1:T(8,128)} %convolution_bitcast_fusion.5), channel_id=1, source_target_pairs={{0,8},{8,0},{16,24},{24,16},{1,9},{9,1},{17,25},{25,17},{2,10},{10... | collective-permute-start | bytes 6291464 | tf_op jit(solution)/shard_map/ppermute | solution.py:49
  119.9 29.8 %collective-permute-start.20 = (f16[1152,256]{0,1:T(8,128)(2,1)S(1)}, f16[1152,256]{0,1:T(8,128)(2,1)S(1)}, u32[]{:S(2)}, u32[]{:S(2)}) collective-permute-start(f16[1152,256]{0,1:T(8,128)(2,1)S(1)} %fusion.25), channel_id=1, source_target_pairs={{0,4},{1,5},{2,6},{3,7},{4,0},{5,1},{6,2},{7,3},{8,12},{9,13},{10,... | collective-permute-start | bytes 1769480 | tf_op jit(solution)/shard_map/ppermute | solution.py:98
  126.8 47.7 %collective-permute-start.10 = (f16[1024,512]{0,1:T(8,128)(2,1)}, f16[1024,512]{0,1:T(8,128)(2,1)}, u32[]{:S(2)}, u32[]{:S(2)}) collective-permute-start(f16[1024,512]{0,1:T(8,128)(2,1)} %fusion.34), channel_id=1, source_target_pairs={{0,16},{8,24},{16,0},{24,8},{1,17},{9,25},{17,1},{25,9},{2,18},{10... | collective-permute-start | bytes 3145736 | tf_op jit(solution)/shard_map/ppermute | solution.py:46
  130.5 4.5 %copy-start.2 = (bf16[1152,512]{0,1:T(8,128)(2,1)S(1)}, bf16[1152,512]{0,1:T(8,128)(2,1)}, u32[]{:S(2)}) copy-start(bf16[1152,512]{0,1:T(8,128)(2,1)} %get-tuple-element.3) | copy-start | bytes 3538948
  130.5 4.5 %copy-start.4 = (bf16[1152,512]{0,1:T(8,128)(2,1)S(1)}, bf16[1152,512]{0,1:T(8,128)(2,1)}, u32[]{:S(2)}) copy-start(bf16[1152,512]{0,1:T(8,128)(2,1)} %copy-done.3) | copy-start | bytes 3538948
  130.5 4.5 %copy-start.6 = (bf16[1152,512]{0,1:T(8,128)(2,1)S(1)}, bf16[1152,512]{0,1:T(8,128)(2,1)}, u32[]{:S(2)}) copy-start(bf16[1152,512]{0,1:T(8,128)(2,1)} %copy-done.5) | copy-start | bytes 3538948
  130.5 40.4 %collective-permute-start.24 = (f16[1152,256]{0,1:T(8,128)(2,1)S(1)}, f16[1152,256]{0,1:T(8,128)(2,1)S(1)}, u32[]{:S(2)}, u32[]{:S(2)}) collective-permute-start(f16[1152,256]{0,1:T(8,128)(2,1)S(1)} %fusion.27), channel_id=1, source_target_pairs={{0,6},{1,7},{2,0},{3,1},{4,2},{5,3},{6,4},{7,5},{8,14},{9,15},{10,... | collective-permute-start | bytes 1769480 | tf_op jit(solution)/shard_map/ppermute | solution.py:98
  134.6 36.3 %collective-permute-start.22 = (f16[1152,256]{0,1:T(8,128)(2,1)S(1)}, f16[1152,256]{0,1:T(8,128)(2,1)S(1)}, u32[]{:S(2)}, u32[]{:S(2)}) collective-permute-start(f16[1152,256]{0,1:T(8,128)(2,1)S(1)} %fusion.26), channel_id=1, source_target_pairs={{0,2},{1,3},{2,4},{3,5},{4,6},{5,7},{6,0},{7,1},{8,10},{9,11},{10,... | collective-permute-start | bytes 1769480 | tf_op jit(solution)/shard_map/ppermute | solution.py:98
  (1 other events, 2.0 us)
